TPU v7x, 256 devices: a whole 4x4x8 slice. The times are simulated.
256 devices in a mesh: box: 64 (over z, x_lo, y), snap: 4 (over x_hi, core).
Axes of the slice: x: 4 (x_hi: 2, x_lo: 2; x = x_hi * 2 + x_lo), y: 4, z: 8, core: 2. Of those that a mesh axis runs over, the one named last changes fastest.
Arguments:
- fields: bfloat16 [4, 320, 48, 1024], P('snap', 'box'), may hold values from -6 to 6
- cotangent: bfloat16 [4, 320, 48, 1024], P('snap', 'box'), may hold values from -0.0068359375 to 0.0068359375
- plane_counts: int32 [4, 64], P('snap', 'box'), may hold values from 2 to 5, as said below
- w_first: bfloat16 [48, 1296], replicated, may hold values from -0.15625 to 0.15625
- b_first: float32 [48], replicated, may hold values from -3 to 3
- w_second: bfloat16 [48, 1296], replicated, may hold values from -0.15625 to 0.15625
- b_second: float32 [48], replicated, may hold values from -3 to 3
Outputs:
- decoded: bfloat16 [4, 320, 48, 1024], P('snap', 'box')
- grad_first: float32 [48, 1296], replicated
- grad_second: float32 [48, 1296], replicated
- bias_grad_first: float32 [48], replicated
- bias_grad_second: float32 [48], replicated
Inputs may be any that keep to these rules, and one draw needn't show every extreme that they name: `plane_counts`: in each snapshot every device holds 2 to 5 planes and the devices hold 184 planes together; a device's planes continue the chain right after those of the device before it along box.
All inputs are finite; a program needn't handle non-finite values.
Results may differ from a plain program's by a relative error of at most 0.008.
Values may be sent and summed in bfloat16 or wider, within the bound.
No kernel may reach another device: no remote copies, remote signals or barrier semaphores. Data moves between devices by JAX's collectives and lax.ppermute only.
A program may use at most 64 MiB of HBM per device.

v0:
```python
import jax
import jax.numpy as jnp
from jax import lax
from jax.sharding import PartitionSpec as P

SIDE = 32


def extended_2(block, sides, width):
    for axis, dim in sides:
        count = lax.axis_size(axis)
        forward = [(i, i + 1) for i in range(count - 1)]
        backward = [(target, source) for source, target in forward]
        low = lax.ppermute(
            lax.slice_in_dim(block, block.shape[dim] - width, None, axis=dim), axis, forward
        )
        high = lax.ppermute(lax.slice_in_dim(block, 0, width, axis=dim), axis, backward)
        block = jnp.concatenate([low, block, high], axis=dim)
    return block


def tap_piece(field, tap, planes, side):
    first = tap // 9
    second = tap // 3 % 3
    third = tap % 3
    zero = jnp.zeros((), jnp.int32)
    return lax.dynamic_slice(
        field, (2 * first, zero, 2 * second, 2 * third), (planes, field.shape[1], side, side)
    )


def conv_forward(padded, kernel):
    width = kernel.shape[0]
    field = padded[0]
    planes = field.shape[0] - 4
    side = field.shape[2] - 4

    def conv_add_tap(tap, total):
        piece = tap_piece(field, tap, planes, side)
        w_tap = lax.dynamic_slice_in_dim(kernel, tap * width, width, 1)
        return total + jnp.einsum("ok,pkij->poij", w_tap, piece, preferred_element_type=jnp.float32)

    total = lax.fori_loop(0, 27, conv_add_tap, jnp.zeros((planes, width, side, side), jnp.float32))
    return total[None]


def weight_grad(padded, upstream):
    field = padded[0]
    grads = upstream[0]
    planes = grads.shape[0]
    width = grads.shape[1]
    side = grads.shape[2]

    def weight_add_tap(tap, total):
        piece = tap_piece(field, tap, planes, side)
        block = jnp.einsum("poij,pkij->ok", grads, piece, preferred_element_type=jnp.float32)
        return lax.dynamic_update_slice_in_dim(total, block[:, None, :], tap, 1)

    total = lax.fori_loop(0, 27, weight_add_tap, jnp.zeros((width, 27, width), jnp.float32))
    return total.reshape(width, 27 * width)


def flipped(kernel):
    width = kernel.shape[0]
    shaped = kernel.reshape(width, 3, 3, 3, width)[:, ::-1, ::-1, ::-1, :]
    return jnp.transpose(shaped, (4, 1, 2, 3, 0)).reshape(width, 27 * width)


def silu_slope(value):
    sigma = jax.nn.sigmoid(value)
    return sigma * (1.0 + value * (1.0 - sigma))


def edge_planes(field, plane_count):
    return jnp.concatenate(
        [field[0:2], lax.dynamic_slice_in_dim(field, plane_count - 2, 2, 0)], axis=0
    )


def extend(field, received, plane_count):
    blank = jnp.zeros((2,) + field.shape[1:], field.dtype)
    extended = jnp.concatenate([received[0:2], field, blank], axis=0)
    extended = lax.dynamic_update_slice_in_dim(extended, received[6:8], plane_count + 2, 0)
    return jnp.pad(extended, ((0, 0), (0, 0), (2, 2), (2, 2)))[None]


def local(fields, cotangent, plane_counts, w_first, b_first, w_second, b_second):
    slots = fields.shape[1]
    width = fields.shape[2]
    plane_count = plane_counts[0, 0]
    keeper = (jnp.arange(slots, dtype=jnp.int32) < plane_count).astype(jnp.bfloat16)[
        :, None, None, None
    ]
    inputs = fields[0].reshape(slots, width, SIDE, SIDE) * keeper
    upstream = cotangent[0].reshape(slots, width, SIDE, SIDE) * keeper
    input_edges = extended_2(edge_planes(inputs, plane_count), (("box", 0),), 2)
    padded_input = extend(inputs, input_edges, plane_count)
    hidden_pre = conv_forward(padded_input, w_first)[0] + b_first[None, :, None, None]
    hidden = jax.nn.silu(hidden_pre).astype(jnp.bfloat16) * keeper
    hidden_edges = extended_2(edge_planes(hidden, plane_count), (("box", 0),), 2)
    padded_hidden = extend(hidden, hidden_edges, plane_count)
    output = (conv_forward(padded_hidden, w_second)[0] + b_second[None, :, None, None]).astype(
        jnp.bfloat16
    ) * keeper
    decoded = output.reshape(1, slots, width, SIDE * SIDE)
    upstream_edges = extended_2(edge_planes(upstream, plane_count), (("box", 0),), 2)
    padded_upstream = extend(upstream, upstream_edges, plane_count)
    grad_second = weight_grad(padded_hidden, upstream[None])
    bias_second = jnp.sum(upstream.astype(jnp.float32), axis=(0, 2, 3))
    hidden_grad = conv_forward(padded_upstream, flipped(w_second))[0]
    pre_grad = (hidden_grad * silu_slope(hidden_pre)).astype(jnp.bfloat16) * keeper
    grad_first = weight_grad(padded_input, pre_grad[None])
    bias_first = jnp.sum(pre_grad.astype(jnp.float32), axis=(0, 2, 3))
    grad_first, grad_second, bias_first, bias_second = lax.psum(
        (grad_first, grad_second, bias_first, bias_second), ("box", "snap")
    )
    return (decoded, grad_first, grad_second, bias_first, bias_second)


def solution(mesh):
    return jax.shard_map(
        local,
        mesh=mesh,
        in_specs=(
            P("snap", "box", None, None),
            P("snap", "box", None, None),
            P("snap", "box"),
            P(),
            P(),
            P(),
            P(),
        ),
        out_specs=(P("snap", "box", None, None), P(), P(), P(), P()),
        check_vma=False,
    )
```

profile of v0, /device:TPU:126, one launch (start us, length us, event | category | flops | bytes accessed | tf_op | source)
XLA Modules:
  0.0 749.3 jit_solution(146112653859606153)
XLA Ops:
  10.8 4.9 collective-permute-start
  19.2 8.0 %collective-permute-done = bf16[2,48,32,32]{1,3,2,0:T(8,128)(2,1)} collective-permute-done((bf16[2,48,32,32]{1,3,2,0:T(8,128)(2,1)}, bf16[2,48,32,32]{1,3,2,0:T(8,128)(2,1)}, u32[]{:S(2)}, u32[]{:S(2)}) %collective-permute-start) | collective-permute-done | bytes 196640 | tf_op jit(solution)/shard_map/ppermute | solution.py:14
  29.2 6.5 collective-permute-done.1
  36.7 2.8 pad.10
  39.5 70.8 %while.85 = (s32[]{:T(128)}, f32[5,48,32,32]{1,3,2,0:T(8,128)S(1)}, bf16[9,48,36,36]{1,3,2,0:T(8,128)(2,1)}, bf16[48,1296]{1,0:T(8,128)(2,1)}, s32[]{:T(128)}, /...) while((s32[]{:T(128)}, f32[5,48,32,32]{1,3,2,0:T(8,128)S(1)}, ...), condition=%wide.region_1.2_spmd.clone, body=%wide.region_0.1_spmd.clone.sunk | while | flops 24084524 | bytes 3289657 | solution.py:43
  47.4 2.5 bitcast_add_fusion.6
  50.0 2.5 bitcast_add_fusion.6
  52.6 2.5 bitcast_add_fusion.6
  55.3 2.5 bitcast_add_fusion.6
  57.9 2.5 bitcast_add_fusion.6
  60.5 2.5 bitcast_add_fusion.6
  63.2 2.5 bitcast_add_fusion.6
  65.8 2.5 bitcast_add_fusion.6
  68.4 2.5 bitcast_add_fusion.6
  71.0 2.5 bitcast_add_fusion.6
  73.7 2.5 bitcast_add_fusion.6
  76.3 2.5 bitcast_add_fusion.6
  78.9 2.5 bitcast_add_fusion.6
  81.5 2.5 bitcast_add_fusion.6
  84.2 2.5 bitcast_add_fusion.6
  86.8 2.5 bitcast_add_fusion.6
  121.2 3.4 rev.3
  128.3 2.6 copy.30
  131.0 3.9 collective-permute-start.5
  134.9 3.9 collective-permute-start.3
  140.7 3.0 maximum_maximum_fusion.2
  143.7 8.4 %collective-permute-done.5 = bf16[2,48,32,32]{1,3,2,0:T(8,128)(2,1)S(1)} collective-permute-done((bf16[2,48,32,32]{1,3,2,0:T(8,128)(2,1)}, bf16[2,48,32,32]{1,3,2,0:T(8,128)(2,1)S(1)}, u32[]{:S(2)}, u32[]{:S(2)}) %collective-permute-start.5) | collective-permute-done | bytes 196640 | tf_op jit(solution)/shard_map/ppermute | solution.py:17
  152.1 8.9 %collective-permute-done.3 = bf16[2,48,32,32]{1,3,2,0:T(8,128)(2,1)S(1)} collective-permute-done((bf16[2,48,32,32]{1,3,2,0:T(8,128)(2,1)}, bf16[2,48,32,32]{1,3,2,0:T(8,128)(2,1)S(1)}, u32[]{:S(2)}, u32[]{:S(2)}) %collective-permute-start.3) | collective-permute-done | bytes 196640 | tf_op jit(solution)/shard_map/ppermute | solution.py:17
  161.9 2.8 pad.11
  164.8 65.6 %while.84 = (s32[]{:T(128)}, f32[48,27,48]{0,2,1:T(8,128)S(1)}, bf16[9,48,36,36]{1,3,2,0:T(8,128)(2,1)}, bf16[5,48,32,32]{1,3,0,2:T(8,128)(2,1)}, s32[]{:T(128)}...) while((s32[]{:T(128)}, f32[48,27,48]{0,2,1:T(8,128)S(1)}, ...), condition=%wide.region_10.11_spmd, body=%wide.region_9.10_spmd.sunk | while | flops 23592996 | bytes 2647021 | solution.py:59
  231.3 4.7 pad.12
  236.0 116.8 %while.87 = (s32[]{:T(128)}, f32[5,48,32,32]{1,3,2,0:T(8,128)}, bf16[9,48,36,36]{1,3,2,0:T(8,128)(2,1)}, bf16[48,1296]{1,0:T(8,128)(2,1)S(1)}, s32[]{:T(128)}, /...) while((s32[]{:T(128)}, f32[5,48,32,32]{1,3,2,0:T(8,128)}, ...), condition=%wide.region_5.6_spmd.clone, body=%wide.region_4.5_spmd.clone.sunk | while | flops 24084524 | bytes 4928057 | solution.py:43
  236.0 3.6 bitcast_add_fusion.8
  239.5 4.4 bitcast_add_fusion.8
  243.9 4.4 bitcast_add_fusion.8
  248.3 4.4 bitcast_add_fusion.8
  252.6 4.4 bitcast_add_fusion.8
  257.0 4.4 bitcast_add_fusion.8
  261.3 4.4 bitcast_add_fusion.8
  265.7 4.4 bitcast_add_fusion.8
  270.0 4.4 bitcast_add_fusion.8
  274.4 4.4 bitcast_add_fusion.8
  278.7 4.4 bitcast_add_fusion.8
  283.1 4.4 bitcast_add_fusion.8
  287.4 4.4 bitcast_add_fusion.8
  291.8 4.4 bitcast_add_fusion.8
  296.1 4.4 bitcast_add_fusion.8
  300.5 4.4 bitcast_add_fusion.8
  304.9 4.4 bitcast_add_fusion.8
  309.2 4.4 bitcast_add_fusion.8
  313.6 4.4 bitcast_add_fusion.8
  317.9 4.4 bitcast_add_fusion.8
  322.3 4.4 bitcast_add_fusion.8
  326.6 4.4 bitcast_add_fusion.8
  331.0 4.4 bitcast_add_fusion.8
  335.3 4.4 bitcast_add_fusion.8
  339.7 4.4 bitcast_add_fusion.8
  344.0 4.4 bitcast_add_fusion.8
  348.4 4.4 bitcast_add_fusion.8
  352.7 3.0 convert_reduce_fusion
  357.1 65.7 %while.83 = (s32[]{:T(128)}, f32[48,27,48]{0,2,1:T(8,128)S(1)}, bf16[9,48,36,36]{1,3,2,0:T(8,128)(2,1)}, bf16[5,48,32,32]{1,3,0,2:T(8,128)(2,1)}, s32[]{:T(128)}...) while((s32[]{:T(128)}, f32[48,27,48]{0,2,1:T(8,128)S(1)}, ...), condition=%wide.region_7.8_spmd, body=%wide.region_6.7_spmd.sunk | while | flops 23592996 | bytes 2647021 | solution.py:59
  423.8 70.8 %while.86 = (s32[]{:T(128)}, f32[5,48,32,32]{1,3,2,0:T(8,128)S(1)}, bf16[9,48,36,36]{1,3,2,0:T(8,128)(2,1)}, bf16[48,1296]{1,0:T(8,128)(2,1)}, s32[]{:T(128)}, /...) while((s32[]{:T(128)}, f32[5,48,32,32]{1,3,2,0:T(8,128)S(1)}, ...), condition=%wide.region_3.4_spmd.clone, body=%wide.region_2.3_spmd.clone.sunk | while | flops 24084524 | bytes 3289657 | solution.py:43
  498.4 69.2 %all-reduce.3 = (f32[48]{0:T(128)}, f32[48]{0:T(128)}) all-reduce(f32[48]{0:T(128)S(1)} %get-tuple-element.795, f32[48]{0:T(128)S(1)} %convert_reduce_fusion.1), channel_id=1, replica_groups=mesh['box'=64,'snap'=4] {'box','snap'}, use_global_device_ids=true, to_apply=%region_13.14 | all-reduce | flops 96 | bytes 768 | tf_op jit(solution)/shard_map/psum | solution.py:114
  567.6 171.5 %all-reduce.7.cloned.1.call-done = (f32[48,1296]{1,0:T(8,128)}, f32[48,1296]{1,0:T(8,128)}) async-done(((f32[48,1296]{1,0:T(8,128)}, f32[48,1296]{1,0:T(8,128)}), (f32[48,1296]{1,0:T(8,128)}, f32[48,1296]{1,0:T(8,128)})) %all-reduce.7.cloned.1.call-update) | async-done | bytes 497680 | tf_op jit(solution)/shard_map/psum | solution.py:114
  (158 shorter events, 258.8 us)
Async XLA Ops:
  7.2 731.9 %all-reduce.7.cloned.1.call-start = ((), (), s32[]{:S(2)}) async-start(), calls=%async_computation | async-start | bytes 1081344 | tf_op jit(solution)/shard_map/psum | solution.py:114
  7.9 102.5 %copy-start.8 = (bf16[5]{0:T(256)(128)(2,1)}, bf16[5]{0:T(256)(128)(2,1)S(1)}, u32[]{:S(2)}) copy-start(bf16[5]{0:T(256)(128)(2,1)S(1)} %compare_convert_fusion) | copy-start | bytes 34
  9.5 8.2 %copy-start.6 = (bf16[1,5,48,1024]{3,2,1,0:T(8,128)(2,1)S(1)}, bf16[1,5,48,1024]{3,2,1,0:T(8,128)(2,1)}, u32[]{:S(2)}) copy-start(bf16[1,5,48,1024]{3,2,1,0:T(8,128)(2,1)} %param.18) | copy-start | bytes 1474564
  9.7 6.1 copy-start.3
  10.8 16.4 %collective-permute-start = (bf16[2,48,32,32]{1,3,2,0:T(8,128)(2,1)}, bf16[2,48,32,32]{1,3,2,0:T(8,128)(2,1)}, u32[]{:S(2)}, u32[]{:S(2)}) collective-permute-start(bf16[2,48,32,32]{1,3,2,0:T(8,128)(2,1)} %get-tuple-element.802), channel_id=1, source_target_pairs={{0,4},{4,8},{8,12},{12,16},{16,20},{20,24},{24,28},{28,32},{32,36}... | collective-permute-start | bytes 589832 | tf_op jit(solution)/shard_map/ppermute | solution.py:14
  15.8 19.8 %collective-permute-start.1 = (bf16[2,48,32,32]{1,3,2,0:T(8,128)(2,1)}, bf16[2,48,32,32]{1,3,2,0:T(8,128)(2,1)}, u32[]{:S(2)}, u32[]{:S(2)}) collective-permute-start(bf16[2,48,32,32]{1,3,2,0:T(8,128)(2,1)} %get-tuple-element.801), channel_id=1, source_target_pairs={{4,0},{8,4},{12,8},{16,12},{20,16},{24,20},{28,24},{32,28},{36,32}... | collective-permute-start | bytes 589832 | tf_op jit(solution)/shard_map/ppermute | solution.py:17
  19.2 17.5 %copy-start.12 = (bf16[9]{0:T(256)(128)(2,1)}, bf16[9]{0:T(256)(128)(2,1)S(1)}, u32[]{:S(2)}) copy-start(bf16[9]{0:T(256)(128)(2,1)S(1)} %pad.21.clone) | copy-start | bytes 58
  39.5 70.9 %copy-start.10 = (f32[48]{0:T(128)S(1)}, f32[48]{0:T(128)}, u32[]{:S(2)}) copy-start(f32[48]{0:T(128)} %param.21) | copy-start | bytes 580
  112.7 1.1 copy-start.1
  112.7 4.3 copy-start.4
  112.7 7.3 copy-start.7
  114.8 23.9 %collective-permute-start.4 = (bf16[2,48,32,32]{1,3,2,0:T(8,128)(2,1)}, bf16[2,48,32,32]{1,3,2,0:T(8,128)(2,1)}, u32[]{:S(2)}, u32[]{:S(2)}) collective-permute-start(bf16[2,48,32,32]{1,3,2,0:T(8,128)(2,1)} %get-tuple-element.798), channel_id=1, source_target_pairs={{0,4},{4,8},{8,12},{12,16},{16,20},{20,24},{24,28},{28,32},{32,36}... | collective-permute-start | bytes 589832 | tf_op jit(solution)/shard_map/ppermute | solution.py:14
  118.1 22.6 %collective-permute-start.2 = (bf16[2,48,32,32]{1,3,2,0:T(8,128)(2,1)}, bf16[2,48,32,32]{1,3,2,0:T(8,128)(2,1)}, u32[]{:S(2)}, u32[]{:S(2)}) collective-permute-start(bf16[2,48,32,32]{1,3,2,0:T(8,128)(2,1)} %get-tuple-element.800), channel_id=1, source_target_pairs={{0,4},{4,8},{8,12},{12,16},{16,20},{20,24},{24,28},{28,32},{32,36}... | collective-permute-start | bytes 589832 | tf_op jit(solution)/shard_map/ppermute | solution.py:14
  126.0 14.7 %copy-start.13 = (bf16[9]{0:T(256)(128)(2,1)S(1)}, bf16[9]{0:T(256)(128)(2,1)}, u32[]{:S(2)}) copy-start(bf16[9]{0:T(256)(128)(2,1)} %copy-done.12) | copy-start | bytes 58
  127.3 13.4 %copy-start.2 = (bf16[5,48,32,32]{1,3,2,0:T(8,128)(2,1)S(1)}, bf16[5,48,32,32]{1,3,2,0:T(8,128)(2,1)}, u32[]{:S(2)}) copy-start(bf16[5,48,32,32]{1,3,2,0:T(8,128)(2,1)} %copy-done.1) | copy-start | bytes 1474564
  127.3 13.4 %copy-start.5 = (bf16[5,48,32,32]{1,3,2,0:T(8,128)(2,1)S(1)}, bf16[5,48,32,32]{1,3,2,0:T(8,128)(2,1)}, u32[]{:S(2)}) copy-start(bf16[5,48,32,32]{1,3,2,0:T(8,128)(2,1)} %copy-done.4) | copy-start | bytes 1474564
  131.0 21.2 %collective-permute-start.5 = (bf16[2,48,32,32]{1,3,2,0:T(8,128)(2,1)}, bf16[2,48,32,32]{1,3,2,0:T(8,128)(2,1)S(1)}, u32[]{:S(2)}, u32[]{:S(2)}) collective-permute-start(bf16[2,48,32,32]{1,3,2,0:T(8,128)(2,1)} %get-tuple-element.797), channel_id=1, source_target_pairs={{4,0},{8,4},{12,8},{16,12},{20,16},{24,20},{28,24},{32,28},{36,32}... | collective-permute-start | bytes 589832 | tf_op jit(solution)/shard_map/ppermute | solution.py:17
  134.9 26.1 %collective-permute-start.3 = (bf16[2,48,32,32]{1,3,2,0:T(8,128)(2,1)}, bf16[2,48,32,32]{1,3,2,0:T(8,128)(2,1)S(1)}, u32[]{:S(2)}, u32[]{:S(2)}) collective-permute-start(bf16[2,48,32,32]{1,3,2,0:T(8,128)(2,1)} %get-tuple-element.799), channel_id=1, source_target_pairs={{4,0},{8,4},{12,8},{16,12},{20,16},{24,20},{28,24},{32,28},{36,32}... | collective-permute-start | bytes 589832 | tf_op jit(solution)/shard_map/ppermute | solution.py:17
  236.0 116.8 %copy-start.9 = (bf16[5]{0:T(256)(128)(2,1)S(1)}, bf16[5]{0:T(256)(128)(2,1)}, u32[]{:S(2)}) copy-start(bf16[5]{0:T(256)(128)(2,1)} %copy-done.8) | copy-start | bytes 34
  236.0 116.8 %copy-start.11 = (f32[48]{0:T(128)S(1)}, f32[48]{0:T(128)}, u32[]{:S(2)}) copy-start(f32[48]{0:T(128)} %param.21) | copy-start | bytes 580
  357.1 66.7 %copy-start = (f32[5,48,32,32]{1,3,2,0:T(8,128)S(1)}, f32[5,48,32,32]{1,3,2,0:T(8,128)}, u32[]{:S(2)}) copy-start(f32[5,48,32,32]{1,3,2,0:T(8,128)} %custom-call.1) | copy-start | bytes 2949124
  423.8 70.8 %copy-start.14 = (f32[48]{0:T(128)S(1)}, f32[48]{0:T(128)}, u32[]{:S(2)}) copy-start(f32[48]{0:T(128)} %param.23) | copy-start | bytes 580
Sparse Core Ops, SparseCore 0:
  494.7 244.2 all-reduce.6
where the time goes:
time: 760 us; the launch traced here: 749 us
  matrix products  379 us (50%)
  waiting for transfers between devices  205 us (27%)
  blocking collectives  69.2 us (9%)
  local copies, waits for them, and re-layouts  38.5 us (5%)
  starting transfers between devices  18.7 us (2%)
  between operations  15 us (2%)
  other arithmetic  12.8 us (2%)
  loops' own time  11 us (1%)
    dot_general x81, matrix products, conv_add_tap(): jnp.einsum('ok,pkij->poij', w_tap, piece, preferred_element_type=jnp.floa...  253 us
    psum x1, waiting for transfers between devices, local(): lax.psum((grad_first, grad_second, bias_first, bias_second), ('box', 'sna...  171 us
    dot_general x54, matrix products, weight_add_tap(): jnp.einsum('poij,pkij->ok', grads, piece, preferred_element_type=jnp.floa...  126 us
    psum x1, blocking collectives, local(): lax.psum((grad_first, grad_second, bias_first, bias_second), ('box', 'sna...  69.2 us
    ppermute x3, waiting for transfers between devices, extended_2(): lax.ppermute(lax.slice_in_dim(block, 0, width, axis=dim), axis, backward)  23.8 us
  transfers between devices with their start and end apart: 7, of which 6 were waited for; matrix products, arithmetic and copies ran while one was open for 3% of the time, Pallas kernels for 0%

commit v1 on v0

v1 whole, which is shorter than its diff:
```python
import functools

import jax
import jax.numpy as jnp
from jax import lax
from jax.experimental import pallas as pl
from jax.experimental.pallas import tpu as pltpu
from jax.sharding import PartitionSpec as P

C = 48
SLOTS = 5
CELLS = 1024
ROWS = 3 * C
TAPS9 = 9 * C
WIDE = CELLS + 256
CHUNK = 256
F32 = jnp.float32
BF16 = jnp.bfloat16


def lane_masks():
    lane = lax.broadcasted_iota(jnp.int32, (C, 128), 1)
    col = lane % 32

    def pick(cond):
        return jnp.where(cond, 1.0, 0.0).astype(BF16)

    return pick(lane < 64), pick(lane >= 64), pick(col >= 2), pick(col < 30)


def roll(v, shift):
    return pltpu.roll(v, shift, 1)


def to_halves(v, masks):
    low, high = masks[:2]
    orig = [v[:, 128 * h : 128 * h + 128] for h in range(8)]
    turned = [roll(o, 64) for o in orig]
    out = []
    for g in range(8):
        m = g // 2
        if g % 2 == 0:
            out.append(orig[m] * low + turned[4 + m] * high)
        else:
            out.append(turned[m] * low + orig[4 + m] * high)
    return out


def from_halves(parts, masks):
    low, high = masks[:2]
    turned = [roll(p, 64) for p in parts]
    first = [parts[2 * m] * low + turned[2 * m + 1] * high for m in range(4)]
    second = [turned[2 * m] * low + parts[2 * m + 1] * high for m in range(4)]
    return first + second


def put_shifts(parts, dst, at, masks):
    low, high, ge2, lt30 = masks
    before = roll(parts[7], 64) * high
    after = roll(parts[0], 64) * low
    for g, t in enumerate([before] + parts + [after]):
        cols = slice(128 * g, 128 * g + 128)
        dst[at, 0:C, cols] = roll(t, 2) * ge2
        dst[at, C : 2 * C, cols] = t
        dst[at, 2 * C : ROWS, cols] = roll(t, 126) * lt30


def split(v):
    return [v[:, 128 * g : 128 * g + 128] for g in range(8)]


def put_zeros(dst, at):
    dst[at] = jnp.zeros((ROWS, WIDE), BF16)


def taps(src, at, start, size):
    return jnp.concatenate(
        [src[at, :, 128 * b + start : 128 * b + start + size] for b in range(3)], axis=0
    )


def outputs_of(e):
    return [(e - 2 * s, s) for s in range(3) if 0 <= e - 2 * s < SLOTS]


def conv_into(acc, w, src):
    seen = set()
    for e in range(SLOTS + 4):
        pairs = outputs_of(e)
        lo, hi = pairs[0][1], pairs[-1][1] + 1
        lhs = w[lo * C : hi * C, :]
        for start in range(0, CELLS, CHUNK):
            y = jnp.dot(lhs, taps(src, e, start, CHUNK), preferred_element_type=F32)
            for p, s in pairs:
                piece = y[(s - lo) * C : (s - lo + 1) * C]
                cols = slice(start, start + CHUNK)
                if (p, start) in seen:
                    acc[p, :, cols] += piece
                else:
                    acc[p, :, cols] = piece
                    seen.add((p, start))


def lane_dot(a, b):
    return lax.dot_general(a, b, (((1,), (1,)), ((), ())), preferred_element_type=F32)


def main_kernel(
    count_ref, x_ref, u_ref, lo_ref, hi_ref, w1_ref, w2_ref, b1_ref,
    hid_ref, head_ref, tail_ref, pay_ref,
    px, pu, ph, w1s, w2s, acc1, acc2, pre, g1, g2,
):
    count = count_ref[0, 0]
    masks = lane_masks()
    for s in range(3):
        w1s[s * C : (s + 1) * C, :] = w1_ref[:, s * TAPS9 : (s + 1) * TAPS9]
    for t in range(27):
        block = w2_ref[:, t * C : (t + 1) * C].astype(F32).T.astype(BF16)
        back = 26 - t
        s, r = back // 9, back % 9
        w2s[s * C : (s + 1) * C, r * C : (r + 1) * C] = block
    for dst in (px, pu):
        put_zeros(dst, SLOTS + 2)
        put_zeros(dst, SLOTS + 3)
    for p in range(SLOTS):
        keep = jnp.where(p < count, 1.0, 0.0).astype(BF16)
        put_shifts(to_halves(x_ref[p] * keep, masks), px, p + 2, masks)
        put_shifts(to_halves(u_ref[p] * keep, masks), pu, p + 2, masks)
    for i in range(2):
        put_shifts(to_halves(lo_ref[i], masks), px, i, masks)
        put_shifts(to_halves(hi_ref[i], masks), px, count + 2 + i, masks)
        put_shifts(to_halves(lo_ref[2 + i], masks), pu, i, masks)
        put_shifts(to_halves(hi_ref[2 + i], masks), pu, count + 2 + i, masks)
    conv_into(acc1, w1s, px)
    conv_into(acc2, w2s, pu)
    bias1 = jnp.zeros((C, CELLS), F32)
    bias2 = jnp.zeros((C, CELLS), F32)
    for p in range(SLOTS):
        keep = jnp.where(p < count, 1.0, 0.0).astype(F32)
        z = acc1[p] + b1_ref[...]
        sig = 1.0 / (1.0 + jnp.exp(-z))
        hid = (z * sig * keep).astype(BF16)
        grad = (acc2[p] * (sig * (1.0 + z * (1.0 - sig))) * keep).astype(BF16)
        hid_ref[p] = hid
        pre[p] = grad
        put_shifts(split(hid), ph, p, masks)
        bias1 += grad.astype(F32)
        bias2 += pu[p + 2, C : 2 * C, 128 : 128 + CELLS].astype(F32) * keep
    for i in range(2):
        head_ref[i] = hid_ref[i]
        tail_ref[i] = hid_ref[count - 2 + i]
    for e in range(SLOTS + 4):
        pairs = outputs_of(e)
        lo, hi = pairs[0][1], pairs[-1][1] + 1
        lhs = jnp.concatenate([pre[p] for p, _ in pairs], axis=0)
        y = lane_dot(lhs, taps(px, e, 0, CELLS))
        if e == 0:
            g1[...] = jnp.zeros((ROWS, TAPS9), F32)
        g1[lo * C : hi * C, :] += y
    for q in range(SLOTS):
        lhs = jnp.concatenate(
            [pu[q + 4 - 2 * s, C : 2 * C, 128 : 128 + CELLS] for s in range(3)], axis=0
        )
        y = lane_dot(lhs, taps(ph, q, 0, CELLS))
        if q == 0:
            g2[...] = y
        else:
            g2[...] += y
    pay_ref[...] = jnp.zeros(pay_ref.shape, BF16)
    pay_ref[0:ROWS, 0:TAPS9] = g1[...].astype(BF16)
    pay_ref[ROWS : 2 * ROWS, 0:TAPS9] = g2[...].astype(BF16)
    pieces = []
    for bias in (bias1, bias2):
        total = jnp.sum(bias, axis=1, keepdims=True)
        high = total.astype(BF16)
        pieces += [high, (total - high.astype(F32)).astype(BF16)]
    pay_ref[0:C, TAPS9 : TAPS9 + 4] = jnp.concatenate(pieces, axis=1)


def spread_kernel(total_ref, g1_ref, g2_ref, bias_ref):
    for s in range(3):
        cols = slice(s * TAPS9, (s + 1) * TAPS9)
        g1_ref[:, cols] = total_ref[s * C : (s + 1) * C, 0:TAPS9].astype(F32)
        g2_ref[:, cols] = total_ref[ROWS + s * C : ROWS + (s + 1) * C, 0:TAPS9].astype(F32)
    four = total_ref[0:C, TAPS9 : TAPS9 + 4].astype(F32)
    bias_ref[...] = jnp.concatenate(
        [four[:, 0:1] + four[:, 1:2], four[:, 2:3] + four[:, 3:4]], axis=1
    )


def out_kernel(count_ref, hid_ref, lo_ref, hi_ref, w2_ref, b2_ref, out_ref, ph, w2s, acc):
    count = count_ref[0, 0]
    masks = lane_masks()
    for s in range(3):
        w2s[s * C : (s + 1) * C, :] = w2_ref[:, s * TAPS9 : (s + 1) * TAPS9]
    put_zeros(ph, SLOTS + 2)
    put_zeros(ph, SLOTS + 3)
    for p in range(SLOTS):
        put_shifts(split(hid_ref[p]), ph, p + 2, masks)
    for i in range(2):
        put_shifts(split(lo_ref[i]), ph, i, masks)
        put_shifts(split(hi_ref[i]), ph, count + 2 + i, masks)
    conv_into(acc, w2s, ph)
    for p in range(SLOTS):
        keep = jnp.where(p < count, 1.0, 0.0).astype(F32)
        z = ((acc[p] + b2_ref[...]) * keep).astype(BF16)
        for g, part in enumerate(from_halves(split(z), masks)):
            out_ref[0, p, :, 128 * g : 128 * g + 128] = part


VM = pl.BlockSpec(memory_space=pltpu.VMEM)
SM = pl.BlockSpec(memory_space=pltpu.SMEM)
PLANES_BF16 = jax.ShapeDtypeStruct((SLOTS, C, CELLS), BF16)
PAIR_BF16 = jax.ShapeDtypeStruct((2, C, CELLS), BF16)
LIMIT = 40 * 1024 * 1024


def run_main(count, x, u, lo, hi, w1, w2, b1, interpret):
    shifted = pltpu.VMEM((SLOTS + 4, ROWS, WIDE), BF16)
    return pl.pallas_call(
        main_kernel,
        out_shape=(
            PLANES_BF16,
            PAIR_BF16,
            PAIR_BF16,
            jax.ShapeDtypeStruct((512, 512), BF16),
        ),
        in_specs=[SM] + [VM] * 7,
        out_specs=[VM] * 4,
        scratch_shapes=[
            shifted,
            shifted,
            pltpu.VMEM((SLOTS, ROWS, WIDE), BF16),
            pltpu.VMEM((ROWS, TAPS9), BF16),
            pltpu.VMEM((ROWS, TAPS9), BF16),
            pltpu.VMEM((SLOTS, C, CELLS), F32),
            pltpu.VMEM((SLOTS, C, CELLS), F32),
            pltpu.VMEM((SLOTS, C, CELLS), BF16),
            pltpu.VMEM((ROWS, TAPS9), F32),
            pltpu.VMEM((ROWS, TAPS9), F32),
        ],
        compiler_params=pltpu.CompilerParams(vmem_limit_bytes=LIMIT),
        cost_estimate=pl.CostEstimate(flops=3_000_000_000, bytes_accessed=4_000_000, transcendentals=500_000),
        interpret=interpret,
        name="grads",
    )(count, x, u, lo, hi, w1, w2, b1)


def run_out(count, hid, lo, hi, w2, b2, interpret):
    return pl.pallas_call(
        out_kernel,
        out_shape=jax.ShapeDtypeStruct((1, SLOTS, C, CELLS), BF16),
        in_specs=[SM] + [VM] * 5,
        out_specs=VM,
        scratch_shapes=[
            pltpu.VMEM((SLOTS + 4, ROWS, WIDE), BF16),
            pltpu.VMEM((ROWS, TAPS9), BF16),
            pltpu.VMEM((SLOTS, C, CELLS), F32),
        ],
        compiler_params=pltpu.CompilerParams(vmem_limit_bytes=LIMIT),
        cost_estimate=pl.CostEstimate(flops=1_000_000_000, bytes_accessed=2_000_000, transcendentals=0),
        interpret=interpret,
        name="decode",
    )(count, hid, lo, hi, w2, b2)


def run_spread(total, interpret):
    grad = jax.ShapeDtypeStruct((C, 27 * C), F32)
    return pl.pallas_call(
        spread_kernel,
        out_shape=(grad, grad, jax.ShapeDtypeStruct((C, 2), F32)),
        in_specs=[VM],
        out_specs=[VM] * 3,
        interpret=interpret,
        name="spread",
    )(total)


def all_reduced(pay, axes):
    parts = lax.axis_size(axes)
    tiles = pay.reshape(64, 8, 4, 128).transpose(0, 2, 1, 3).reshape(parts, -1, 128)
    mine = lax.all_to_all(tiles, axes, 0, 0, tiled=True)
    total = jnp.sum(mine.astype(F32), axis=0, keepdims=True).astype(BF16)
    spread = jnp.broadcast_to(total, (parts,) + total.shape[1:])
    tiles = lax.all_to_all(spread, axes, 0, 0, tiled=True)
    return tiles.reshape(64, 4, 8, 128).transpose(0, 2, 1, 3).reshape(512, 512)


def local(interpret, fields, cotangent, plane_counts, w_first, b_first, w_second, b_second):
    count = plane_counts[0, 0]
    x = fields[0]
    u = cotangent[0]
    size = lax.axis_size("box")
    forward = [(i, i + 1) for i in range(size - 1)]
    backward = [(i + 1, i) for i in range(size - 1)]
    zero = jnp.zeros((), jnp.int32)
    last = lambda v: lax.dynamic_slice(v, (count - 2, zero, zero), (2, C, CELLS))
    lo = lax.ppermute(jnp.concatenate([last(x), last(u)], axis=0), "box", forward)
    hi = lax.ppermute(jnp.concatenate([x[0:2], u[0:2]], axis=0), "box", backward)
    hid, head, tail, pay = run_main(
        plane_counts, x, u, lo, hi, w_first, w_second, b_first[:, None], interpret
    )
    hid_lo = lax.ppermute(tail, "box", forward)
    hid_hi = lax.ppermute(head, "box", backward)
    total = all_reduced(pay, ("box", "snap"))
    decoded = run_out(plane_counts, hid, hid_lo, hid_hi, w_second, b_second[:, None], interpret)
    grad_first, grad_second, bias = run_spread(total, interpret)
    return decoded, grad_first, grad_second, bias[:, 0], bias[:, 1]


def solution(mesh, interpret=False):
    return jax.shard_map(
        functools.partial(local, interpret),
        mesh=mesh,
        in_specs=(
            P("snap", "box", None, None),
            P("snap", "box", None, None),
            P("snap", "box"),
            P(),
            P(),
            P(),
            P(),
        ),
        out_specs=(P("snap", "box", None, None), P(), P(), P(), P()),
        check_vma=False,
    )
```

time: 760 us -> 99.2 us (0.13)
  the two profiles are of different devices: /device:TPU:126 before, /device:TPU:1 now
where the time goes in v1:
time: 99.2 us; the launch traced here: 98.8 us
  blocking collectives  44.6 us (45%)
  waiting for transfers between devices  19 us (19%)
  starting transfers between devices  15.6 us (16%)
  Pallas kernels  13.1 us (13%)
  local copies, waits for them, and re-layouts  4.69 us (5%)
  between operations  1.42 us (1%)
    all_to_all x1, blocking collectives, all_reduced(): mine = lax.all_to_all(tiles, axes, 0, 0, tiled=True)  44.6 us
    pallas_call x1, Pallas kernels, run_main(): pl.pallas_call(main_kernel, out_shape=(PLANES_BF16, PAIR_BF16, PAIR_BF16,...  8.02 us
    all_to_all x1, starting transfers between devices, all_reduced(): tiles = lax.all_to_all(spread, axes, 0, 0, tiled=True)  5.16 us
    ppermute x1, waiting for transfers between devices, local(): hid_hi = lax.ppermute(head, 'box', backward)  4.91 us
    ppermute x1, starting transfers between devices, local(): lax.ppermute(jnp.concatenate([last(x), last(u)], axis=0), 'box', forward)  4.81 us
    ppermute x1, waiting for transfers between devices, local(): hid_lo = lax.ppermute(tail, 'box', forward)  4.45 us
    ppermute x1, waiting for transfers between devices, local(): lax.ppermute(jnp.concatenate([x[0:2], u[0:2]], axis=0), 'box', backward)  4.3 us
    all_to_all x1, waiting for transfers between devices, all_reduced(): tiles = lax.all_to_all(spread, axes, 0, 0, tiled=True)  4.26 us
  transfers between devices with their start and end apart: 5, of which 5 were waited for; matrix products, arithmetic and copies ran while one was open for 0% of the time, Pallas kernels for 3%

profile of v1, /device:TPU:1, one launch (start us, length us, event | category | flops | bytes accessed | tf_op | source)
XLA Modules:
  0.0 98.8 jit_solution(2895228279871313831)
XLA Ops:
  1.3 1.3 %slice_bitcast_fusion = (bf16[2,48,1024]{2,1,0:T(8,128)(2,1)S(1)}, bf16[2,48,1024]{2,1,0:T(8,128)(2,1)S(1)}, bf16[2,48,1024]{2,1,0:T(8,128)(2,1)S(1)}, bf16[2,48,1024]{2,1,0:T(8,128)(2,1)S(1)}) fusion(bf16[1,5,48,1024]{3,2,1,0:T(8,128)(2,1)} %param.8, s32[]{:T(128)S(6)} %select_n.4, bf16[1,5,48,1024]{3,2,1,0:T(8,128)(2,1)} %param.7), kind=kLoop, calls=%fused_computation.2 | loop fusion | bytes 1572868 | tf_op jit(solution)/shard_map/slice | solution.py:299
  2.6 0.0 copy-start.1
  2.6 0.0 copy-start
  2.6 1.4 %collective-permute-start.1 = (bf16[4,48,1024]{2,1,0:T(8,128)(2,1)S(1)}, bf16[4,48,1024]{2,1,0:T(8,128)(2,1)S(1)}, u32[]{:S(2)}, u32[]{:S(2)}) collective-permute-start(bf16[4,48,1024]{2,1,0:T(8,128)(2,1)S(1)} %pad_maximum_fusion.1), channel_id=1, source_target_pairs={{4,0},{8,4},{12,8},{16,12},{20,16},{24,20},{28,24},{32,28},{36,32}... | collective-permute-start | bytes 1179656 | tf_op jit(solution)/shard_map/ppermute | solution.py:299
  4.1 0.0 copy-start.2
  4.1 0.0 copy-start.3
  4.1 0.0 copy-start.5
  4.1 4.8 %collective-permute-start = (bf16[4,48,1024]{2,1,0:T(8,128)(2,1)S(1)}, bf16[4,48,1024]{2,1,0:T(8,128)(2,1)S(1)}, u32[]{:S(2)}, u32[]{:S(2)}) collective-permute-start(bf16[4,48,1024]{2,1,0:T(8,128)(2,1)S(1)} %pad_maximum_fusion), channel_id=1, source_target_pairs={{0,4},{4,8},{8,12},{12,16},{16,20},{20,24},{24,28},{28,32},{32,36}... | collective-permute-start | bytes 1179656 | tf_op jit(solution)/shard_map/ppermute | solution.py:298
  9.0 0.0 copy-done.5
  9.0 0.1 copy.14.b1_ref
  9.1 4.3 %collective-permute-done.1.hi_ref = bf16[4,48,1024]{2,1,0:T(8,128)(2,1)S(1)} collective-permute-done((bf16[4,48,1024]{2,1,0:T(8,128)(2,1)S(1)}, bf16[4,48,1024]{2,1,0:T(8,128)(2,1)S(1)}, u32[]{:S(2)}, u32[]{:S(2)}) %collective-permute-start.1) | collective-permute-done | bytes 393248 | tf_op jit(solution)/shard_map/ppermute | solution.py:299
  13.4 1.1 %collective-permute-done.lo_ref = bf16[4,48,1024]{2,1,0:T(8,128)(2,1)S(1)} collective-permute-done((bf16[4,48,1024]{2,1,0:T(8,128)(2,1)S(1)}, bf16[4,48,1024]{2,1,0:T(8,128)(2,1)S(1)}, u32[]{:S(2)}, u32[]{:S(2)}) %collective-permute-start) | collective-permute-done | bytes 393248 | tf_op jit(solution)/shard_map/ppermute | solution.py:298
  14.5 0.0 copy-done.1
  14.5 0.0 copy-done
  14.5 0.0 copy-done.2
  14.5 0.0 copy-done.3
  14.5 8.0 %grads.1 = (bf16[5,48,1024]{2,1,0:T(8,128)(2,1)S(1)}, bf16[2,48,1024]{2,1,0:T(8,128)(2,1)S(1)}, bf16[2,48,1024]{2,1,0:T(8,128)(2,1)S(1)}, bf16[512,512]{1,0:T(8,128)(2,1)S(1)}) custom-call(s32[1,1]{1,0:T(1,128)S(6)} %copy.16.count_ref, bf16[5,48,1024]{2,1,0:T(8,128)(2,1)S(1)} %bitcast.25, bf16[5,48,1024]{2,1,0:T(8,128)(2,1)S(1)} %bitcast.26, ...), custom_call_target="tpu_custom_call" | custom-call | flops 3000000000 | bytes 4000000 | tf_op jit(solution)/shard_map/grads/pallas_call | solution.py:220
  22.5 44.6 %all_to_all.10 = bf16[256,8,128]{2,1,0:T(8,128)(2,1)S(1)} all-to-all(bf16[256,8,128]{2,1,0:T(8,128)(2,1)S(1)} %bitcast.24), channel_id=1, replica_groups=mesh['box'=64,'snap'=4] {'box','snap'}, dimensions={0} | all-to-all | bytes 1048576 | tf_op jit(solution)/shard_map/all_to_all | solution.py:282
  67.2 0.3 reduce_sum.12
  67.4 0.9 broadcast_in_dim.14
  68.3 5.2 %all-to-all-start.1 = ((bf16[256,8,128]{2,1,0:T(8,128)(2,1)}), bf16[256,8,128]{2,1,0:T(8,128)(2,1)S(1)}, u32[]{:S(2)}, u32[]{:S(2)}) async-start(bf16[256,8,128]{2,1,0:T(8,128)(2,1)} %broadcast_in_dim.14), calls=%async_computation.1 | async-start | bytes 1048576 | tf_op jit(solution)/shard_map/all_to_all | solution.py:285
  73.5 2.9 %collective-permute-start.2 = (bf16[2,48,1024]{2,1,0:T(8,128)(2,1)S(1)}, bf16[2,48,1024]{2,1,0:T(8,128)(2,1)S(1)}, u32[]{:S(2)}, u32[]{:S(2)}) collective-permute-start(bf16[2,48,1024]{2,1,0:T(8,128)(2,1)S(1)} %get-tuple-element.13), channel_id=1, source_target_pairs={{0,4},{4,8},{8,12},{12,16},{16,20},{20,24},{24,28},{28,32},{32,36}... | collective-permute-start | bytes 589832 | tf_op jit(solution)/shard_map/ppermute | solution.py:303
  76.3 0.0 copy-start.6
  76.3 1.3 %collective-permute-start.3 = (bf16[2,48,1024]{2,1,0:T(8,128)(2,1)S(1)}, bf16[2,48,1024]{2,1,0:T(8,128)(2,1)S(1)}, u32[]{:S(2)}, u32[]{:S(2)}) collective-permute-start(bf16[2,48,1024]{2,1,0:T(8,128)(2,1)S(1)} %get-tuple-element.14), channel_id=1, source_target_pairs={{4,0},{8,4},{12,8},{16,12},{20,16},{24,20},{28,24},{32,28},{36,32}... | collective-permute-start | bytes 589832 | tf_op jit(solution)/shard_map/ppermute | solution.py:304
  77.6 0.0 copy-done.6
  77.7 0.1 copy.15.b2_ref
  77.8 4.4 %collective-permute-done.2.lo_ref = bf16[2,48,1024]{2,1,0:T(8,128)(2,1)S(1)} collective-permute-done((bf16[2,48,1024]{2,1,0:T(8,128)(2,1)S(1)}, bf16[2,48,1024]{2,1,0:T(8,128)(2,1)S(1)}, u32[]{:S(2)}, u32[]{:S(2)}) %collective-permute-start.2) | collective-permute-done | bytes 196640 | tf_op jit(solution)/shard_map/ppermute | solution.py:303
  82.2 4.9 %collective-permute-done.3.hi_ref = bf16[2,48,1024]{2,1,0:T(8,128)(2,1)S(1)} collective-permute-done((bf16[2,48,1024]{2,1,0:T(8,128)(2,1)S(1)}, bf16[2,48,1024]{2,1,0:T(8,128)(2,1)S(1)}, u32[]{:S(2)}, u32[]{:S(2)}) %collective-permute-start.3) | collective-permute-done | bytes 196640 | tf_op jit(solution)/shard_map/ppermute | solution.py:304
  87.1 3.1 %decode.1 = bf16[1,5,48,1024]{3,2,1,0:T(8,128)(2,1)} custom-call(s32[1,1]{1,0:T(1,128)S(6)} %copy.16.count_ref, bf16[5,48,1024]{2,1,0:T(8,128)(2,1)S(1)} %get-tuple-element.12.hid_ref, bf16[2,48,1024]{2,1,0:T(8,128)(2,1)S(1)} %collective-permute-done.2.lo_ref, bf16[2,48,1024]{2,1,0:T(8,128)(2,1)S(1)} %collective-permute-done.3.hi_ref, ...), custom_call_target="tpu_custom_call" | custom-call | flops 1000000000 | bytes 2000000 | tf_op jit(solution)/shard_map/decode/pallas_call | solution.py:250
  90.2 4.3 %all-to-all-done.1 = bf16[256,8,128]{2,1,0:T(8,128)(2,1)S(1)} async-done(((bf16[256,8,128]{2,1,0:T(8,128)(2,1)}), bf16[256,8,128]{2,1,0:T(8,128)(2,1)S(1)}, u32[]{:S(2)}, u32[]{:S(2)}) %all-to-all-start.1) | async-done | bytes 524320 | tf_op jit(solution)/shard_map/all_to_all | solution.py:285
  94.5 0.0 copy-start.4
  94.5 0.8 copy-done.4
  95.3 1.9 %spread.1 = (f32[48,1296]{1,0:T(8,128)}, f32[48,1296]{1,0:T(8,128)}, f32[48,2]{1,0:T(8,128)}) custom-call(bf16[512,512]{1,0:T(8,128)(2,1)} %bitcast.27), custom_call_target="tpu_custom_call" | custom-call | tf_op jit(solution)/shard_map/spread/pallas_call | solution.py:269
  97.3 1.5 %slice_reduce_fusion = (f32[48]{0:T(128)}, f32[48]{0:T(128)}) fusion(f32[48,2]{1,0:T(8,128)} %get-tuple-element.18), kind=kLoop, calls=%fused_computation.6 | loop fusion | bytes 768 | tf_op jit(solution)/shard_map/slice | solution.py:308
  (2 shorter events, 0.1 us)
Async XLA Ops:
  2.6 11.9 %copy-start.1 = (bf16[1,5,48,1024]{3,2,1,0:T(8,128)(2,1)S(1)}, bf16[1,5,48,1024]{3,2,1,0:T(8,128)(2,1)}, u32[]{:S(2)}) copy-start(bf16[1,5,48,1024]{3,2,1,0:T(8,128)(2,1)} %param.8) | copy-start | bytes 1474564
  2.6 11.9 %copy-start = (bf16[1,5,48,1024]{3,2,1,0:T(8,128)(2,1)S(1)}, bf16[1,5,48,1024]{3,2,1,0:T(8,128)(2,1)}, u32[]{:S(2)}) copy-start(bf16[1,5,48,1024]{3,2,1,0:T(8,128)(2,1)} %param.7) | copy-start | bytes 1474564
  2.6 10.7 %collective-permute-start.1 = (bf16[4,48,1024]{2,1,0:T(8,128)(2,1)S(1)}, bf16[4,48,1024]{2,1,0:T(8,128)(2,1)S(1)}, u32[]{:S(2)}, u32[]{:S(2)}) collective-permute-start(bf16[4,48,1024]{2,1,0:T(8,128)(2,1)S(1)} %pad_maximum_fusion.1), channel_id=1, source_target_pairs={{4,0},{8,4},{12,8},{16,12},{20,16},{24,20},{28,24},{32,28},{36,32}... | collective-permute-start | bytes 1179656 | tf_op jit(solution)/shard_map/ppermute | solution.py:299
  4.1 10.4 %copy-start.2 = (bf16[48,1296]{1,0:T(8,128)(2,1)S(1)}, bf16[48,1296]{1,0:T(8,128)(2,1)}, u32[]{:S(2)}) copy-start(bf16[48,1296]{1,0:T(8,128)(2,1)} %w1_ref.1) | copy-start | bytes 373252
  4.1 10.4 %copy-start.3 = (bf16[48,1296]{1,0:T(8,128)(2,1)S(1)}, bf16[48,1296]{1,0:T(8,128)(2,1)}, u32[]{:S(2)}) copy-start(bf16[48,1296]{1,0:T(8,128)(2,1)} %w2_ref.3) | copy-start | bytes 373252
  4.1 4.8 %copy-start.5 = (f32[48]{0:T(128)S(1)}, f32[48]{0:T(128)}, u32[]{:S(2)}) copy-start(f32[48]{0:T(128)} %param.11) | copy-start | bytes 580
  4.1 10.3 %collective-permute-start = (bf16[4,48,1024]{2,1,0:T(8,128)(2,1)S(1)}, bf16[4,48,1024]{2,1,0:T(8,128)(2,1)S(1)}, u32[]{:S(2)}, u32[]{:S(2)}) collective-permute-start(bf16[4,48,1024]{2,1,0:T(8,128)(2,1)S(1)} %pad_maximum_fusion), channel_id=1, source_target_pairs={{0,4},{4,8},{8,12},{12,16},{16,20},{20,24},{24,28},{28,32},{32,36}... | collective-permute-start | bytes 1179656 | tf_op jit(solution)/shard_map/ppermute | solution.py:298
  68.3 26.2 %all-to-all-start.1 = ((bf16[256,8,128]{2,1,0:T(8,128)(2,1)}), bf16[256,8,128]{2,1,0:T(8,128)(2,1)S(1)}, u32[]{:S(2)}, u32[]{:S(2)}) async-start(bf16[256,8,128]{2,1,0:T(8,128)(2,1)} %broadcast_in_dim.14), calls=%async_computation.1 | async-start | bytes 1048576 | tf_op jit(solution)/shard_map/all_to_all | solution.py:285
  73.5 8.7 %collective-permute-start.2 = (bf16[2,48,1024]{2,1,0:T(8,128)(2,1)S(1)}, bf16[2,48,1024]{2,1,0:T(8,128)(2,1)S(1)}, u32[]{:S(2)}, u32[]{:S(2)}) collective-permute-start(bf16[2,48,1024]{2,1,0:T(8,128)(2,1)S(1)} %get-tuple-element.13), channel_id=1, source_target_pairs={{0,4},{4,8},{8,12},{12,16},{16,20},{20,24},{24,28},{28,32},{32,36}... | collective-permute-start | bytes 589832 | tf_op jit(solution)/shard_map/ppermute | solution.py:303
  76.3 1.3 %copy-start.6 = (f32[48]{0:T(128)S(1)}, f32[48]{0:T(128)}, u32[]{:S(2)}) copy-start(f32[48]{0:T(128)} %param.13) | copy-start | bytes 580
  76.3 10.8 %collective-permute-start.3 = (bf16[2,48,1024]{2,1,0:T(8,128)(2,1)S(1)}, bf16[2,48,1024]{2,1,0:T(8,128)(2,1)S(1)}, u32[]{:S(2)}, u32[]{:S(2)}) collective-permute-start(bf16[2,48,1024]{2,1,0:T(8,128)(2,1)S(1)} %get-tuple-element.14), channel_id=1, source_target_pairs={{4,0},{8,4},{12,8},{16,12},{20,16},{24,20},{28,24},{32,28},{36,32}... | collective-permute-start | bytes 589832 | tf_op jit(solution)/shard_map/ppermute | solution.py:304
  94.5 0.8 copy-start.4

commit v2 on v1

v2 whole, which is shorter than its diff:
```python
import functools

import jax
import jax.numpy as jnp
from jax import lax
from jax.experimental import pallas as pl
from jax.experimental.pallas import tpu as pltpu
from jax.sharding import PartitionSpec as P

C = 48
SLOTS = 5
CELLS = 1024
ROWS = 3 * C
TAPS9 = 9 * C
WIDE = CELLS + 256
CHUNK = 256
F32 = jnp.float32
BF16 = jnp.bfloat16


def lane_masks():
    lane = lax.broadcasted_iota(jnp.int32, (C, 128), 1)
    col = lane % 32

    def pick(cond):
        return jnp.where(cond, 1.0, 0.0).astype(BF16)

    return pick(lane < 64), pick(lane >= 64), pick(col >= 2), pick(col < 30)


def roll(v, shift):
    return pltpu.roll(v, shift, 1)


def to_halves(v, masks):
    low, high = masks[:2]
    orig = [v[:, 128 * h : 128 * h + 128] for h in range(8)]
    turned = [roll(o, 64) for o in orig]
    out = []
    for g in range(8):
        m = g // 2
        if g % 2 == 0:
            out.append(orig[m] * low + turned[4 + m] * high)
        else:
            out.append(turned[m] * low + orig[4 + m] * high)
    return out


def from_halves(parts, masks):
    low, high = masks[:2]
    turned = [roll(p, 64) for p in parts]
    first = [parts[2 * m] * low + turned[2 * m + 1] * high for m in range(4)]
    second = [turned[2 * m] * low + parts[2 * m + 1] * high for m in range(4)]
    return first + second


def put_shifts(parts, dst, at, masks):
    low, high, ge2, lt30 = masks
    before = roll(parts[7], 64) * high
    after = roll(parts[0], 64) * low
    for g, t in enumerate([before] + parts + [after]):
        cols = slice(128 * g, 128 * g + 128)
        dst[at, 0:C, cols] = roll(t, 2) * ge2
        dst[at, C : 2 * C, cols] = t
        dst[at, 2 * C : ROWS, cols] = roll(t, 126) * lt30


def split(v):
    return [v[:, 128 * g : 128 * g + 128] for g in range(8)]


def put_zeros(dst, at):
    dst[at] = jnp.zeros((ROWS, WIDE), BF16)


def taps(src, at, start, size):
    return jnp.concatenate(
        [src[at, :, 128 * b + start : 128 * b + start + size] for b in range(3)], axis=0
    )


def outputs_of(q):
    return [(q + 2 - 2 * s, s) for s in range(3) if 0 <= q + 2 - 2 * s < SLOTS]


def conv_local(acc, w, src):
    seen = set()
    for q in range(SLOTS):
        pairs = outputs_of(q)
        lo, hi = pairs[0][1], pairs[-1][1] + 1
        lhs = w[lo * C : hi * C, :]
        for start in range(0, CELLS, CHUNK):
            y = jnp.dot(lhs, taps(src, q, start, CHUNK), preferred_element_type=F32)
            cols = slice(start, start + CHUNK)
            for p, s in pairs:
                piece = y[(s - lo) * C : (s - lo + 1) * C]
                if (p, start) in seen:
                    acc[p, :, cols] += piece
                else:
                    acc[p, :, cols] = piece
                    seen.add((p, start))


def conv_halo(acc, w, src, count):
    for i in range(2):
        for start in range(0, CELLS, CHUNK):
            cols = slice(start, start + CHUNK)
            below = taps(src, i, start, CHUNK)
            acc[i, :, cols] += jnp.dot(w[0:C, :], below, preferred_element_type=F32)
            above = taps(src, 2 + i, start, CHUNK)
            y = jnp.dot(w[2 * C : 3 * C, :], above, preferred_element_type=F32)
            acc[count - 2 + i, :, cols] += y


def lane_dot(a, b):
    return lax.dot_general(a, b, (((1,), (1,)), ((), ())), preferred_element_type=F32)


def middle(ref, at):
    return ref[at, C : 2 * C, 128 : 128 + CELLS]


def stack_taps(w_ref, dst):
    for s in range(3):
        dst[s * C : (s + 1) * C, :] = w_ref[:, s * TAPS9 : (s + 1) * TAPS9]


def front_kernel(count_ref, x_ref, u_ref, w1_ref, w2_ref, px, pu, w2s, acc1, acc2, w1s):
    count = count_ref[0, 0]
    masks = lane_masks()
    stack_taps(w1_ref, w1s)
    turned = w2_ref[...].astype(F32).T
    for s in range(3):
        rows = [26 - 9 * s - r for r in range(9)]
        w2s[s * C : (s + 1) * C, :] = jnp.concatenate(
            [turned[t * C : (t + 1) * C] for t in rows], axis=1
        ).astype(BF16)
    for p in range(SLOTS):
        keep = jnp.where(p < count, 1.0, 0.0).astype(BF16)
        put_shifts(to_halves(x_ref[p] * keep, masks), px, p, masks)
        put_shifts(to_halves(u_ref[p] * keep, masks), pu, p, masks)
    conv_local(acc1, w1s, px)
    conv_local(acc2, w2s, pu)


def main_kernel(
    count_ref, px, pu, w2s, acc1, acc2, lo_ref, hi_ref, w1_ref, b1_ref,
    ph, head_ref, tail_ref, tiles,
    hx, hu, ue, w1s, more1, more2, pre, g1, g2,
):
    count = count_ref[0, 0]
    masks = lane_masks()
    stack_taps(w1_ref, w1s)
    for i in range(2):
        for src, at in ((lo_ref, i), (hi_ref, 2 + i)):
            put_shifts(to_halves(src[i], masks), hx, at, masks)
            put_shifts(to_halves(src[2 + i], masks), hu, at, masks)
    for p in range(SLOTS):
        more1[p] = acc1[p]
        more2[p] = acc2[p]
        ue[p + 2] = middle(pu, p)
    ue[SLOTS + 2] = jnp.zeros((C, CELLS), BF16)
    ue[SLOTS + 3] = jnp.zeros((C, CELLS), BF16)
    for i in range(2):
        ue[i] = middle(hu, i)
        ue[count + 2 + i] = middle(hu, 2 + i)
    conv_halo(more1, w1s, hx, count)
    conv_halo(more2, w2s, hu, count)
    bias1 = jnp.zeros((C, 128), F32)
    bias2 = jnp.zeros((C, 128), F32)
    for p in range(SLOTS):
        keep = jnp.where(p < count, 1.0, 0.0).astype(F32)
        parts = []
        for g in range(8):
            cols = slice(128 * g, 128 * g + 128)
            z = more1[p, :, cols] + b1_ref[...]
            sig = 1.0 / (1.0 + jnp.exp(-z))
            parts.append((z * sig * keep).astype(BF16))
            slope = sig * (1.0 + z * (1.0 - sig))
            grad = (more2[p, :, cols] * slope * keep).astype(BF16)
            pre[p, :, cols] = grad
            bias1 += grad.astype(F32)
            bias2 += pu[p, C : 2 * C, 128 * g + 128 : 128 * g + 256].astype(F32)
        put_shifts(parts, ph, p, masks)
    for i in range(2):
        head_ref[i] = middle(ph, i)
        tail_ref[i] = middle(ph, count - 2 + i)
    for q in range(SLOTS):
        lhs = jnp.concatenate([ue[q + 4 - 2 * s] for s in range(3)], axis=0)
        y = lane_dot(lhs, taps(ph, q, 0, CELLS))
        if q == 0:
            g2[...] = y
        else:
            g2[...] += y
    g1[...] = jnp.zeros((ROWS, TAPS9), F32)
    for q in range(SLOTS):
        pairs = outputs_of(q)
        lo, hi = pairs[0][1], pairs[-1][1] + 1
        lhs = jnp.concatenate([pre[p] for p, _ in pairs], axis=0)
        g1[lo * C : hi * C, :] += lane_dot(lhs, taps(px, q, 0, CELLS))
    for i in range(2):
        g1[0:C, :] += lane_dot(pre[i], taps(hx, i, 0, CELLS))
        g1[2 * C : ROWS, :] += lane_dot(pre[count - 2 + i], taps(hx, 2 + i, 0, CELLS))
    columns = []
    for bias in (bias1, bias2):
        total = jnp.sum(bias, axis=1, keepdims=True)
        high = total.astype(BF16).astype(F32)
        columns += [high, total - high]
    extra = jnp.concatenate(columns + [jnp.zeros((C, 28), F32)], axis=1)
    none = jnp.zeros((16, 32), F32)
    for j in range(9):
        ends = []
        for r in (2 * j, 2 * j + 1):
            src, row = (g1, r * 16) if r < 9 else (g2, r * 16 - ROWS)
            for l in range(3):
                tiles[r * 3 + l] = src[row : row + 16, 128 * l : 128 * l + 128].astype(BF16)
            ends.append(src[row : row + 16, 384:TAPS9])
        ends.append(extra[16 * j : 16 * j + 16] if j < 3 else none)
        tiles[54 + j] = jnp.concatenate(ends, axis=1).astype(BF16)
    tiles[63] = jnp.zeros((16, 128), BF16)


def spread_kernel(tiles, g1_ref, g2_ref, bias1_ref, bias2_ref):
    for r in range(18):
        out = g1_ref if r < 9 else g2_ref
        s, row = (r % 9) // 3, (r % 3) * 16
        parts = [tiles[r * 3 + l].astype(F32) for l in range(3)]
        at = C * (r % 2)
        parts.append(tiles[54 + r // 2].astype(F32)[:, at : at + C])
        out[row : row + 16, s * TAPS9 : (s + 1) * TAPS9] = jnp.concatenate(parts, axis=1)
    four = jnp.concatenate([tiles[54 + j].astype(F32)[:, 96:100] for j in range(3)], axis=0)
    row = lax.broadcasted_iota(jnp.int32, (C, C), 0)
    col = lax.broadcasted_iota(jnp.int32, (C, C), 1)
    for out, j in ((bias1_ref, 0), (bias2_ref, 2)):
        both = four[:, j : j + 1] + four[:, j + 1 : j + 2]
        out[...] = jnp.sum(jnp.where(row == col, both, 0.0), axis=0, keepdims=True)


def out_kernel(count_ref, ph, lo_ref, hi_ref, w2_ref, b2_ref, out_ref, hh, w2s, acc):
    count = count_ref[0, 0]
    masks = lane_masks()
    stack_taps(w2_ref, w2s)
    for i in range(2):
        put_shifts(split(lo_ref[i]), hh, i, masks)
        put_shifts(split(hi_ref[i]), hh, 2 + i, masks)
    conv_local(acc, w2s, ph)
    conv_halo(acc, w2s, hh, count)
    for p in range(SLOTS):
        keep = jnp.where(p < count, 1.0, 0.0).astype(F32)
        z = ((acc[p] + b2_ref[...]) * keep).astype(BF16)
        for g, part in enumerate(from_halves(split(z), masks)):
            out_ref[0, p, :, 128 * g : 128 * g + 128] = part


TILES = 64
VM = pl.BlockSpec(memory_space=pltpu.VMEM)
SM = pl.BlockSpec(memory_space=pltpu.SMEM)
PAIR_BF16 = jax.ShapeDtypeStruct((2, C, CELLS), BF16)
SHIFTED = jax.ShapeDtypeStruct((SLOTS, ROWS, WIDE), BF16)
SUMS = jax.ShapeDtypeStruct((SLOTS, C, CELLS), F32)
WEIGHT = (ROWS, TAPS9)
MIB = 1024 * 1024


def call(kernel, name, args, outs, scratch, limit, flops, interpret):
    return pl.pallas_call(
        kernel,
        out_shape=outs,
        in_specs=[SM if a.dtype == jnp.int32 else VM for a in args],
        out_specs=[VM] * len(outs),
        scratch_shapes=[pltpu.VMEM(shape, kind) for shape, kind in scratch],
        compiler_params=pltpu.CompilerParams(vmem_limit_bytes=limit * MIB),
        cost_estimate=pl.CostEstimate(flops=flops, bytes_accessed=2_000_000, transcendentals=0),
        interpret=interpret,
        name=name,
    )(*args)


def gradient_sum(tiles):
    axes = ("box", "snap")
    parts = lax.axis_size(axes)
    mine = lax.all_to_all(tiles.reshape(parts, -1, 128), axes, 0, 0, tiled=True)
    total = jnp.sum(mine.astype(F32), axis=0, keepdims=True).astype(BF16)
    spread = jnp.broadcast_to(total, (parts,) + total.shape[1:])
    return lax.all_to_all(spread, axes, 0, 0, tiled=True).reshape(TILES, 16, 128)


def local(interpret, fields, cotangent, plane_counts, w_first, b_first, w_second, b_second):
    count = plane_counts[0, 0]
    x = fields[0]
    u = cotangent[0]
    size = lax.axis_size("box")
    forward = [(i, i + 1) for i in range(size - 1)]
    backward = [(i + 1, i) for i in range(size - 1)]
    zero = jnp.zeros((), jnp.int32)
    last = lambda v: lax.dynamic_slice(v, (count - 2, zero, zero), (2, C, CELLS))
    lo = lax.ppermute(jnp.concatenate([last(x), last(u)], axis=0), "box", forward)
    hi = lax.ppermute(jnp.concatenate([x[0:2], u[0:2]], axis=0), "box", backward)
    px, pu, w2s, acc1, acc2 = call(
        front_kernel, "front", (plane_counts, x, u, w_first, w_second),
        (SHIFTED, SHIFTED, jax.ShapeDtypeStruct(WEIGHT, BF16), SUMS, SUMS),
        [(WEIGHT, BF16)], 16, 1_200_000_000, interpret,
    )
    halo = ((4, ROWS, WIDE), BF16)
    ph, head, tail, tiles = call(
        main_kernel, "grads",
        (plane_counts, px, pu, w2s, acc1, acc2, lo, hi, w_first, b_first[:, None]),
        (SHIFTED, PAIR_BF16, PAIR_BF16, jax.ShapeDtypeStruct((TILES, 16, 128), BF16)),
        [
            halo, halo, ((SLOTS + 4, C, CELLS), BF16), (WEIGHT, BF16),
            ((SLOTS, C, CELLS), F32), ((SLOTS, C, CELLS), F32), ((SLOTS, C, CELLS), BF16),
            (WEIGHT, F32), (WEIGHT, F32),
        ],
        32, 2_000_000_000, interpret,
    )
    hid_lo = lax.ppermute(tail, "box", forward)
    hid_hi = lax.ppermute(head, "box", backward)
    tiles = gradient_sum(tiles)
    (decoded,) = call(
        out_kernel, "decode", (plane_counts, ph, hid_lo, hid_hi, w_second, b_second[:, None]),
        (jax.ShapeDtypeStruct((1, SLOTS, C, CELLS), BF16),),
        [halo, (WEIGHT, BF16), ((SLOTS, C, CELLS), F32)], 20, 1_000_000_000, interpret,
    )
    grad = jax.ShapeDtypeStruct((C, 27 * C), F32)
    line = jax.ShapeDtypeStruct((1, C), F32)
    grad_first, grad_second, bias_first, bias_second = call(
        spread_kernel, "spread", (tiles,), (grad, grad, line, line), [], 8, 100_000_000, interpret,
    )
    return decoded, grad_first, grad_second, bias_first[0], bias_second[0]


def solution(mesh, interpret=False):
    return jax.shard_map(
        functools.partial(local, interpret),
        mesh=mesh,
        in_specs=(
            P("snap", "box", None, None),
            P("snap", "box", None, None),
            P("snap", "box"),
            P(),
            P(),
            P(),
            P(),
        ),
        out_specs=(P("snap", "box", None, None), P(), P(), P(), P()),
        check_vma=False,
    )
```

time: 99.2 us -> 87.9 us (0.89)
  the two profiles are of different devices: /device:TPU:1 before, /device:TPU:126 now
where the time goes in v2:
time: 87.9 us; the launch traced here: 87.6 us
  starting transfers between devices  24.6 us (28%)
  waiting for transfers between devices  22.1 us (25%)
  blocking collectives  20.4 us (23%)
  Pallas kernels  13.6 us (15%)
  local copies, waits for them, and re-layouts  5.03 us (6%)
  between operations  1.53 us (2%)
    all_to_all x1, blocking collectives, gradient_sum(): mine = lax.all_to_all(tiles.reshape(parts, -1, 128), axes, 0, 0, tiled=True)  20.4 us
    pallas_call x4, Pallas kernels, call(): pl.pallas_call(kernel, out_shape=outs, in_specs=[SM if a.dtype == jnp.int...  13.6 us
    all_to_all x1, starting transfers between devices, gradient_sum(): lax.all_to_all(spread, axes, 0, 0, tiled=True).reshape(TILES, 16, 128)  10.8 us
    ppermute x1, waiting for transfers between devices, local(): lax.ppermute(jnp.concatenate([x[0:2], u[0:2]], axis=0), 'box', backward)  8.38 us
    ppermute x1, waiting for transfers between devices, local(): hid_hi = lax.ppermute(head, 'box', backward)  7.75 us
    ppermute x1, starting transfers between devices, local(): lax.ppermute(jnp.concatenate([last(x), last(u)], axis=0), 'box', forward)  4.96 us
    ppermute x1, starting transfers between devices, local(): hid_lo = lax.ppermute(tail, 'box', forward)  4.93 us
    ppermute x1, waiting for transfers between devices, local(): hid_lo = lax.ppermute(tail, 'box', forward)  3 us
  transfers between devices with their start and end apart: 5, of which 4 were waited for; matrix products, arithmetic and copies ran while one was open for 0% of the time, Pallas kernels for 7%

profile of v2, /device:TPU:126, one launch (start us, length us, event | category | flops | bytes accessed | tf_op | source)
XLA Modules:
  0.0 87.6 jit_solution(6198384464918555296)
XLA Ops:
  0.6 0.0 copy-start
  0.6 0.0 copy-start.1
  0.7 0.0 copy-start.6
  0.7 0.0 copy-start.2
  0.7 0.0 copy-start.3
  1.4 1.3 %slice_bitcast_fusion = (bf16[2,48,1024]{2,1,0:T(8,128)(2,1)S(1)}, bf16[2,48,1024]{2,1,0:T(8,128)(2,1)S(1)}, bf16[2,48,1024]{2,1,0:T(8,128)(2,1)S(1)}, bf16[2,48,1024]{2,1,0:T(8,128)(2,1)S(1)}) fusion(bf16[1,5,48,1024]{3,2,1,0:T(8,128)(2,1)} %param.8, s32[]{:T(128)S(6)} %select_n.4, bf16[1,5,48,1024]{3,2,1,0:T(8,128)(2,1)} %param.7), kind=kLoop, calls=%fused_computation.2 | loop fusion | bytes 1572868 | tf_op jit(solution)/shard_map/slice | solution.py:298
  2.8 5.0 %collective-permute-start = (bf16[4,48,1024]{2,1,0:T(8,128)(2,1)S(1)}, bf16[4,48,1024]{2,1,0:T(8,128)(2,1)S(1)}, u32[]{:S(2)}, u32[]{:S(2)}) collective-permute-start(bf16[4,48,1024]{2,1,0:T(8,128)(2,1)S(1)} %pad_maximum_fusion), channel_id=1, source_target_pairs={{0,4},{4,8},{8,12},{12,16},{16,20},{20,24},{24,28},{28,32},{32,36}... | collective-permute-start | bytes 1179656 | tf_op jit(solution)/shard_map/ppermute | solution.py:297
  7.8 1.9 %collective-permute-start.1 = (bf16[4,48,1024]{2,1,0:T(8,128)(2,1)S(1)}, bf16[4,48,1024]{2,1,0:T(8,128)(2,1)S(1)}, u32[]{:S(2)}, u32[]{:S(2)}) collective-permute-start(bf16[4,48,1024]{2,1,0:T(8,128)(2,1)S(1)} %pad_maximum_fusion.1), channel_id=1, source_target_pairs={{4,0},{8,4},{12,8},{16,12},{20,16},{24,20},{28,24},{32,28},{36,32}... | collective-permute-start | bytes 1179656 | tf_op jit(solution)/shard_map/ppermute | solution.py:298
  9.7 0.0 copy-done.6
  9.7 0.1 copy.12.b1_ref
  9.8 0.0 copy-done
  9.8 0.0 copy-done.1
  9.8 0.0 copy-done.2
  9.8 0.0 copy-done.3
  9.8 3.3 %front.1 = (bf16[5,144,1280]{2,1,0:T(8,128)(2,1)S(1)}, bf16[5,144,1280]{2,1,0:T(8,128)(2,1)S(1)}, bf16[144,432]{1,0:T(8,128)(2,1)S(1)}, f32[5,48,1024]{2,1,0:T(8,128)S(1)}, f32[5,48,1024]{2,1,0:T(8,128)S(1)}) custom-call(s32[1,1]{1,0:T(1,128)S(6)} %copy.14.count_ref, bf16[5,48,1024]{2,1,0:T(8,128)(2,1)S(1)} %bitcast.18, bf16[5,48,1024]{2,1,0:T(8,128)(2,1)S(1)} %bitcast.19, ...), custom_call_target="tpu_custom_call" | custom-call | flops 1200000000 | bytes 2000000 | tf_op jit(solution)/shard_map/front/pallas_call | solution.py:266
  13.1 2.9 %collective-permute-done.lo_ref = bf16[4,48,1024]{2,1,0:T(8,128)(2,1)S(1)} collective-permute-done((bf16[4,48,1024]{2,1,0:T(8,128)(2,1)S(1)}, bf16[4,48,1024]{2,1,0:T(8,128)(2,1)S(1)}, u32[]{:S(2)}, u32[]{:S(2)}) %collective-permute-start) | collective-permute-done | bytes 393248 | tf_op jit(solution)/shard_map/ppermute | solution.py:297
  16.1 8.4 %collective-permute-done.1.hi_ref = bf16[4,48,1024]{2,1,0:T(8,128)(2,1)S(1)} collective-permute-done((bf16[4,48,1024]{2,1,0:T(8,128)(2,1)S(1)}, bf16[4,48,1024]{2,1,0:T(8,128)(2,1)S(1)}, u32[]{:S(2)}, u32[]{:S(2)}) %collective-permute-start.1) | collective-permute-done | bytes 393248 | tf_op jit(solution)/shard_map/ppermute | solution.py:298
  24.5 0.0 copy-start.7
  24.5 6.8 %grads.1 = (bf16[5,144,1280]{2,1,0:T(8,128)(2,1)S(1)}, bf16[2,48,1024]{2,1,0:T(8,128)(2,1)S(1)}, bf16[2,48,1024]{2,1,0:T(8,128)(2,1)S(1)}, bf16[64,16,128]{2,1,0:T(8,128)(2,1)S(1)}) custom-call(s32[1,1]{1,0:T(1,128)S(6)} %copy.14.count_ref, bf16[5,144,1280]{2,1,0:T(8,128)(2,1)S(1)} %get-tuple-element.18.px, bf16[5,144,1280]{2,1,0:T(8,128)(2,1)S(1)} %get-tuple-element.19.pu, ...), custom_call_target="tpu_custom_call" | custom-call | flops 2000000000 | bytes 2000000 | tf_op jit(solution)/shard_map/grads/pallas_call | solution.py:266
  31.3 0.0 copy-start.4
  31.3 1.3 %copy-done.4 = bf16[5,144,1280]{2,1,0:T(8,128)(2,1)} copy-done((bf16[5,144,1280]{2,1,0:T(8,128)(2,1)}, bf16[5,144,1280]{2,1,0:T(8,128)(2,1)S(1)}, u32[]{:S(2)}) %copy-start.4) | copy-done | bytes 1843224
  32.5 20.4 %all_to_all.10 = bf16[256,4,128]{2,1,0:T(4,128)(2,1)S(1)} all-to-all(bf16[256,4,128]{2,1,0:T(4,128)(2,1)S(1)} %bitcast.21), channel_id=1, replica_groups=mesh['box'=64,'snap'=4] {'box','snap'}, dimensions={0} | all-to-all | bytes 524288 | tf_op jit(solution)/shard_map/all_to_all | solution.py:282
  53.0 0.3 reduce_sum.12
  53.3 0.8 broadcast_in_dim.14
  54.0 10.8 %all-to-all-start.1 = ((bf16[256,4,128]{2,1,0:T(4,128)(2,1)}), bf16[256,4,128]{2,1,0:T(4,128)(2,1)S(1)}, u32[]{:S(2)}, u32[]{:S(2)}) async-start(bf16[256,4,128]{2,1,0:T(4,128)(2,1)} %broadcast_in_dim.14), calls=%async_computation.1 | async-start | bytes 524288 | tf_op jit(solution)/shard_map/all_to_all | solution.py:285
  64.9 4.9 %collective-permute-start.2 = (bf16[2,48,1024]{2,1,0:T(8,128)(2,1)S(1)}, bf16[2,48,1024]{2,1,0:T(8,128)(2,1)S(1)}, u32[]{:S(2)}, u32[]{:S(2)}) collective-permute-start(bf16[2,48,1024]{2,1,0:T(8,128)(2,1)S(1)} %get-tuple-element.24), channel_id=1, source_target_pairs={{0,4},{4,8},{8,12},{12,16},{16,20},{20,24},{24,28},{28,32},{32,36}... | collective-permute-start | bytes 589832 | tf_op jit(solution)/shard_map/ppermute | solution.py:316
  69.8 1.9 %collective-permute-start.3 = (bf16[2,48,1024]{2,1,0:T(8,128)(2,1)S(1)}, bf16[2,48,1024]{2,1,0:T(8,128)(2,1)S(1)}, u32[]{:S(2)}, u32[]{:S(2)}) collective-permute-start(bf16[2,48,1024]{2,1,0:T(8,128)(2,1)S(1)} %get-tuple-element.25), channel_id=1, source_target_pairs={{4,0},{8,4},{12,8},{16,12},{20,16},{24,20},{28,24},{32,28},{36,32}... | collective-permute-start | bytes 589832 | tf_op jit(solution)/shard_map/ppermute | solution.py:317
  71.7 0.0 copy-done.7
  71.8 0.1 copy.13.b2_ref
  71.8 3.0 %collective-permute-done.2.lo_ref = bf16[2,48,1024]{2,1,0:T(8,128)(2,1)S(1)} collective-permute-done((bf16[2,48,1024]{2,1,0:T(8,128)(2,1)S(1)}, bf16[2,48,1024]{2,1,0:T(8,128)(2,1)S(1)}, u32[]{:S(2)}, u32[]{:S(2)}) %collective-permute-start.2) | collective-permute-done | bytes 196640 | tf_op jit(solution)/shard_map/ppermute | solution.py:316
  74.8 7.8 %collective-permute-done.3.hi_ref = bf16[2,48,1024]{2,1,0:T(8,128)(2,1)S(1)} collective-permute-done((bf16[2,48,1024]{2,1,0:T(8,128)(2,1)S(1)}, bf16[2,48,1024]{2,1,0:T(8,128)(2,1)S(1)}, u32[]{:S(2)}, u32[]{:S(2)}) %collective-permute-start.3) | collective-permute-done | bytes 196640 | tf_op jit(solution)/shard_map/ppermute | solution.py:317
  82.6 0.0 copy-start.5
  82.6 1.5 %copy-done.5 = bf16[5,144,1280]{2,1,0:T(8,128)(2,1)S(1)} copy-done((bf16[5,144,1280]{2,1,0:T(8,128)(2,1)S(1)}, bf16[5,144,1280]{2,1,0:T(8,128)(2,1)}, u32[]{:S(2)}) %copy-start.5) | copy-done | bytes 1843224
  84.1 2.5 %decode.1 = bf16[1,5,48,1024]{3,2,1,0:T(8,128)(2,1)} custom-call(s32[1,1]{1,0:T(1,128)S(6)} %copy.14.count_ref, bf16[5,144,1280]{2,1,0:T(8,128)(2,1)S(1)} %copy-done.5, bf16[2,48,1024]{2,1,0:T(8,128)(2,1)S(1)} %collective-permute-done.2.lo_ref, bf16[2,48,1024]{2,1,0:T(8,128)(2,1)S(1)} %collective-permute-done.3.hi_ref, bf16[48,1296]{1,0:T(8,128)(2,1)S(1)} %copy-done.3, ...), custom_call_target="tpu_custom_call" | custom-call | flops 1000000000 | bytes 2000000 | tf_op jit(solution)/shard_map/decode/pallas_call | solution.py:266
  86.6 0.0 all-to-all-done.1
  86.6 1.0 %spread.1 = (f32[48,1296]{1,0:T(8,128)}, f32[48,1296]{1,0:T(8,128)}, f32[1,48]{1,0:T(1,128)}, f32[1,48]{1,0:T(1,128)}) custom-call(bf16[64,16,128]{2,1,0:T(8,128)(2,1)S(1)} %bitcast.20), custom_call_target="tpu_custom_call" | custom-call | flops 100000000 | bytes 2000000 | tf_op jit(solution)/shard_map/spread/pallas_call | solution.py:266
  (2 shorter events, 0.1 us)
Async XLA Ops:
  0.6 9.2 %copy-start = (bf16[1,5,48,1024]{3,2,1,0:T(8,128)(2,1)S(1)}, bf16[1,5,48,1024]{3,2,1,0:T(8,128)(2,1)}, u32[]{:S(2)}) copy-start(bf16[1,5,48,1024]{3,2,1,0:T(8,128)(2,1)} %param.7) | copy-start | bytes 1474564
  0.6 9.2 %copy-start.1 = (bf16[1,5,48,1024]{3,2,1,0:T(8,128)(2,1)S(1)}, bf16[1,5,48,1024]{3,2,1,0:T(8,128)(2,1)}, u32[]{:S(2)}) copy-start(bf16[1,5,48,1024]{3,2,1,0:T(8,128)(2,1)} %param.8) | copy-start | bytes 1474564
  0.7 9.0 %copy-start.6 = (f32[48]{0:T(128)S(1)}, f32[48]{0:T(128)}, u32[]{:S(2)}) copy-start(f32[48]{0:T(128)} %param.11) | copy-start | bytes 580
  0.7 9.1 %copy-start.2 = (bf16[48,1296]{1,0:T(8,128)(2,1)S(1)}, bf16[48,1296]{1,0:T(8,128)(2,1)}, u32[]{:S(2)}) copy-start(bf16[48,1296]{1,0:T(8,128)(2,1)} %w1_ref.3) | copy-start | bytes 373252
  0.7 9.1 %copy-start.3 = (bf16[48,1296]{1,0:T(8,128)(2,1)S(1)}, bf16[48,1296]{1,0:T(8,128)(2,1)}, u32[]{:S(2)}) copy-start(bf16[48,1296]{1,0:T(8,128)(2,1)} %w2_ref.3) | copy-start | bytes 373252
  2.8 13.3 %collective-permute-start = (bf16[4,48,1024]{2,1,0:T(8,128)(2,1)S(1)}, bf16[4,48,1024]{2,1,0:T(8,128)(2,1)S(1)}, u32[]{:S(2)}, u32[]{:S(2)}) collective-permute-start(bf16[4,48,1024]{2,1,0:T(8,128)(2,1)S(1)} %pad_maximum_fusion), channel_id=1, source_target_pairs={{0,4},{4,8},{8,12},{12,16},{16,20},{20,24},{24,28},{28,32},{32,36}... | collective-permute-start | bytes 1179656 | tf_op jit(solution)/shard_map/ppermute | solution.py:297
  7.8 16.7 %collective-permute-start.1 = (bf16[4,48,1024]{2,1,0:T(8,128)(2,1)S(1)}, bf16[4,48,1024]{2,1,0:T(8,128)(2,1)S(1)}, u32[]{:S(2)}, u32[]{:S(2)}) collective-permute-start(bf16[4,48,1024]{2,1,0:T(8,128)(2,1)S(1)} %pad_maximum_fusion.1), channel_id=1, source_target_pairs={{4,0},{8,4},{12,8},{16,12},{20,16},{24,20},{28,24},{32,28},{36,32}... | collective-permute-start | bytes 1179656 | tf_op jit(solution)/shard_map/ppermute | solution.py:298
  24.5 47.3 %copy-start.7 = (f32[48]{0:T(128)S(1)}, f32[48]{0:T(128)}, u32[]{:S(2)}) copy-start(f32[48]{0:T(128)} %param.13) | copy-start | bytes 580
  31.3 1.3 %copy-start.4 = (bf16[5,144,1280]{2,1,0:T(8,128)(2,1)}, bf16[5,144,1280]{2,1,0:T(8,128)(2,1)S(1)}, u32[]{:S(2)}) copy-start(bf16[5,144,1280]{2,1,0:T(8,128)(2,1)S(1)} %get-tuple-element.23.ph) | copy-start | bytes 5529604
  54.0 32.6 %all-to-all-start.1 = ((bf16[256,4,128]{2,1,0:T(4,128)(2,1)}), bf16[256,4,128]{2,1,0:T(4,128)(2,1)S(1)}, u32[]{:S(2)}, u32[]{:S(2)}) async-start(bf16[256,4,128]{2,1,0:T(4,128)(2,1)} %broadcast_in_dim.14), calls=%async_computation.1 | async-start | bytes 524288 | tf_op jit(solution)/shard_map/all_to_all | solution.py:285
  64.9 10.0 %collective-permute-start.2 = (bf16[2,48,1024]{2,1,0:T(8,128)(2,1)S(1)}, bf16[2,48,1024]{2,1,0:T(8,128)(2,1)S(1)}, u32[]{:S(2)}, u32[]{:S(2)}) collective-permute-start(bf16[2,48,1024]{2,1,0:T(8,128)(2,1)S(1)} %get-tuple-element.24), channel_id=1, source_target_pairs={{0,4},{4,8},{8,12},{12,16},{16,20},{20,24},{24,28},{28,32},{32,36}... | collective-permute-start | bytes 589832 | tf_op jit(solution)/shard_map/ppermute | solution.py:316
  69.8 12.8 %collective-permute-start.3 = (bf16[2,48,1024]{2,1,0:T(8,128)(2,1)S(1)}, bf16[2,48,1024]{2,1,0:T(8,128)(2,1)S(1)}, u32[]{:S(2)}, u32[]{:S(2)}) collective-permute-start(bf16[2,48,1024]{2,1,0:T(8,128)(2,1)S(1)} %get-tuple-element.25), channel_id=1, source_target_pairs={{4,0},{8,4},{12,8},{16,12},{20,16},{24,20},{28,24},{32,28},{36,32}... | collective-permute-start | bytes 589832 | tf_op jit(solution)/shard_map/ppermute | solution.py:317
  82.6 1.5 %copy-start.5 = (bf16[5,144,1280]{2,1,0:T(8,128)(2,1)S(1)}, bf16[5,144,1280]{2,1,0:T(8,128)(2,1)}, u32[]{:S(2)}) copy-start(bf16[5,144,1280]{2,1,0:T(8,128)(2,1)} %copy-done.4) | copy-start | bytes 5529604

commit v3 on v2

--- a/solution.py
+++ b/solution.py
@@ -116,6 +116,22 @@
     return lax.dot_general(a, b, (((1,), (1,)), ((), ())), preferred_element_type=F32)
 
 
+def padded(parts, masks):
+    low, high = masks[:2]
+    return [roll(parts[7], 64) * high] + parts + [roll(parts[0], 64) * low]
+
+
+def rows_of(src, planes):
+    pieces = [
+        src[p, :, 128 * (2 - b) : 128 * (2 - b) + CELLS] for p in planes for b in range(3)
+    ]
+    return jnp.concatenate(pieces, axis=0)
+
+
+def center(src, at):
+    return src[at, :, 128 : 128 + CELLS]
+
+
 def middle(ref, at):
     return ref[at, C : 2 * C, 128 : 128 + CELLS]
 
@@ -145,8 +161,8 @@
 
 def main_kernel(
     count_ref, px, pu, w2s, acc1, acc2, lo_ref, hi_ref, w1_ref, b1_ref,
-    ph, head_ref, tail_ref, tiles,
-    hx, hu, ue, w1s, more1, more2, pre, g1, g2,
+    hid, head_ref, tail_ref, tiles,
+    ph, hx, hu, ue, w1s, more1, more2, pre, g1, g2,
 ):
     count = count_ref[0, 0]
     masks = lane_masks()
@@ -158,12 +174,12 @@
     for p in range(SLOTS):
         more1[p] = acc1[p]
         more2[p] = acc2[p]
-        ue[p + 2] = middle(pu, p)
-    ue[SLOTS + 2] = jnp.zeros((C, CELLS), BF16)
-    ue[SLOTS + 3] = jnp.zeros((C, CELLS), BF16)
-    for i in range(2):
-        ue[i] = middle(hu, i)
-        ue[count + 2 + i] = middle(hu, 2 + i)
+        ue[p + 2] = pu[p, C : 2 * C, :]
+    ue[SLOTS + 2] = jnp.zeros((C, WIDE), BF16)
+    ue[SLOTS + 3] = jnp.zeros((C, WIDE), BF16)
+    for i in range(2):
+        ue[i] = hu[i, C : 2 * C, :]
+        ue[count + 2 + i] = hu[2 + i, C : 2 * C, :]
     conv_halo(more1, w1s, hx, count)
     conv_halo(more2, w2s, hu, count)
     bias1 = jnp.zeros((C, 128), F32)
@@ -171,6 +187,7 @@
     for p in range(SLOTS):
         keep = jnp.where(p < count, 1.0, 0.0).astype(F32)
         parts = []
+        grads = []
         for g in range(8):
             cols = slice(128 * g, 128 * g + 128)
             z = more1[p, :, cols] + b1_ref[...]
@@ -178,57 +195,63 @@
             parts.append((z * sig * keep).astype(BF16))
             slope = sig * (1.0 + z * (1.0 - sig))
             grad = (more2[p, :, cols] * slope * keep).astype(BF16)
-            pre[p, :, cols] = grad
+            grads.append(grad)
             bias1 += grad.astype(F32)
             bias2 += pu[p, C : 2 * C, 128 * g + 128 : 128 * g + 256].astype(F32)
         put_shifts(parts, ph, p, masks)
+        for g, t in enumerate(padded(grads, masks)):
+            pre[p, :, 128 * g : 128 * g + 128] = t
+    for p in range(SLOTS):
+        hid[p] = middle(ph, p)
     for i in range(2):
         head_ref[i] = middle(ph, i)
         tail_ref[i] = middle(ph, count - 2 + i)
     for q in range(SLOTS):
-        lhs = jnp.concatenate([ue[q + 4 - 2 * s] for s in range(3)], axis=0)
-        y = lane_dot(lhs, taps(ph, q, 0, CELLS))
+        y = lane_dot(rows_of(ue, [q + 4, q + 2, q]), center(ph, q))
         if q == 0:
             g2[...] = y
         else:
             g2[...] += y
-    g1[...] = jnp.zeros((ROWS, TAPS9), F32)
+    g1[...] = jnp.zeros((TAPS9, ROWS), F32)
     for q in range(SLOTS):
         pairs = outputs_of(q)
         lo, hi = pairs[0][1], pairs[-1][1] + 1
-        lhs = jnp.concatenate([pre[p] for p, _ in pairs], axis=0)
-        g1[lo * C : hi * C, :] += lane_dot(lhs, taps(px, q, 0, CELLS))
-    for i in range(2):
-        g1[0:C, :] += lane_dot(pre[i], taps(hx, i, 0, CELLS))
-        g1[2 * C : ROWS, :] += lane_dot(pre[count - 2 + i], taps(hx, 2 + i, 0, CELLS))
+        y = lane_dot(rows_of(pre, [p for p, _ in pairs]), center(px, q))
+        g1[lo * ROWS : hi * ROWS, :] += y
+    for i in range(2):
+        g1[0:ROWS, :] += lane_dot(rows_of(pre, [i]), center(hx, i))
+        y = lane_dot(rows_of(pre, [count - 2 + i]), center(hx, 2 + i))
+        g1[2 * ROWS : TAPS9, :] += y
     columns = []
     for bias in (bias1, bias2):
         total = jnp.sum(bias, axis=1, keepdims=True)
         high = total.astype(BF16).astype(F32)
         columns += [high, total - high]
-    extra = jnp.concatenate(columns + [jnp.zeros((C, 28), F32)], axis=1)
-    none = jnp.zeros((16, 32), F32)
-    for j in range(9):
-        ends = []
-        for r in (2 * j, 2 * j + 1):
-            src, row = (g1, r * 16) if r < 9 else (g2, r * 16 - ROWS)
-            for l in range(3):
-                tiles[r * 3 + l] = src[row : row + 16, 128 * l : 128 * l + 128].astype(BF16)
-            ends.append(src[row : row + 16, 384:TAPS9])
-        ends.append(extra[16 * j : 16 * j + 16] if j < 3 else none)
-        tiles[54 + j] = jnp.concatenate(ends, axis=1).astype(BF16)
+    ends = []
+    for r in range(54):
+        src, row = (g1, r * 16) if r < 27 else (g2, r * 16 - TAPS9)
+        tiles[r] = src[row : row + 16, 0:128].astype(BF16)
+        ends.append(src[row : row + 16, 128:ROWS])
+    ends += [jnp.zeros((16, 16), F32)] * 2
+    for j in range(7):
+        tiles[54 + j] = jnp.concatenate(ends[8 * j : 8 * j + 8], axis=1).astype(BF16)
+    four = jnp.concatenate(columns, axis=1)
+    row = [four[16 * j : 16 * j + 16] for j in range(3)] + [jnp.zeros((16, 116), F32)]
+    tiles[61] = jnp.concatenate(row, axis=1).astype(BF16)
+    tiles[62] = jnp.zeros((16, 128), BF16)
     tiles[63] = jnp.zeros((16, 128), BF16)
 
 
 def spread_kernel(tiles, g1_ref, g2_ref, bias1_ref, bias2_ref):
-    for r in range(18):
-        out = g1_ref if r < 9 else g2_ref
-        s, row = (r % 9) // 3, (r % 3) * 16
-        parts = [tiles[r * 3 + l].astype(F32) for l in range(3)]
-        at = C * (r % 2)
-        parts.append(tiles[54 + r // 2].astype(F32)[:, at : at + C])
-        out[row : row + 16, s * TAPS9 : (s + 1) * TAPS9] = jnp.concatenate(parts, axis=1)
-    four = jnp.concatenate([tiles[54 + j].astype(F32)[:, 96:100] for j in range(3)], axis=0)
+    for r in range(54):
+        out = g1_ref if r < 27 else g2_ref
+        n, row = (r % 27) // 3, (r % 3) * 16
+        at = 16 * (r % 8)
+        end = tiles[54 + r // 8].astype(F32)[:, at : at + 16]
+        block = jnp.concatenate([tiles[r].astype(F32), end], axis=1)
+        out[row : row + 16, n * ROWS : (n + 1) * ROWS] = block
+    last = tiles[61].astype(F32)
+    four = jnp.concatenate([last[:, 4 * j : 4 * j + 4] for j in range(3)], axis=0)
     row = lax.broadcasted_iota(jnp.int32, (C, C), 0)
     col = lax.broadcasted_iota(jnp.int32, (C, C), 1)
     for out, j in ((bias1_ref, 0), (bias2_ref, 2)):
@@ -236,13 +259,15 @@
         out[...] = jnp.sum(jnp.where(row == col, both, 0.0), axis=0, keepdims=True)
 
 
-def out_kernel(count_ref, ph, lo_ref, hi_ref, w2_ref, b2_ref, out_ref, hh, w2s, acc):
+def out_kernel(count_ref, hid, lo_ref, hi_ref, w2_ref, b2_ref, out_ref, ph, hh, w2s, acc):
     count = count_ref[0, 0]
     masks = lane_masks()
     stack_taps(w2_ref, w2s)
     for i in range(2):
         put_shifts(split(lo_ref[i]), hh, i, masks)
         put_shifts(split(hi_ref[i]), hh, 2 + i, masks)
+    for p in range(SLOTS):
+        put_shifts(split(hid[p]), ph, p, masks)
     conv_local(acc, w2s, ph)
     conv_halo(acc, w2s, hh, count)
     for p in range(SLOTS):
@@ -302,14 +327,14 @@
         [(WEIGHT, BF16)], 16, 1_200_000_000, interpret,
     )
     halo = ((4, ROWS, WIDE), BF16)
-    ph, head, tail, tiles = call(
+    hid, head, tail, tiles = call(
         main_kernel, "grads",
         (plane_counts, px, pu, w2s, acc1, acc2, lo, hi, w_first, b_first[:, None]),
-        (SHIFTED, PAIR_BF16, PAIR_BF16, jax.ShapeDtypeStruct((TILES, 16, 128), BF16)),
+        (jax.ShapeDtypeStruct((SLOTS, C, CELLS), BF16), PAIR_BF16, PAIR_BF16, jax.ShapeDtypeStruct((TILES, 16, 128), BF16)),
         [
-            halo, halo, ((SLOTS + 4, C, CELLS), BF16), (WEIGHT, BF16),
-            ((SLOTS, C, CELLS), F32), ((SLOTS, C, CELLS), F32), ((SLOTS, C, CELLS), BF16),
-            (WEIGHT, F32), (WEIGHT, F32),
+            ((SLOTS, ROWS, WIDE), BF16), halo, halo, ((SLOTS + 4, C, WIDE), BF16), (WEIGHT, BF16),
+            ((SLOTS, C, CELLS), F32), ((SLOTS, C, CELLS), F32), ((SLOTS, C, WIDE), BF16),
+            ((TAPS9, ROWS), F32), ((TAPS9, ROWS), F32),
         ],
         32, 2_000_000_000, interpret,
     )
@@ -317,9 +342,9 @@
     hid_hi = lax.ppermute(head, "box", backward)
     tiles = gradient_sum(tiles)
     (decoded,) = call(
-        out_kernel, "decode", (plane_counts, ph, hid_lo, hid_hi, w_second, b_second[:, None]),
+        out_kernel, "decode", (plane_counts, hid, hid_lo, hid_hi, w_second, b_second[:, None]),
         (jax.ShapeDtypeStruct((1, SLOTS, C, CELLS), BF16),),
-        [halo, (WEIGHT, BF16), ((SLOTS, C, CELLS), F32)], 20, 1_000_000_000, interpret,
+        [((SLOTS, ROWS, WIDE), BF16), halo, (WEIGHT, BF16), ((SLOTS, C, CELLS), F32)], 24, 1_000_000_000, interpret,
     )
     grad = jax.ShapeDtypeStruct((C, 27 * C), F32)
     line = jax.ShapeDtypeStruct((1, C), F32)

time: 87.9 us -> 84.6 us (0.962)
  local copies, waits for them, and re-layouts: 5.03 us -> 2.26 us
    unnamed x16 -> x12, local copies, waits for them, and re-layouts: 2.79 us -> 0.02 us
where the time goes in v3:
time: 84.6 us; the launch traced here: 84.3 us
  starting transfers between devices  24.6 us (29%)
  waiting for transfers between devices  22.1 us (26%)
  blocking collectives  20.4 us (24%)
  Pallas kernels  13.1 us (15%)
  local copies, waits for them, and re-layouts  2.26 us (3%)
  between operations  1.52 us (2%)
    all_to_all x1, blocking collectives, gradient_sum(): mine = lax.all_to_all(tiles.reshape(parts, -1, 128), axes, 0, 0, tiled=True)  20.4 us
    pallas_call x4, Pallas kernels, call(): pl.pallas_call(kernel, out_shape=outs, in_specs=[SM if a.dtype == jnp.int...  13.1 us
    all_to_all x1, starting transfers between devices, gradient_sum(): lax.all_to_all(spread, axes, 0, 0, tiled=True).reshape(TILES, 16, 128)  10.8 us
    ppermute x1, waiting for transfers between devices, local(): lax.ppermute(jnp.concatenate([x[0:2], u[0:2]], axis=0), 'box', backward)  8.38 us
    ppermute x1, waiting for transfers between devices, local(): hid_hi = lax.ppermute(head, 'box', backward)  7.75 us
    ppermute x1, starting transfers between devices, local(): lax.ppermute(jnp.concatenate([last(x), last(u)], axis=0), 'box', forward)  4.96 us
    ppermute x1, starting transfers between devices, local(): hid_lo = lax.ppermute(tail, 'box', forward)  4.93 us
    ppermute x1, waiting for transfers between devices, local(): hid_lo = lax.ppermute(tail, 'box', forward)  3 us
  transfers between devices with their start and end apart: 5, of which 4 were waited for; matrix products, arithmetic and copies ran while one was open for 0% of the time, Pallas kernels for 7%

profile of v3, /device:TPU:126, one launch (start us, length us, event | category | flops | bytes accessed | tf_op | source)
XLA Modules:
  0.0 84.3 jit_solution(15673844981618994376)
XLA Ops:
  0.6 0.0 copy-start
  0.6 0.0 copy-start.1
  0.7 0.0 copy-start.4
  0.7 0.0 copy-start.2
  0.7 0.0 copy-start.3
  1.4 1.3 %slice_bitcast_fusion = (bf16[2,48,1024]{2,1,0:T(8,128)(2,1)S(1)}, bf16[2,48,1024]{2,1,0:T(8,128)(2,1)S(1)}, bf16[2,48,1024]{2,1,0:T(8,128)(2,1)S(1)}, bf16[2,48,1024]{2,1,0:T(8,128)(2,1)S(1)}) fusion(bf16[1,5,48,1024]{3,2,1,0:T(8,128)(2,1)} %param.8, s32[]{:T(128)S(6)} %select_n.4, bf16[1,5,48,1024]{3,2,1,0:T(8,128)(2,1)} %param.7), kind=kLoop, calls=%fused_computation.2 | loop fusion | bytes 1572868 | tf_op jit(solution)/shard_map/slice | solution.py:323
  2.8 5.0 %collective-permute-start = (bf16[4,48,1024]{2,1,0:T(8,128)(2,1)S(1)}, bf16[4,48,1024]{2,1,0:T(8,128)(2,1)S(1)}, u32[]{:S(2)}, u32[]{:S(2)}) collective-permute-start(bf16[4,48,1024]{2,1,0:T(8,128)(2,1)S(1)} %pad_maximum_fusion), channel_id=1, source_target_pairs={{0,4},{4,8},{8,12},{12,16},{16,20},{20,24},{24,28},{28,32},{32,36}... | collective-permute-start | bytes 1179656 | tf_op jit(solution)/shard_map/ppermute | solution.py:322
  7.8 1.9 %collective-permute-start.1 = (bf16[4,48,1024]{2,1,0:T(8,128)(2,1)S(1)}, bf16[4,48,1024]{2,1,0:T(8,128)(2,1)S(1)}, u32[]{:S(2)}, u32[]{:S(2)}) collective-permute-start(bf16[4,48,1024]{2,1,0:T(8,128)(2,1)S(1)} %pad_maximum_fusion.1), channel_id=1, source_target_pairs={{4,0},{8,4},{12,8},{16,12},{20,16},{24,20},{28,24},{32,28},{36,32}... | collective-permute-start | bytes 1179656 | tf_op jit(solution)/shard_map/ppermute | solution.py:323
  9.7 0.0 copy-done.4
  9.7 0.1 copy.12.b1_ref
  9.8 0.0 copy-done
  9.8 0.0 copy-done.1
  9.8 0.0 copy-done.2
  9.8 0.0 copy-done.3
  9.8 3.3 %front.1 = (bf16[5,144,1280]{2,1,0:T(8,128)(2,1)S(1)}, bf16[5,144,1280]{2,1,0:T(8,128)(2,1)S(1)}, bf16[144,432]{1,0:T(8,128)(2,1)S(1)}, f32[5,48,1024]{2,1,0:T(8,128)S(1)}, f32[5,48,1024]{2,1,0:T(8,128)S(1)}) custom-call(s32[1,1]{1,0:T(1,128)S(6)} %copy.14.count_ref, bf16[5,48,1024]{2,1,0:T(8,128)(2,1)S(1)} %bitcast.18, bf16[5,48,1024]{2,1,0:T(8,128)(2,1)S(1)} %bitcast.19, ...), custom_call_target="tpu_custom_call" | custom-call | flops 1200000000 | bytes 2000000 | tf_op jit(solution)/shard_map/front/pallas_call | solution.py:291
  13.1 2.9 %collective-permute-done.lo_ref = bf16[4,48,1024]{2,1,0:T(8,128)(2,1)S(1)} collective-permute-done((bf16[4,48,1024]{2,1,0:T(8,128)(2,1)S(1)}, bf16[4,48,1024]{2,1,0:T(8,128)(2,1)S(1)}, u32[]{:S(2)}, u32[]{:S(2)}) %collective-permute-start) | collective-permute-done | bytes 393248 | tf_op jit(solution)/shard_map/ppermute | solution.py:322
  16.1 8.4 %collective-permute-done.1.hi_ref = bf16[4,48,1024]{2,1,0:T(8,128)(2,1)S(1)} collective-permute-done((bf16[4,48,1024]{2,1,0:T(8,128)(2,1)S(1)}, bf16[4,48,1024]{2,1,0:T(8,128)(2,1)S(1)}, u32[]{:S(2)}, u32[]{:S(2)}) %collective-permute-start.1) | collective-permute-done | bytes 393248 | tf_op jit(solution)/shard_map/ppermute | solution.py:323
  24.5 0.0 copy-start.5
  24.5 5.3 %grads.1 = (bf16[5,48,1024]{2,1,0:T(8,128)(2,1)S(1)}, bf16[2,48,1024]{2,1,0:T(8,128)(2,1)S(1)}, bf16[2,48,1024]{2,1,0:T(8,128)(2,1)S(1)}, bf16[64,16,128]{2,1,0:T(8,128)(2,1)S(1)}) custom-call(s32[1,1]{1,0:T(1,128)S(6)} %copy.14.count_ref, bf16[5,144,1280]{2,1,0:T(8,128)(2,1)S(1)} %get-tuple-element.18.px, bf16[5,144,1280]{2,1,0:T(8,128)(2,1)S(1)} %get-tuple-element.19.pu, ...), custom_call_target="tpu_custom_call" | custom-call | flops 2000000000 | bytes 2000000 | tf_op jit(solution)/shard_map/grads/pallas_call | solution.py:291
  29.7 20.4 %all_to_all.10 = bf16[256,4,128]{2,1,0:T(4,128)(2,1)S(1)} all-to-all(bf16[256,4,128]{2,1,0:T(4,128)(2,1)S(1)} %bitcast.21), channel_id=1, replica_groups=mesh['box'=64,'snap'=4] {'box','snap'}, dimensions={0} | all-to-all | bytes 524288 | tf_op jit(solution)/shard_map/all_to_all | solution.py:307
  50.1 0.3 reduce_sum.12
  50.4 0.8 broadcast_in_dim.14
  51.2 10.8 %all-to-all-start.1 = ((bf16[256,4,128]{2,1,0:T(4,128)(2,1)}), bf16[256,4,128]{2,1,0:T(4,128)(2,1)S(1)}, u32[]{:S(2)}, u32[]{:S(2)}) async-start(bf16[256,4,128]{2,1,0:T(4,128)(2,1)} %broadcast_in_dim.14), calls=%async_computation.1 | async-start | bytes 524288 | tf_op jit(solution)/shard_map/all_to_all | solution.py:310
  62.1 4.9 %collective-permute-start.2 = (bf16[2,48,1024]{2,1,0:T(8,128)(2,1)S(1)}, bf16[2,48,1024]{2,1,0:T(8,128)(2,1)S(1)}, u32[]{:S(2)}, u32[]{:S(2)}) collective-permute-start(bf16[2,48,1024]{2,1,0:T(8,128)(2,1)S(1)} %get-tuple-element.24), channel_id=1, source_target_pairs={{0,4},{4,8},{8,12},{12,16},{16,20},{20,24},{24,28},{28,32},{32,36}... | collective-permute-start | bytes 589832 | tf_op jit(solution)/shard_map/ppermute | solution.py:341
  67.0 1.9 %collective-permute-start.3 = (bf16[2,48,1024]{2,1,0:T(8,128)(2,1)S(1)}, bf16[2,48,1024]{2,1,0:T(8,128)(2,1)S(1)}, u32[]{:S(2)}, u32[]{:S(2)}) collective-permute-start(bf16[2,48,1024]{2,1,0:T(8,128)(2,1)S(1)} %get-tuple-element.25), channel_id=1, source_target_pairs={{4,0},{8,4},{12,8},{16,12},{20,16},{24,20},{28,24},{32,28},{36,32}... | collective-permute-start | bytes 589832 | tf_op jit(solution)/shard_map/ppermute | solution.py:342
  68.9 0.0 copy-done.5
  68.9 0.1 copy.13.b2_ref
  69.0 3.0 %collective-permute-done.2.lo_ref = bf16[2,48,1024]{2,1,0:T(8,128)(2,1)S(1)} collective-permute-done((bf16[2,48,1024]{2,1,0:T(8,128)(2,1)S(1)}, bf16[2,48,1024]{2,1,0:T(8,128)(2,1)S(1)}, u32[]{:S(2)}, u32[]{:S(2)}) %collective-permute-start.2) | collective-permute-done | bytes 196640 | tf_op jit(solution)/shard_map/ppermute | solution.py:341
  72.0 7.8 %collective-permute-done.3.hi_ref = bf16[2,48,1024]{2,1,0:T(8,128)(2,1)S(1)} collective-permute-done((bf16[2,48,1024]{2,1,0:T(8,128)(2,1)S(1)}, bf16[2,48,1024]{2,1,0:T(8,128)(2,1)S(1)}, u32[]{:S(2)}, u32[]{:S(2)}) %collective-permute-start.3) | collective-permute-done | bytes 196640 | tf_op jit(solution)/shard_map/ppermute | solution.py:342
  79.8 2.6 %decode.1 = bf16[1,5,48,1024]{3,2,1,0:T(8,128)(2,1)} custom-call(s32[1,1]{1,0:T(1,128)S(6)} %copy.14.count_ref, bf16[5,48,1024]{2,1,0:T(8,128)(2,1)S(1)} %get-tuple-element.23.hid, bf16[2,48,1024]{2,1,0:T(8,128)(2,1)S(1)} %collective-permute-done.2.lo_ref, bf16[2,48,1024]{2,1,0:T(8,128)(2,1)S(1)} %collective-permute-done.3.hi_ref, ...), custom_call_target="tpu_custom_call" | custom-call | flops 1000000000 | bytes 2000000 | tf_op jit(solution)/shard_map/decode/pallas_call | solution.py:291
  82.4 0.0 all-to-all-done.1
  82.4 1.9 %spread.1 = (f32[48,1296]{1,0:T(8,128)}, f32[48,1296]{1,0:T(8,128)}, f32[1,48]{1,0:T(1,128)}, f32[1,48]{1,0:T(1,128)}) custom-call(bf16[64,16,128]{2,1,0:T(8,128)(2,1)S(1)} %bitcast.20), custom_call_target="tpu_custom_call" | custom-call | flops 100000000 | bytes 2000000 | tf_op jit(solution)/shard_map/spread/pallas_call | solution.py:291
  (2 shorter events, 0.1 us)
Async XLA Ops:
  0.6 9.2 %copy-start = (bf16[1,5,48,1024]{3,2,1,0:T(8,128)(2,1)S(1)}, bf16[1,5,48,1024]{3,2,1,0:T(8,128)(2,1)}, u32[]{:S(2)}) copy-start(bf16[1,5,48,1024]{3,2,1,0:T(8,128)(2,1)} %param.7) | copy-start | bytes 1474564
  0.6 9.2 %copy-start.1 = (bf16[1,5,48,1024]{3,2,1,0:T(8,128)(2,1)S(1)}, bf16[1,5,48,1024]{3,2,1,0:T(8,128)(2,1)}, u32[]{:S(2)}) copy-start(bf16[1,5,48,1024]{3,2,1,0:T(8,128)(2,1)} %param.8) | copy-start | bytes 1474564
  0.7 9.0 %copy-start.4 = (f32[48]{0:T(128)S(1)}, f32[48]{0:T(128)}, u32[]{:S(2)}) copy-start(f32[48]{0:T(128)} %param.11) | copy-start | bytes 580
  0.7 9.1 %copy-start.2 = (bf16[48,1296]{1,0:T(8,128)(2,1)S(1)}, bf16[48,1296]{1,0:T(8,128)(2,1)}, u32[]{:S(2)}) copy-start(bf16[48,1296]{1,0:T(8,128)(2,1)} %w1_ref.3) | copy-start | bytes 373252
  0.7 9.1 %copy-start.3 = (bf16[48,1296]{1,0:T(8,128)(2,1)S(1)}, bf16[48,1296]{1,0:T(8,128)(2,1)}, u32[]{:S(2)}) copy-start(bf16[48,1296]{1,0:T(8,128)(2,1)} %w2_ref.3) | copy-start | bytes 373252
  2.8 13.3 %collective-permute-start = (bf16[4,48,1024]{2,1,0:T(8,128)(2,1)S(1)}, bf16[4,48,1024]{2,1,0:T(8,128)(2,1)S(1)}, u32[]{:S(2)}, u32[]{:S(2)}) collective-permute-start(bf16[4,48,1024]{2,1,0:T(8,128)(2,1)S(1)} %pad_maximum_fusion), channel_id=1, source_target_pairs={{0,4},{4,8},{8,12},{12,16},{16,20},{20,24},{24,28},{28,32},{32,36}... | collective-permute-start | bytes 1179656 | tf_op jit(solution)/shard_map/ppermute | solution.py:322
  7.8 16.7 %collective-permute-start.1 = (bf16[4,48,1024]{2,1,0:T(8,128)(2,1)S(1)}, bf16[4,48,1024]{2,1,0:T(8,128)(2,1)S(1)}, u32[]{:S(2)}, u32[]{:S(2)}) collective-permute-start(bf16[4,48,1024]{2,1,0:T(8,128)(2,1)S(1)} %pad_maximum_fusion.1), channel_id=1, source_target_pairs={{4,0},{8,4},{12,8},{16,12},{20,16},{24,20},{28,24},{32,28},{36,32}... | collective-permute-start | bytes 1179656 | tf_op jit(solution)/shard_map/ppermute | solution.py:323
  24.5 44.5 %copy-start.5 = (f32[48]{0:T(128)S(1)}, f32[48]{0:T(128)}, u32[]{:S(2)}) copy-start(f32[48]{0:T(128)} %param.13) | copy-start | bytes 580
  51.2 31.2 %all-to-all-start.1 = ((bf16[256,4,128]{2,1,0:T(4,128)(2,1)}), bf16[256,4,128]{2,1,0:T(4,128)(2,1)S(1)}, u32[]{:S(2)}, u32[]{:S(2)}) async-start(bf16[256,4,128]{2,1,0:T(4,128)(2,1)} %broadcast_in_dim.14), calls=%async_computation.1 | async-start | bytes 524288 | tf_op jit(solution)/shard_map/all_to_all | solution.py:310
  62.1 10.0 %collective-permute-start.2 = (bf16[2,48,1024]{2,1,0:T(8,128)(2,1)S(1)}, bf16[2,48,1024]{2,1,0:T(8,128)(2,1)S(1)}, u32[]{:S(2)}, u32[]{:S(2)}) collective-permute-start(bf16[2,48,1024]{2,1,0:T(8,128)(2,1)S(1)} %get-tuple-element.24), channel_id=1, source_target_pairs={{0,4},{4,8},{8,12},{12,16},{16,20},{20,24},{24,28},{28,32},{32,36}... | collective-permute-start | bytes 589832 | tf_op jit(solution)/shard_map/ppermute | solution.py:341
  67.0 12.8 %collective-permute-start.3 = (bf16[2,48,1024]{2,1,0:T(8,128)(2,1)S(1)}, bf16[2,48,1024]{2,1,0:T(8,128)(2,1)S(1)}, u32[]{:S(2)}, u32[]{:S(2)}) collective-permute-start(bf16[2,48,1024]{2,1,0:T(8,128)(2,1)S(1)} %get-tuple-element.25), channel_id=1, source_target_pairs={{4,0},{8,4},{12,8},{16,12},{20,16},{24,20},{28,24},{32,28},{36,32}... | collective-permute-start | bytes 589832 | tf_op jit(solution)/shard_map/ppermute | solution.py:342

commit v4 on v3

--- a/solution.py
+++ b/solution.py
@@ -101,15 +101,12 @@
                     seen.add((p, start))
 
 
-def conv_halo(acc, w, src, count):
+def conv_halo(acc, w, src, first):
     for i in range(2):
         for start in range(0, CELLS, CHUNK):
             cols = slice(start, start + CHUNK)
-            below = taps(src, i, start, CHUNK)
-            acc[i, :, cols] += jnp.dot(w[0:C, :], below, preferred_element_type=F32)
-            above = taps(src, 2 + i, start, CHUNK)
-            y = jnp.dot(w[2 * C : 3 * C, :], above, preferred_element_type=F32)
-            acc[count - 2 + i, :, cols] += y
+            y = jnp.dot(w, taps(src, i, start, CHUNK), preferred_element_type=F32)
+            acc[first + i, :, cols] += y
 
 
 def lane_dot(a, b):
@@ -141,7 +138,7 @@
         dst[s * C : (s + 1) * C, :] = w_ref[:, s * TAPS9 : (s + 1) * TAPS9]
 
 
-def front_kernel(count_ref, x_ref, u_ref, w1_ref, w2_ref, px, pu, w2s, acc1, acc2, w1s):
+def front_kernel(count_ref, x_ref, u_ref, w1_ref, w2_ref, px, pu, w1s, w2s, acc1, acc2):
     count = count_ref[0, 0]
     masks = lane_masks()
     stack_taps(w1_ref, w1s)
@@ -159,29 +156,40 @@
     conv_local(acc2, w2s, pu)
 
 
+def low_kernel(w1s, w2s, acc1, acc2, lo_ref, lx, lu, sum1, sum2):
+    masks = lane_masks()
+    for i in range(2):
+        put_shifts(to_halves(lo_ref[i], masks), lx, i, masks)
+        put_shifts(to_halves(lo_ref[2 + i], masks), lu, i, masks)
+    for i in range(2):
+        sum1[i] = acc1[i]
+        sum2[i] = acc2[i]
+    conv_halo(sum1, w1s[0:C, :], lx, 0)
+    conv_halo(sum2, w2s[0:C, :], lu, 0)
+
+
 def main_kernel(
-    count_ref, px, pu, w2s, acc1, acc2, lo_ref, hi_ref, w1_ref, b1_ref,
+    count_ref, px, pu, w1s, w2s, acc1, acc2, two1, two2, lx, lu, hi_ref, b1_ref,
     hid, head_ref, tail_ref, tiles,
-    ph, hx, hu, ue, w1s, more1, more2, pre, g1, g2,
+    more1, more2, ph, hx, hu, ue, pre, g1, g2,
 ):
     count = count_ref[0, 0]
     masks = lane_masks()
-    stack_taps(w1_ref, w1s)
-    for i in range(2):
-        for src, at in ((lo_ref, i), (hi_ref, 2 + i)):
-            put_shifts(to_halves(src[i], masks), hx, at, masks)
-            put_shifts(to_halves(src[2 + i], masks), hu, at, masks)
-    for p in range(SLOTS):
-        more1[p] = acc1[p]
-        more2[p] = acc2[p]
+    for i in range(2):
+        put_shifts(to_halves(hi_ref[i], masks), hx, i, masks)
+        put_shifts(to_halves(hi_ref[2 + i], masks), hu, i, masks)
+    for p in range(SLOTS):
         ue[p + 2] = pu[p, C : 2 * C, :]
     ue[SLOTS + 2] = jnp.zeros((C, WIDE), BF16)
     ue[SLOTS + 3] = jnp.zeros((C, WIDE), BF16)
     for i in range(2):
-        ue[i] = hu[i, C : 2 * C, :]
-        ue[count + 2 + i] = hu[2 + i, C : 2 * C, :]
-    conv_halo(more1, w1s, hx, count)
-    conv_halo(more2, w2s, hu, count)
+        ue[i] = lu[i, C : 2 * C, :]
+        ue[count + 2 + i] = hu[i, C : 2 * C, :]
+    for p in range(SLOTS):
+        more1[p] = two1[p] if p < 2 else acc1[p]
+        more2[p] = two2[p] if p < 2 else acc2[p]
+    conv_halo(more1, w1s[2 * C : 3 * C, :], hx, count - 2)
+    conv_halo(more2, w2s[2 * C : 3 * C, :], hu, count - 2)
     bias1 = jnp.zeros((C, 128), F32)
     bias2 = jnp.zeros((C, 128), F32)
     for p in range(SLOTS):
@@ -219,8 +227,8 @@
         y = lane_dot(rows_of(pre, [p for p, _ in pairs]), center(px, q))
         g1[lo * ROWS : hi * ROWS, :] += y
     for i in range(2):
-        g1[0:ROWS, :] += lane_dot(rows_of(pre, [i]), center(hx, i))
-        y = lane_dot(rows_of(pre, [count - 2 + i]), center(hx, 2 + i))
+        g1[0:ROWS, :] += lane_dot(rows_of(pre, [i]), center(lx, i))
+        y = lane_dot(rows_of(pre, [count - 2 + i]), center(hx, i))
         g1[2 * ROWS : TAPS9, :] += y
     columns = []
     for bias in (bias1, bias2):
@@ -231,10 +239,10 @@
     for r in range(54):
         src, row = (g1, r * 16) if r < 27 else (g2, r * 16 - TAPS9)
         tiles[r] = src[row : row + 16, 0:128].astype(BF16)
-        ends.append(src[row : row + 16, 128:ROWS])
-    ends += [jnp.zeros((16, 16), F32)] * 2
+        ends.append(src[row : row + 16, 128:ROWS].astype(BF16))
+    ends += [jnp.zeros((16, 16), BF16)] * 2
     for j in range(7):
-        tiles[54 + j] = jnp.concatenate(ends[8 * j : 8 * j + 8], axis=1).astype(BF16)
+        tiles[54 + j] = jnp.concatenate(ends[8 * j : 8 * j + 8], axis=1)
     four = jnp.concatenate(columns, axis=1)
     row = [four[16 * j : 16 * j + 16] for j in range(3)] + [jnp.zeros((16, 116), F32)]
     tiles[61] = jnp.concatenate(row, axis=1).astype(BF16)
@@ -243,13 +251,14 @@
 
 
 def spread_kernel(tiles, g1_ref, g2_ref, bias1_ref, bias2_ref):
-    for r in range(54):
-        out = g1_ref if r < 27 else g2_ref
-        n, row = (r % 27) // 3, (r % 3) * 16
-        at = 16 * (r % 8)
-        end = tiles[54 + r // 8].astype(F32)[:, at : at + 16]
-        block = jnp.concatenate([tiles[r].astype(F32), end], axis=1)
-        out[row : row + 16, n * ROWS : (n + 1) * ROWS] = block
+    for r in range(6):
+        pieces = []
+        for n in range(9):
+            t = (r // 3) * 27 + n * 3 + r % 3
+            pieces += [tiles[t], tiles[54 + t // 8, :, 16 * (t % 8) : 16 * (t % 8) + 16]]
+        out = g1_ref if r < 3 else g2_ref
+        row = (r % 3) * 16
+        out[row : row + 16, :] = jnp.concatenate(pieces, axis=1).astype(F32)
     last = tiles[61].astype(F32)
     four = jnp.concatenate([last[:, 4 * j : 4 * j + 4] for j in range(3)], axis=0)
     row = lax.broadcasted_iota(jnp.int32, (C, C), 0)
@@ -259,17 +268,18 @@
         out[...] = jnp.sum(jnp.where(row == col, both, 0.0), axis=0, keepdims=True)
 
 
-def out_kernel(count_ref, hid, lo_ref, hi_ref, w2_ref, b2_ref, out_ref, ph, hh, w2s, acc):
+def out_kernel(count_ref, hid, lo_ref, hi_ref, w2_ref, b2_ref, out_ref, ph, lh, hh, w2s, acc):
     count = count_ref[0, 0]
     masks = lane_masks()
     stack_taps(w2_ref, w2s)
     for i in range(2):
-        put_shifts(split(lo_ref[i]), hh, i, masks)
-        put_shifts(split(hi_ref[i]), hh, 2 + i, masks)
+        put_shifts(split(lo_ref[i]), lh, i, masks)
+        put_shifts(split(hi_ref[i]), hh, i, masks)
     for p in range(SLOTS):
         put_shifts(split(hid[p]), ph, p, masks)
     conv_local(acc, w2s, ph)
-    conv_halo(acc, w2s, hh, count)
+    conv_halo(acc, w2s[0:C, :], lh, 0)
+    conv_halo(acc, w2s[2 * C : 3 * C, :], hh, count - 2)
     for p in range(SLOTS):
         keep = jnp.where(p < count, 1.0, 0.0).astype(F32)
         z = ((acc[p] + b2_ref[...]) * keep).astype(BF16)
@@ -321,19 +331,25 @@
     last = lambda v: lax.dynamic_slice(v, (count - 2, zero, zero), (2, C, CELLS))
     lo = lax.ppermute(jnp.concatenate([last(x), last(u)], axis=0), "box", forward)
     hi = lax.ppermute(jnp.concatenate([x[0:2], u[0:2]], axis=0), "box", backward)
-    px, pu, w2s, acc1, acc2 = call(
+    stacked = jax.ShapeDtypeStruct(WEIGHT, BF16)
+    px, pu, w1s, w2s, acc1, acc2 = call(
         front_kernel, "front", (plane_counts, x, u, w_first, w_second),
-        (SHIFTED, SHIFTED, jax.ShapeDtypeStruct(WEIGHT, BF16), SUMS, SUMS),
-        [(WEIGHT, BF16)], 16, 1_200_000_000, interpret,
-    )
-    halo = ((4, ROWS, WIDE), BF16)
+        (SHIFTED, SHIFTED, stacked, stacked, SUMS, SUMS), [], 16, 1_200_000_000, interpret,
+    )
+    halo = ((2, ROWS, WIDE), BF16)
+    low_shape = jax.ShapeDtypeStruct((2, ROWS, WIDE), BF16)
+    two = jax.ShapeDtypeStruct((2, C, CELLS), F32)
+    lx, lu, two1, two2 = call(
+        low_kernel, "low", (w1s, w2s, acc1, acc2, lo),
+        (low_shape, low_shape, two, two), [], 16, 300_000_000, interpret,
+    )
     hid, head, tail, tiles = call(
         main_kernel, "grads",
-        (plane_counts, px, pu, w2s, acc1, acc2, lo, hi, w_first, b_first[:, None]),
+        (plane_counts, px, pu, w1s, w2s, acc1, acc2, two1, two2, lx, lu, hi, b_first[:, None]),
         (jax.ShapeDtypeStruct((SLOTS, C, CELLS), BF16), PAIR_BF16, PAIR_BF16, jax.ShapeDtypeStruct((TILES, 16, 128), BF16)),
         [
-            ((SLOTS, ROWS, WIDE), BF16), halo, halo, ((SLOTS + 4, C, WIDE), BF16), (WEIGHT, BF16),
-            ((SLOTS, C, CELLS), F32), ((SLOTS, C, CELLS), F32), ((SLOTS, C, WIDE), BF16),
+            ((SLOTS, C, CELLS), F32), ((SLOTS, C, CELLS), F32), ((SLOTS, ROWS, WIDE), BF16),
+            halo, halo, ((SLOTS + 4, C, WIDE), BF16), ((SLOTS, C, WIDE), BF16),
             ((TAPS9, ROWS), F32), ((TAPS9, ROWS), F32),
         ],
         32, 2_000_000_000, interpret,
@@ -344,7 +360,7 @@
     (decoded,) = call(
         out_kernel, "decode", (plane_counts, hid, hid_lo, hid_hi, w_second, b_second[:, None]),
         (jax.ShapeDtypeStruct((1, SLOTS, C, CELLS), BF16),),
-        [((SLOTS, ROWS, WIDE), BF16), halo, (WEIGHT, BF16), ((SLOTS, C, CELLS), F32)], 24, 1_000_000_000, interpret,
+        [((SLOTS, ROWS, WIDE), BF16), halo, halo, (WEIGHT, BF16), ((SLOTS, C, CELLS), F32)], 24, 1_000_000_000, interpret,
     )
     grad = jax.ShapeDtypeStruct((C, 27 * C), F32)
     line = jax.ShapeDtypeStruct((1, C), F32)

time: 84.6 us -> 82.7 us (0.978)
  waiting for transfers between devices: 22.1 us -> 20.8 us
    ppermute x1, waiting for transfers between devices: 8.38 us -> 7.06 us  [local(): lax.ppermute(jnp.concatenate([x[0:2], u[0:2]], axis=0), 'box', backward)]
    pallas_call x4 -> x5, Pallas kernels: 13.1 us -> 12.6 us  [call(): pl.pallas_call(kernel, out_shape=outs, in_specs=[SM if a.dtype == jnp.int...]
  transfers between devices with their start and end apart: 5 -> 5, of which waited for: 4 -> 4; matrix products, arithmetic and copies ran while one was open for 0% -> 0% of each run, Pallas kernels for 7% -> 9%
where the time goes in v4:
time: 82.7 us; the launch traced here: 82.5 us
  starting transfers between devices  24.6 us (30%)
  waiting for transfers between devices  20.8 us (25%)
  blocking collectives  20.4 us (25%)
  Pallas kernels  12.6 us (15%)
  local copies, waits for them, and re-layouts  2.26 us (3%)
  between operations  1.52 us (2%)
    all_to_all x1, blocking collectives, gradient_sum(): mine = lax.all_to_all(tiles.reshape(parts, -1, 128), axes, 0, 0, tiled=True)  20.4 us
    pallas_call x5, Pallas kernels, call(): pl.pallas_call(kernel, out_shape=outs, in_specs=[SM if a.dtype == jnp.int...  12.6 us
    all_to_all x1, starting transfers between devices, gradient_sum(): lax.all_to_all(spread, axes, 0, 0, tiled=True).reshape(TILES, 16, 128)  10.8 us
    ppermute x1, waiting for transfers between devices, local(): hid_hi = lax.ppermute(head, 'box', backward)  7.75 us
    ppermute x1, waiting for transfers between devices, local(): lax.ppermute(jnp.concatenate([x[0:2], u[0:2]], axis=0), 'box', backward)  7.06 us
    ppermute x1, starting transfers between devices, local(): lax.ppermute(jnp.concatenate([last(x), last(u)], axis=0), 'box', forward)  4.96 us
    ppermute x1, starting transfers between devices, local(): hid_lo = lax.ppermute(tail, 'box', forward)  4.93 us
    ppermute x1, waiting for transfers between devices, local(): hid_lo = lax.ppermute(tail, 'box', forward)  3 us
  transfers between devices with their start and end apart: 5, of which 4 were waited for; matrix products, arithmetic and copies ran while one was open for 0% of the time, Pallas kernels for 9%

profile of v4, /device:TPU:126, one launch (start us, length us, event | category | flops | bytes accessed | tf_op | source)
XLA Modules:
  0.0 82.5 jit_solution(15248875482266474028)
XLA Ops:
  0.6 0.0 copy-start
  0.6 0.0 copy-start.1
  0.7 0.0 copy-start.4
  0.7 0.0 copy-start.2
  0.7 0.0 copy-start.3
  1.4 1.3 %slice_bitcast_fusion = (bf16[2,48,1024]{2,1,0:T(8,128)(2,1)S(1)}, bf16[2,48,1024]{2,1,0:T(8,128)(2,1)S(1)}, bf16[2,48,1024]{2,1,0:T(8,128)(2,1)S(1)}, bf16[2,48,1024]{2,1,0:T(8,128)(2,1)S(1)}) fusion(bf16[1,5,48,1024]{3,2,1,0:T(8,128)(2,1)} %param.8, s32[]{:T(128)S(6)} %select_n.4, bf16[1,5,48,1024]{3,2,1,0:T(8,128)(2,1)} %param.7), kind=kLoop, calls=%fused_computation.2 | loop fusion | bytes 1572868 | tf_op jit(solution)/shard_map/slice | solution.py:333
  2.8 5.0 %collective-permute-start = (bf16[4,48,1024]{2,1,0:T(8,128)(2,1)S(1)}, bf16[4,48,1024]{2,1,0:T(8,128)(2,1)S(1)}, u32[]{:S(2)}, u32[]{:S(2)}) collective-permute-start(bf16[4,48,1024]{2,1,0:T(8,128)(2,1)S(1)} %pad_maximum_fusion), channel_id=1, source_target_pairs={{0,4},{4,8},{8,12},{12,16},{16,20},{20,24},{24,28},{28,32},{32,36}... | collective-permute-start | bytes 1179656 | tf_op jit(solution)/shard_map/ppermute | solution.py:332
  7.8 1.9 %collective-permute-start.1 = (bf16[4,48,1024]{2,1,0:T(8,128)(2,1)S(1)}, bf16[4,48,1024]{2,1,0:T(8,128)(2,1)S(1)}, u32[]{:S(2)}, u32[]{:S(2)}) collective-permute-start(bf16[4,48,1024]{2,1,0:T(8,128)(2,1)S(1)} %pad_maximum_fusion.1), channel_id=1, source_target_pairs={{4,0},{8,4},{12,8},{16,12},{20,16},{24,20},{28,24},{32,28},{36,32}... | collective-permute-start | bytes 1179656 | tf_op jit(solution)/shard_map/ppermute | solution.py:333
  9.7 0.0 copy-done.4
  9.7 0.1 copy.12.b1_ref
  9.8 0.0 copy-done
  9.8 0.0 copy-done.1
  9.8 0.0 copy-done.2
  9.8 0.0 copy-done.3
  9.8 3.3 %front.1 = (bf16[5,144,1280]{2,1,0:T(8,128)(2,1)S(1)}, bf16[5,144,1280]{2,1,0:T(8,128)(2,1)S(1)}, bf16[144,432]{1,0:T(8,128)(2,1)S(1)}, bf16[144,432]{1,0:T(8,12...) custom-call(s32[1,1]{1,0:T(1,128)S(6)} %copy.14.count_ref, bf16[5,48,1024]{2,1,0:T(8,128)(2,1)S(1)} %bitcast.18, ...), custom_call_target="tpu_custom_call" | custom-call | flops 1200000000 | bytes 2000000 | tf_op jit(solution)/shard_map/front/pallas_call | solution.py:301
  13.1 2.9 %collective-permute-done.lo_ref = bf16[4,48,1024]{2,1,0:T(8,128)(2,1)S(1)} collective-permute-done((bf16[4,48,1024]{2,1,0:T(8,128)(2,1)S(1)}, bf16[4,48,1024]{2,1,0:T(8,128)(2,1)S(1)}, u32[]{:S(2)}, u32[]{:S(2)}) %collective-permute-start) | collective-permute-done | bytes 393248 | tf_op jit(solution)/shard_map/ppermute | solution.py:332
  16.1 1.3 %low.1 = (bf16[2,144,1280]{2,1,0:T(8,128)(2,1)S(1)}, bf16[2,144,1280]{2,1,0:T(8,128)(2,1)S(1)}, f32[2,48,1024]{2,1,0:T(8,128)S(1)}, f32[2,48,1024]{2,1,0:T(8,128)S(1)}) custom-call(bf16[144,432]{1,0:T(8,128)(2,1)S(1)} %get-tuple-element.25.w1s, bf16[144,432]{1,0:T(8,128)(2,1)S(1)} %get-tuple-element.26.w2s, f32[5,48,1024]{2,1,0:T(8,128)S(1)} %get-tuple-element.27.acc1, ...), custom_call_target="tpu_custom_call" | custom-call | flops 300000000 | bytes 2000000 | tf_op jit(solution)/shard_map/low/pallas_call | solution.py:301
  17.4 7.1 %collective-permute-done.1.hi_ref = bf16[4,48,1024]{2,1,0:T(8,128)(2,1)S(1)} collective-permute-done((bf16[4,48,1024]{2,1,0:T(8,128)(2,1)S(1)}, bf16[4,48,1024]{2,1,0:T(8,128)(2,1)S(1)}, u32[]{:S(2)}, u32[]{:S(2)}) %collective-permute-start.1) | collective-permute-done | bytes 393248 | tf_op jit(solution)/shard_map/ppermute | solution.py:333
  24.5 0.0 copy-start.5
  24.5 4.3 %grads.1 = (bf16[5,48,1024]{2,1,0:T(8,128)(2,1)S(1)}, bf16[2,48,1024]{2,1,0:T(8,128)(2,1)S(1)}, bf16[2,48,1024]{2,1,0:T(8,128)(2,1)S(1)}, bf16[64,16,128]{2,1,0:T(8,128)(2,1)S(1)}) custom-call(s32[1,1]{1,0:T(1,128)S(6)} %copy.14.count_ref, bf16[5,144,1280]{2,1,0:T(8,128)(2,1)S(1)} %get-tuple-element.23.px, bf16[5,144,1280]{2,1,0:T(8,128)(2,1)S(1)} %get-tuple-element.24.pu, ...), custom_call_target="tpu_custom_call" | custom-call | flops 2000000000 | bytes 2000000 | tf_op jit(solution)/shard_map/grads/pallas_call | solution.py:301
  28.7 20.4 %all_to_all.10 = bf16[256,4,128]{2,1,0:T(4,128)(2,1)S(1)} all-to-all(bf16[256,4,128]{2,1,0:T(4,128)(2,1)S(1)} %bitcast.21), channel_id=1, replica_groups=mesh['box'=64,'snap'=4] {'box','snap'}, dimensions={0} | all-to-all | bytes 524288 | tf_op jit(solution)/shard_map/all_to_all | solution.py:317
  49.1 0.3 reduce_sum.12
  49.4 0.8 broadcast_in_dim.14
  50.2 10.8 %all-to-all-start.1 = ((bf16[256,4,128]{2,1,0:T(4,128)(2,1)}), bf16[256,4,128]{2,1,0:T(4,128)(2,1)S(1)}, u32[]{:S(2)}, u32[]{:S(2)}) async-start(bf16[256,4,128]{2,1,0:T(4,128)(2,1)} %broadcast_in_dim.14), calls=%async_computation.1 | async-start | bytes 524288 | tf_op jit(solution)/shard_map/all_to_all | solution.py:320
  61.1 4.9 %collective-permute-start.2 = (bf16[2,48,1024]{2,1,0:T(8,128)(2,1)S(1)}, bf16[2,48,1024]{2,1,0:T(8,128)(2,1)S(1)}, u32[]{:S(2)}, u32[]{:S(2)}) collective-permute-start(bf16[2,48,1024]{2,1,0:T(8,128)(2,1)S(1)} %get-tuple-element.34), channel_id=1, source_target_pairs={{0,4},{4,8},{8,12},{12,16},{16,20},{20,24},{24,28},{28,32},{32,36}... | collective-permute-start | bytes 589832 | tf_op jit(solution)/shard_map/ppermute | solution.py:357
  66.0 1.9 %collective-permute-start.3 = (bf16[2,48,1024]{2,1,0:T(8,128)(2,1)S(1)}, bf16[2,48,1024]{2,1,0:T(8,128)(2,1)S(1)}, u32[]{:S(2)}, u32[]{:S(2)}) collective-permute-start(bf16[2,48,1024]{2,1,0:T(8,128)(2,1)S(1)} %get-tuple-element.35), channel_id=1, source_target_pairs={{4,0},{8,4},{12,8},{16,12},{20,16},{24,20},{28,24},{32,28},{36,32}... | collective-permute-start | bytes 589832 | tf_op jit(solution)/shard_map/ppermute | solution.py:358
  67.9 0.0 copy-done.5
  67.9 0.1 copy.13.b2_ref
  68.0 3.0 %collective-permute-done.2.lo_ref = bf16[2,48,1024]{2,1,0:T(8,128)(2,1)S(1)} collective-permute-done((bf16[2,48,1024]{2,1,0:T(8,128)(2,1)S(1)}, bf16[2,48,1024]{2,1,0:T(8,128)(2,1)S(1)}, u32[]{:S(2)}, u32[]{:S(2)}) %collective-permute-start.2) | collective-permute-done | bytes 196640 | tf_op jit(solution)/shard_map/ppermute | solution.py:357
  71.0 7.8 %collective-permute-done.3.hi_ref = bf16[2,48,1024]{2,1,0:T(8,128)(2,1)S(1)} collective-permute-done((bf16[2,48,1024]{2,1,0:T(8,128)(2,1)S(1)}, bf16[2,48,1024]{2,1,0:T(8,128)(2,1)S(1)}, u32[]{:S(2)}, u32[]{:S(2)}) %collective-permute-start.3) | collective-permute-done | bytes 196640 | tf_op jit(solution)/shard_map/ppermute | solution.py:358
  78.8 2.7 %decode.1 = bf16[1,5,48,1024]{3,2,1,0:T(8,128)(2,1)} custom-call(s32[1,1]{1,0:T(1,128)S(6)} %copy.14.count_ref, bf16[5,48,1024]{2,1,0:T(8,128)(2,1)S(1)} %get-tuple-element.33.hid, bf16[2,48,1024]{2,1,0:T(8,128)(2,1)S(1)} %collective-permute-done.2.lo_ref, bf16[2,48,1024]{2,1,0:T(8,128)(2,1)S(1)} %collective-permute-done.3.hi_ref, ...), custom_call_target="tpu_custom_call" | custom-call | flops 1000000000 | bytes 2000000 | tf_op jit(solution)/shard_map/decode/pallas_call | solution.py:301
  81.5 0.0 all-to-all-done.1
  81.5 1.0 %spread.1 = (f32[48,1296]{1,0:T(8,128)}, f32[48,1296]{1,0:T(8,128)}, f32[1,48]{1,0:T(1,128)}, f32[1,48]{1,0:T(1,128)}) custom-call(bf16[64,16,128]{2,1,0:T(8,128)(2,1)S(1)} %bitcast.20), custom_call_target="tpu_custom_call" | custom-call | flops 100000000 | bytes 2000000 | tf_op jit(solution)/shard_map/spread/pallas_call | solution.py:301
  (2 shorter events, 0.1 us)
Async XLA Ops:
  0.6 9.2 %copy-start = (bf16[1,5,48,1024]{3,2,1,0:T(8,128)(2,1)S(1)}, bf16[1,5,48,1024]{3,2,1,0:T(8,128)(2,1)}, u32[]{:S(2)}) copy-start(bf16[1,5,48,1024]{3,2,1,0:T(8,128)(2,1)} %param.7) | copy-start | bytes 1474564
  0.6 9.2 %copy-start.1 = (bf16[1,5,48,1024]{3,2,1,0:T(8,128)(2,1)S(1)}, bf16[1,5,48,1024]{3,2,1,0:T(8,128)(2,1)}, u32[]{:S(2)}) copy-start(bf16[1,5,48,1024]{3,2,1,0:T(8,128)(2,1)} %param.8) | copy-start | bytes 1474564
  0.7 9.0 %copy-start.4 = (f32[48]{0:T(128)S(1)}, f32[48]{0:T(128)}, u32[]{:S(2)}) copy-start(f32[48]{0:T(128)} %param.11) | copy-start | bytes 580
  0.7 9.1 %copy-start.2 = (bf16[48,1296]{1,0:T(8,128)(2,1)S(1)}, bf16[48,1296]{1,0:T(8,128)(2,1)}, u32[]{:S(2)}) copy-start(bf16[48,1296]{1,0:T(8,128)(2,1)} %w1_ref.1) | copy-start | bytes 373252
  0.7 9.1 %copy-start.3 = (bf16[48,1296]{1,0:T(8,128)(2,1)S(1)}, bf16[48,1296]{1,0:T(8,128)(2,1)}, u32[]{:S(2)}) copy-start(bf16[48,1296]{1,0:T(8,128)(2,1)} %w2_ref.3) | copy-start | bytes 373252
  2.8 13.3 %collective-permute-start = (bf16[4,48,1024]{2,1,0:T(8,128)(2,1)S(1)}, bf16[4,48,1024]{2,1,0:T(8,128)(2,1)S(1)}, u32[]{:S(2)}, u32[]{:S(2)}) collective-permute-start(bf16[4,48,1024]{2,1,0:T(8,128)(2,1)S(1)} %pad_maximum_fusion), channel_id=1, source_target_pairs={{0,4},{4,8},{8,12},{12,16},{16,20},{20,24},{24,28},{28,32},{32,36}... | collective-permute-start | bytes 1179656 | tf_op jit(solution)/shard_map/ppermute | solution.py:332
  7.8 16.7 %collective-permute-start.1 = (bf16[4,48,1024]{2,1,0:T(8,128)(2,1)S(1)}, bf16[4,48,1024]{2,1,0:T(8,128)(2,1)S(1)}, u32[]{:S(2)}, u32[]{:S(2)}) collective-permute-start(bf16[4,48,1024]{2,1,0:T(8,128)(2,1)S(1)} %pad_maximum_fusion.1), channel_id=1, source_target_pairs={{4,0},{8,4},{12,8},{16,12},{20,16},{24,20},{28,24},{32,28},{36,32}... | collective-permute-start | bytes 1179656 | tf_op jit(solution)/shard_map/ppermute | solution.py:333
  24.5 43.5 %copy-start.5 = (f32[48]{0:T(128)S(1)}, f32[48]{0:T(128)}, u32[]{:S(2)}) copy-start(f32[48]{0:T(128)} %param.13) | copy-start | bytes 580
  50.2 31.3 %all-to-all-start.1 = ((bf16[256,4,128]{2,1,0:T(4,128)(2,1)}), bf16[256,4,128]{2,1,0:T(4,128)(2,1)S(1)}, u32[]{:S(2)}, u32[]{:S(2)}) async-start(bf16[256,4,128]{2,1,0:T(4,128)(2,1)} %broadcast_in_dim.14), calls=%async_computation.1 | async-start | bytes 524288 | tf_op jit(solution)/shard_map/all_to_all | solution.py:320
  61.1 10.0 %collective-permute-start.2 = (bf16[2,48,1024]{2,1,0:T(8,128)(2,1)S(1)}, bf16[2,48,1024]{2,1,0:T(8,128)(2,1)S(1)}, u32[]{:S(2)}, u32[]{:S(2)}) collective-permute-start(bf16[2,48,1024]{2,1,0:T(8,128)(2,1)S(1)} %get-tuple-element.34), channel_id=1, source_target_pairs={{0,4},{4,8},{8,12},{12,16},{16,20},{20,24},{24,28},{28,32},{32,36}... | collective-permute-start | bytes 589832 | tf_op jit(solution)/shard_map/ppermute | solution.py:357
  66.0 12.8 %collective-permute-start.3 = (bf16[2,48,1024]{2,1,0:T(8,128)(2,1)S(1)}, bf16[2,48,1024]{2,1,0:T(8,128)(2,1)S(1)}, u32[]{:S(2)}, u32[]{:S(2)}) collective-permute-start(bf16[2,48,1024]{2,1,0:T(8,128)(2,1)S(1)} %get-tuple-element.35), channel_id=1, source_target_pairs={{4,0},{8,4},{12,8},{16,12},{20,16},{24,20},{28,24},{32,28},{36,32}... | collective-permute-start | bytes 589832 | tf_op jit(solution)/shard_map/ppermute | solution.py:358

commit v5 on v4

--- a/solution.py
+++ b/solution.py
@@ -250,6 +250,19 @@
     tiles[63] = jnp.zeros((16, 128), BF16)
 
 
+def total_kernel(rows, src, out):
+    total = src[0].astype(F32)
+    for i in range(1, src.shape[0]):
+        total += src[i].astype(F32)
+    copies = total.shape[0] // rows
+    part = total[0:rows]
+    for i in range(1, copies):
+        part += total[i * rows : (i + 1) * rows]
+    block = jnp.concatenate([part] * copies, axis=0).astype(BF16)
+    for i in range(out.shape[0]):
+        out[i] = block
+
+
 def spread_kernel(tiles, g1_ref, g2_ref, bias1_ref, bias2_ref):
     for r in range(6):
         pieces = []
@@ -311,12 +324,17 @@
     )(*args)
 
 
-def gradient_sum(tiles):
+def gradient_sum(tiles, interpret):
     axes = ("box", "snap")
     parts = lax.axis_size(axes)
-    mine = lax.all_to_all(tiles.reshape(parts, -1, 128), axes, 0, 0, tiled=True)
-    total = jnp.sum(mine.astype(F32), axis=0, keepdims=True).astype(BF16)
-    spread = jnp.broadcast_to(total, (parts,) + total.shape[1:])
+    rows = TILES * 16 // parts
+    shape = (-1, max(rows, 16), 128)
+    mine = lax.all_to_all(tiles.reshape(parts, rows, 128), axes, 0, 0, tiled=True).reshape(shape)
+    (spread,) = call(
+        functools.partial(total_kernel, rows), "total", (mine,),
+        (jax.ShapeDtypeStruct(mine.shape, BF16),), [], 4, 1_000_000, interpret,
+    )
+    spread = spread.reshape(parts, rows, 128)
     return lax.all_to_all(spread, axes, 0, 0, tiled=True).reshape(TILES, 16, 128)
 
 
@@ -356,7 +374,7 @@
     )
     hid_lo = lax.ppermute(tail, "box", forward)
     hid_hi = lax.ppermute(head, "box", backward)
-    tiles = gradient_sum(tiles)
+    tiles = gradient_sum(tiles, interpret)
     (decoded,) = call(
         out_kernel, "decode", (plane_counts, hid, hid_lo, hid_hi, w_second, b_second[:, None]),
         (jax.ShapeDtypeStruct((1, SLOTS, C, CELLS), BF16),),

time: 82.7 us -> 82.5 us (level)
    pallas_call x5 -> x6, Pallas kernels: 12.6 us -> 13.4 us  [call(): pl.pallas_call(kernel, out_shape=outs, in_specs=[SM if a.dtype == jnp.int...]
where the time goes in v5:
time: 82.5 us; the launch traced here: 82.2 us
  starting transfers between devices  24.6 us (30%)
  waiting for transfers between devices  20.8 us (25%)
  blocking collectives  20.4 us (25%)
  Pallas kernels  13.4 us (16%)
  between operations  1.52 us (2%)
  local copies, waits for them, and re-layouts  1.48 us (2%)
    all_to_all x1, blocking collectives, gradient_sum(): lax.all_to_all(tiles.reshape(parts, rows, 128), axes, 0, 0, tiled=True)  20.4 us
    pallas_call x6, Pallas kernels, call(): pl.pallas_call(kernel, out_shape=outs, in_specs=[SM if a.dtype == jnp.int...  13.4 us
    all_to_all x1, starting transfers between devices, gradient_sum(): lax.all_to_all(spread, axes, 0, 0, tiled=True).reshape(TILES, 16, 128)  10.8 us
    ppermute x1, waiting for transfers between devices, local(): hid_hi = lax.ppermute(head, 'box', backward)  7.75 us
    ppermute x1, waiting for transfers between devices, local(): lax.ppermute(jnp.concatenate([x[0:2], u[0:2]], axis=0), 'box', backward)  7.06 us
    ppermute x1, starting transfers between devices, local(): lax.ppermute(jnp.concatenate([last(x), last(u)], axis=0), 'box', forward)  4.96 us
    ppermute x1, starting transfers between devices, local(): hid_lo = lax.ppermute(tail, 'box', forward)  4.93 us
    ppermute x1, waiting for transfers between devices, local(): hid_lo = lax.ppermute(tail, 'box', forward)  3 us
  transfers between devices with their start and end apart: 5, of which 4 were waited for; matrix products, arithmetic and copies ran while one was open for 0% of the time, Pallas kernels for 9%

profile of v5, /device:TPU:126, one launch (start us, length us, event | category | flops | bytes accessed | tf_op | source)
XLA Modules:
  0.0 82.2 jit_solution(18122321711072907229)
XLA Ops:
  0.6 0.0 copy-start
  0.6 0.0 copy-start.1
  0.7 0.0 copy-start.4
  0.7 0.0 copy-start.2
  0.7 0.0 copy-start.3
  1.4 1.3 %slice_bitcast_fusion = (bf16[2,48,1024]{2,1,0:T(8,128)(2,1)S(1)}, bf16[2,48,1024]{2,1,0:T(8,128)(2,1)S(1)}, bf16[2,48,1024]{2,1,0:T(8,128)(2,1)S(1)}, bf16[2,48,1024]{2,1,0:T(8,128)(2,1)S(1)}) fusion(bf16[1,5,48,1024]{3,2,1,0:T(8,128)(2,1)} %param.8, s32[]{:T(128)S(6)} %select_n.4, bf16[1,5,48,1024]{3,2,1,0:T(8,128)(2,1)} %param.7), kind=kLoop, calls=%fused_computation.2 | loop fusion | bytes 1572868 | tf_op jit(solution)/shard_map/slice | solution.py:351
  2.8 5.0 %collective-permute-start = (bf16[4,48,1024]{2,1,0:T(8,128)(2,1)S(1)}, bf16[4,48,1024]{2,1,0:T(8,128)(2,1)S(1)}, u32[]{:S(2)}, u32[]{:S(2)}) collective-permute-start(bf16[4,48,1024]{2,1,0:T(8,128)(2,1)S(1)} %pad_maximum_fusion), channel_id=1, source_target_pairs={{0,4},{4,8},{8,12},{12,16},{16,20},{20,24},{24,28},{28,32},{32,36}... | collective-permute-start | bytes 1179656 | tf_op jit(solution)/shard_map/ppermute | solution.py:350
  7.8 1.9 %collective-permute-start.1 = (bf16[4,48,1024]{2,1,0:T(8,128)(2,1)S(1)}, bf16[4,48,1024]{2,1,0:T(8,128)(2,1)S(1)}, u32[]{:S(2)}, u32[]{:S(2)}) collective-permute-start(bf16[4,48,1024]{2,1,0:T(8,128)(2,1)S(1)} %pad_maximum_fusion.1), channel_id=1, source_target_pairs={{4,0},{8,4},{12,8},{16,12},{20,16},{24,20},{28,24},{32,28},{36,32}... | collective-permute-start | bytes 1179656 | tf_op jit(solution)/shard_map/ppermute | solution.py:351
  9.7 0.0 copy-done.4
  9.7 0.1 copy.12.b1_ref
  9.8 0.0 copy-done
  9.8 0.0 copy-done.1
  9.8 0.0 copy-done.2
  9.8 0.0 copy-done.3
  9.8 3.3 %front.1 = (bf16[5,144,1280]{2,1,0:T(8,128)(2,1)S(1)}, bf16[5,144,1280]{2,1,0:T(8,128)(2,1)S(1)}, bf16[144,432]{1,0:T(8,128)(2,1)S(1)}, bf16[144,432]{1,0:T(8,12...) custom-call(s32[1,1]{1,0:T(1,128)S(6)} %copy.14.count_ref, bf16[5,48,1024]{2,1,0:T(8,128)(2,1)S(1)} %bitcast.21, ...), custom_call_target="tpu_custom_call" | custom-call | flops 1200000000 | bytes 2000000 | tf_op jit(solution)/shard_map/front/pallas_call | solution.py:314
  13.1 2.9 %collective-permute-done.lo_ref = bf16[4,48,1024]{2,1,0:T(8,128)(2,1)S(1)} collective-permute-done((bf16[4,48,1024]{2,1,0:T(8,128)(2,1)S(1)}, bf16[4,48,1024]{2,1,0:T(8,128)(2,1)S(1)}, u32[]{:S(2)}, u32[]{:S(2)}) %collective-permute-start) | collective-permute-done | bytes 393248 | tf_op jit(solution)/shard_map/ppermute | solution.py:350
  16.1 1.3 %low.1 = (bf16[2,144,1280]{2,1,0:T(8,128)(2,1)S(1)}, bf16[2,144,1280]{2,1,0:T(8,128)(2,1)S(1)}, f32[2,48,1024]{2,1,0:T(8,128)S(1)}, f32[2,48,1024]{2,1,0:T(8,128)S(1)}) custom-call(bf16[144,432]{1,0:T(8,128)(2,1)S(1)} %get-tuple-element.25.w1s, bf16[144,432]{1,0:T(8,128)(2,1)S(1)} %get-tuple-element.26.w2s, f32[5,48,1024]{2,1,0:T(8,128)S(1)} %get-tuple-element.27.acc1, ...), custom_call_target="tpu_custom_call" | custom-call | flops 300000000 | bytes 2000000 | tf_op jit(solution)/shard_map/low/pallas_call | solution.py:314
  17.4 7.1 %collective-permute-done.1.hi_ref = bf16[4,48,1024]{2,1,0:T(8,128)(2,1)S(1)} collective-permute-done((bf16[4,48,1024]{2,1,0:T(8,128)(2,1)S(1)}, bf16[4,48,1024]{2,1,0:T(8,128)(2,1)S(1)}, u32[]{:S(2)}, u32[]{:S(2)}) %collective-permute-start.1) | collective-permute-done | bytes 393248 | tf_op jit(solution)/shard_map/ppermute | solution.py:351
  24.5 0.0 copy-start.5
  24.5 4.3 %grads.1 = (bf16[5,48,1024]{2,1,0:T(8,128)(2,1)S(1)}, bf16[2,48,1024]{2,1,0:T(8,128)(2,1)S(1)}, bf16[2,48,1024]{2,1,0:T(8,128)(2,1)S(1)}, bf16[64,16,128]{2,1,0:T(8,128)(2,1)S(1)}) custom-call(s32[1,1]{1,0:T(1,128)S(6)} %copy.14.count_ref, bf16[5,144,1280]{2,1,0:T(8,128)(2,1)S(1)} %get-tuple-element.23.px, bf16[5,144,1280]{2,1,0:T(8,128)(2,1)S(1)} %get-tuple-element.24.pu, ...), custom_call_target="tpu_custom_call" | custom-call | flops 2000000000 | bytes 2000000 | tf_op jit(solution)/shard_map/grads/pallas_call | solution.py:314
  28.7 20.4 %all_to_all.10 = bf16[256,4,128]{2,1,0:T(4,128)(2,1)S(1)} all-to-all(bf16[256,4,128]{2,1,0:T(4,128)(2,1)S(1)} %bitcast.24), channel_id=1, replica_groups=mesh['box'=64,'snap'=4] {'box','snap'}, dimensions={0} | all-to-all | bytes 524288 | tf_op jit(solution)/shard_map/all_to_all | solution.py:332
  49.2 0.8 total.1
  50.0 10.8 %all-to-all-start.1 = ((bf16[256,4,128]{2,1,0:T(4,128)(2,1)}), bf16[256,4,128]{2,1,0:T(4,128)(2,1)S(1)}, u32[]{:S(2)}, u32[]{:S(2)}) async-start(bf16[256,4,128]{2,1,0:T(4,128)(2,1)} %bitcast.12), calls=%async_computation.1 | async-start | bytes 524288 | tf_op jit(solution)/shard_map/all_to_all | solution.py:338
  60.8 4.9 %collective-permute-start.2 = (bf16[2,48,1024]{2,1,0:T(8,128)(2,1)S(1)}, bf16[2,48,1024]{2,1,0:T(8,128)(2,1)S(1)}, u32[]{:S(2)}, u32[]{:S(2)}) collective-permute-start(bf16[2,48,1024]{2,1,0:T(8,128)(2,1)S(1)} %get-tuple-element.34), channel_id=1, source_target_pairs={{0,4},{4,8},{8,12},{12,16},{16,20},{20,24},{24,28},{28,32},{32,36}... | collective-permute-start | bytes 589832 | tf_op jit(solution)/shard_map/ppermute | solution.py:375
  65.8 1.9 %collective-permute-start.3 = (bf16[2,48,1024]{2,1,0:T(8,128)(2,1)S(1)}, bf16[2,48,1024]{2,1,0:T(8,128)(2,1)S(1)}, u32[]{:S(2)}, u32[]{:S(2)}) collective-permute-start(bf16[2,48,1024]{2,1,0:T(8,128)(2,1)S(1)} %get-tuple-element.35), channel_id=1, source_target_pairs={{4,0},{8,4},{12,8},{16,12},{20,16},{24,20},{28,24},{32,28},{36,32}... | collective-permute-start | bytes 589832 | tf_op jit(solution)/shard_map/ppermute | solution.py:376
  67.7 0.0 copy-done.5
  67.7 0.1 copy.13.b2_ref
  67.8 3.0 %collective-permute-done.2.lo_ref = bf16[2,48,1024]{2,1,0:T(8,128)(2,1)S(1)} collective-permute-done((bf16[2,48,1024]{2,1,0:T(8,128)(2,1)S(1)}, bf16[2,48,1024]{2,1,0:T(8,128)(2,1)S(1)}, u32[]{:S(2)}, u32[]{:S(2)}) %collective-permute-start.2) | collective-permute-done | bytes 196640 | tf_op jit(solution)/shard_map/ppermute | solution.py:375
  70.8 7.8 %collective-permute-done.3.hi_ref = bf16[2,48,1024]{2,1,0:T(8,128)(2,1)S(1)} collective-permute-done((bf16[2,48,1024]{2,1,0:T(8,128)(2,1)S(1)}, bf16[2,48,1024]{2,1,0:T(8,128)(2,1)S(1)}, u32[]{:S(2)}, u32[]{:S(2)}) %collective-permute-start.3) | collective-permute-done | bytes 196640 | tf_op jit(solution)/shard_map/ppermute | solution.py:376
  78.5 2.7 %decode.1 = bf16[1,5,48,1024]{3,2,1,0:T(8,128)(2,1)} custom-call(s32[1,1]{1,0:T(1,128)S(6)} %copy.14.count_ref, bf16[5,48,1024]{2,1,0:T(8,128)(2,1)S(1)} %get-tuple-element.33.hid, bf16[2,48,1024]{2,1,0:T(8,128)(2,1)S(1)} %collective-permute-done.2.lo_ref, bf16[2,48,1024]{2,1,0:T(8,128)(2,1)S(1)} %collective-permute-done.3.hi_ref, ...), custom_call_target="tpu_custom_call" | custom-call | flops 1000000000 | bytes 2000000 | tf_op jit(solution)/shard_map/decode/pallas_call | solution.py:314
  81.2 0.0 all-to-all-done.1
  81.2 1.0 %spread.1 = (f32[48,1296]{1,0:T(8,128)}, f32[48,1296]{1,0:T(8,128)}, f32[1,48]{1,0:T(1,128)}, f32[1,48]{1,0:T(1,128)}) custom-call(bf16[64,16,128]{2,1,0:T(8,128)(2,1)S(1)} %bitcast.23), custom_call_target="tpu_custom_call" | custom-call | flops 100000000 | bytes 2000000 | tf_op jit(solution)/shard_map/spread/pallas_call | solution.py:314
  (2 shorter events, 0.1 us)
Async XLA Ops:
  0.6 9.2 %copy-start = (bf16[1,5,48,1024]{3,2,1,0:T(8,128)(2,1)S(1)}, bf16[1,5,48,1024]{3,2,1,0:T(8,128)(2,1)}, u32[]{:S(2)}) copy-start(bf16[1,5,48,1024]{3,2,1,0:T(8,128)(2,1)} %param.7) | copy-start | bytes 1474564
  0.6 9.2 %copy-start.1 = (bf16[1,5,48,1024]{3,2,1,0:T(8,128)(2,1)S(1)}, bf16[1,5,48,1024]{3,2,1,0:T(8,128)(2,1)}, u32[]{:S(2)}) copy-start(bf16[1,5,48,1024]{3,2,1,0:T(8,128)(2,1)} %param.8) | copy-start | bytes 1474564
  0.7 9.0 %copy-start.4 = (f32[48]{0:T(128)S(1)}, f32[48]{0:T(128)}, u32[]{:S(2)}) copy-start(f32[48]{0:T(128)} %param.11) | copy-start | bytes 580
  0.7 9.1 %copy-start.2 = (bf16[48,1296]{1,0:T(8,128)(2,1)S(1)}, bf16[48,1296]{1,0:T(8,128)(2,1)}, u32[]{:S(2)}) copy-start(bf16[48,1296]{1,0:T(8,128)(2,1)} %w1_ref.1) | copy-start | bytes 373252
  0.7 9.1 %copy-start.3 = (bf16[48,1296]{1,0:T(8,128)(2,1)S(1)}, bf16[48,1296]{1,0:T(8,128)(2,1)}, u32[]{:S(2)}) copy-start(bf16[48,1296]{1,0:T(8,128)(2,1)} %w2_ref.3) | copy-start | bytes 373252
  2.8 13.3 %collective-permute-start = (bf16[4,48,1024]{2,1,0:T(8,128)(2,1)S(1)}, bf16[4,48,1024]{2,1,0:T(8,128)(2,1)S(1)}, u32[]{:S(2)}, u32[]{:S(2)}) collective-permute-start(bf16[4,48,1024]{2,1,0:T(8,128)(2,1)S(1)} %pad_maximum_fusion), channel_id=1, source_target_pairs={{0,4},{4,8},{8,12},{12,16},{16,20},{20,24},{24,28},{28,32},{32,36}... | collective-permute-start | bytes 1179656 | tf_op jit(solution)/shard_map/ppermute | solution.py:350
  7.8 16.7 %collective-permute-start.1 = (bf16[4,48,1024]{2,1,0:T(8,128)(2,1)S(1)}, bf16[4,48,1024]{2,1,0:T(8,128)(2,1)S(1)}, u32[]{:S(2)}, u32[]{:S(2)}) collective-permute-start(bf16[4,48,1024]{2,1,0:T(8,128)(2,1)S(1)} %pad_maximum_fusion.1), channel_id=1, source_target_pairs={{4,0},{8,4},{12,8},{16,12},{20,16},{24,20},{28,24},{32,28},{36,32}... | collective-permute-start | bytes 1179656 | tf_op jit(solution)/shard_map/ppermute | solution.py:351
  24.5 43.2 %copy-start.5 = (f32[48]{0:T(128)S(1)}, f32[48]{0:T(128)}, u32[]{:S(2)}) copy-start(f32[48]{0:T(128)} %param.13) | copy-start | bytes 580
  50.0 31.3 %all-to-all-start.1 = ((bf16[256,4,128]{2,1,0:T(4,128)(2,1)}), bf16[256,4,128]{2,1,0:T(4,128)(2,1)S(1)}, u32[]{:S(2)}, u32[]{:S(2)}) async-start(bf16[256,4,128]{2,1,0:T(4,128)(2,1)} %bitcast.12), calls=%async_computation.1 | async-start | bytes 524288 | tf_op jit(solution)/shard_map/all_to_all | solution.py:338
  60.8 10.0 %collective-permute-start.2 = (bf16[2,48,1024]{2,1,0:T(8,128)(2,1)S(1)}, bf16[2,48,1024]{2,1,0:T(8,128)(2,1)S(1)}, u32[]{:S(2)}, u32[]{:S(2)}) collective-permute-start(bf16[2,48,1024]{2,1,0:T(8,128)(2,1)S(1)} %get-tuple-element.34), channel_id=1, source_target_pairs={{0,4},{4,8},{8,12},{12,16},{16,20},{20,24},{24,28},{28,32},{32,36}... | collective-permute-start | bytes 589832 | tf_op jit(solution)/shard_map/ppermute | solution.py:375
  65.8 12.8 %collective-permute-start.3 = (bf16[2,48,1024]{2,1,0:T(8,128)(2,1)S(1)}, bf16[2,48,1024]{2,1,0:T(8,128)(2,1)S(1)}, u32[]{:S(2)}, u32[]{:S(2)}) collective-permute-start(bf16[2,48,1024]{2,1,0:T(8,128)(2,1)S(1)} %get-tuple-element.35), channel_id=1, source_target_pairs={{4,0},{8,4},{12,8},{16,12},{20,16},{24,20},{28,24},{32,28},{36,32}... | collective-permute-start | bytes 589832 | tf_op jit(solution)/shard_map/ppermute | solution.py:376

commit v6 on v5

--- a/solution.py
+++ b/solution.py
@@ -281,16 +281,22 @@
         out[...] = jnp.sum(jnp.where(row == col, both, 0.0), axis=0, keepdims=True)
 
 
-def out_kernel(count_ref, hid, lo_ref, hi_ref, w2_ref, b2_ref, out_ref, ph, lh, hh, w2s, acc):
+def inner_kernel(hid, w2_ref, w2s, acc, ph):
+    masks = lane_masks()
+    stack_taps(w2_ref, w2s)
+    for p in range(SLOTS):
+        put_shifts(split(hid[p]), ph, p, masks)
+    conv_local(acc, w2s, ph)
+
+
+def out_kernel(count_ref, w2s, inner, lo_ref, hi_ref, b2_ref, out_ref, lh, hh, acc):
     count = count_ref[0, 0]
     masks = lane_masks()
-    stack_taps(w2_ref, w2s)
+    for p in range(SLOTS):
+        acc[p] = inner[p]
     for i in range(2):
         put_shifts(split(lo_ref[i]), lh, i, masks)
         put_shifts(split(hi_ref[i]), hh, i, masks)
-    for p in range(SLOTS):
-        put_shifts(split(hid[p]), ph, p, masks)
-    conv_local(acc, w2s, ph)
     conv_halo(acc, w2s[0:C, :], lh, 0)
     conv_halo(acc, w2s[2 * C : 3 * C, :], hh, count - 2)
     for p in range(SLOTS):
@@ -375,10 +381,14 @@
     hid_lo = lax.ppermute(tail, "box", forward)
     hid_hi = lax.ppermute(head, "box", backward)
     tiles = gradient_sum(tiles, interpret)
+    second, inner = call(
+        inner_kernel, "inner", (hid, w_second), (stacked, SUMS),
+        [((SLOTS, ROWS, WIDE), BF16)], 16, 1_000_000_000, interpret,
+    )
     (decoded,) = call(
-        out_kernel, "decode", (plane_counts, hid, hid_lo, hid_hi, w_second, b_second[:, None]),
+        out_kernel, "decode", (plane_counts, second, inner, hid_lo, hid_hi, b_second[:, None]),
         (jax.ShapeDtypeStruct((1, SLOTS, C, CELLS), BF16),),
-        [((SLOTS, ROWS, WIDE), BF16), halo, halo, (WEIGHT, BF16), ((SLOTS, C, CELLS), F32)], 24, 1_000_000_000, interpret,
+        [halo, halo, ((SLOTS, C, CELLS), F32)], 16, 300_000_000, interpret,
     )
     grad = jax.ShapeDtypeStruct((C, 27 * C), F32)
     line = jax.ShapeDtypeStruct((1, C), F32)

time: 82.5 us -> 81.7 us (level)
  waiting for transfers between devices: 20.8 us -> 19.7 us
    ppermute x1, waiting for transfers between devices: 3 us -> 1.9 us  [local(): hid_lo = lax.ppermute(tail, 'box', forward)]
    pallas_call x6 -> x7, Pallas kernels: 13.4 us -> 13.7 us  [call(): pl.pallas_call(kernel, out_shape=outs, in_specs=[SM if a.dtype == jnp.int...]
where the time goes in v6:
time: 81.7 us; the launch traced here: 81.4 us
  starting transfers between devices  24.6 us (30%)
  blocking collectives  20.4 us (25%)
  waiting for transfers between devices  19.7 us (24%)
  Pallas kernels  13.7 us (17%)
  between operations  1.53 us (2%)
  local copies, waits for them, and re-layouts  1.48 us (2%)
    all_to_all x1, blocking collectives, gradient_sum(): lax.all_to_all(tiles.reshape(parts, rows, 128), axes, 0, 0, tiled=True)  20.4 us
    pallas_call x7, Pallas kernels, call(): pl.pallas_call(kernel, out_shape=outs, in_specs=[SM if a.dtype == jnp.int...  13.7 us
    all_to_all x1, starting transfers between devices, gradient_sum(): lax.all_to_all(spread, axes, 0, 0, tiled=True).reshape(TILES, 16, 128)  10.8 us
    ppermute x1, waiting for transfers between devices, local(): hid_hi = lax.ppermute(head, 'box', backward)  7.75 us
    ppermute x1, waiting for transfers between devices, local(): lax.ppermute(jnp.concatenate([x[0:2], u[0:2]], axis=0), 'box', backward)  7.06 us
    ppermute x1, starting transfers between devices, local(): lax.ppermute(jnp.concatenate([last(x), last(u)], axis=0), 'box', forward)  4.96 us
    ppermute x1, starting transfers between devices, local(): hid_lo = lax.ppermute(tail, 'box', forward)  4.93 us
    ppermute x1, waiting for transfers between devices, local(): lax.ppermute(jnp.concatenate([last(x), last(u)], axis=0), 'box', forward)  2.94 us
  transfers between devices with their start and end apart: 5, of which 4 were waited for; matrix products, arithmetic and copies ran while one was open for 0% of the time, Pallas kernels for 9%

profile of v6, /device:TPU:126, one launch (start us, length us, event | category | flops | bytes accessed | tf_op | source)
XLA Modules:
  0.0 81.4 jit_solution(5238519364189591879)
XLA Ops:
  0.6 0.0 copy-start
  0.6 0.0 copy-start.1
  0.7 0.0 copy-start.4
  0.7 0.0 copy-start.2
  0.7 0.0 copy-start.3
  1.4 1.3 %slice_bitcast_fusion = (bf16[2,48,1024]{2,1,0:T(8,128)(2,1)S(1)}, bf16[2,48,1024]{2,1,0:T(8,128)(2,1)S(1)}, bf16[2,48,1024]{2,1,0:T(8,128)(2,1)S(1)}, bf16[2,48,1024]{2,1,0:T(8,128)(2,1)S(1)}) fusion(bf16[1,5,48,1024]{3,2,1,0:T(8,128)(2,1)} %param.8, s32[]{:T(128)S(6)} %select_n.4, bf16[1,5,48,1024]{3,2,1,0:T(8,128)(2,1)} %param.7), kind=kLoop, calls=%fused_computation.2 | loop fusion | bytes 1572868 | tf_op jit(solution)/shard_map/slice | solution.py:357
  2.8 5.0 %collective-permute-start = (bf16[4,48,1024]{2,1,0:T(8,128)(2,1)S(1)}, bf16[4,48,1024]{2,1,0:T(8,128)(2,1)S(1)}, u32[]{:S(2)}, u32[]{:S(2)}) collective-permute-start(bf16[4,48,1024]{2,1,0:T(8,128)(2,1)S(1)} %pad_maximum_fusion), channel_id=1, source_target_pairs={{0,4},{4,8},{8,12},{12,16},{16,20},{20,24},{24,28},{28,32},{32,36}... | collective-permute-start | bytes 1179656 | tf_op jit(solution)/shard_map/ppermute | solution.py:356
  7.8 1.9 %collective-permute-start.1 = (bf16[4,48,1024]{2,1,0:T(8,128)(2,1)S(1)}, bf16[4,48,1024]{2,1,0:T(8,128)(2,1)S(1)}, u32[]{:S(2)}, u32[]{:S(2)}) collective-permute-start(bf16[4,48,1024]{2,1,0:T(8,128)(2,1)S(1)} %pad_maximum_fusion.1), channel_id=1, source_target_pairs={{4,0},{8,4},{12,8},{16,12},{20,16},{24,20},{28,24},{32,28},{36,32}... | collective-permute-start | bytes 1179656 | tf_op jit(solution)/shard_map/ppermute | solution.py:357
  9.7 0.0 copy-done.4
  9.7 0.1 copy.12.b1_ref
  9.8 0.0 copy-done
  9.8 0.0 copy-done.1
  9.8 0.0 copy-done.2
  9.8 0.0 copy-done.3
  9.8 3.3 %front.1 = (bf16[5,144,1280]{2,1,0:T(8,128)(2,1)S(1)}, bf16[5,144,1280]{2,1,0:T(8,128)(2,1)S(1)}, bf16[144,432]{1,0:T(8,128)(2,1)S(1)}, bf16[144,432]{1,0:T(8,12...) custom-call(s32[1,1]{1,0:T(1,128)S(6)} %copy.14.count_ref, bf16[5,48,1024]{2,1,0:T(8,128)(2,1)S(1)} %bitcast.21, ...), custom_call_target="tpu_custom_call" | custom-call | flops 1200000000 | bytes 2000000 | tf_op jit(solution)/shard_map/front/pallas_call | solution.py:320
  13.1 2.9 %collective-permute-done.lo_ref = bf16[4,48,1024]{2,1,0:T(8,128)(2,1)S(1)} collective-permute-done((bf16[4,48,1024]{2,1,0:T(8,128)(2,1)S(1)}, bf16[4,48,1024]{2,1,0:T(8,128)(2,1)S(1)}, u32[]{:S(2)}, u32[]{:S(2)}) %collective-permute-start) | collective-permute-done | bytes 393248 | tf_op jit(solution)/shard_map/ppermute | solution.py:356
  16.1 1.3 %low.1 = (bf16[2,144,1280]{2,1,0:T(8,128)(2,1)S(1)}, bf16[2,144,1280]{2,1,0:T(8,128)(2,1)S(1)}, f32[2,48,1024]{2,1,0:T(8,128)S(1)}, f32[2,48,1024]{2,1,0:T(8,128)S(1)}) custom-call(bf16[144,432]{1,0:T(8,128)(2,1)S(1)} %get-tuple-element.27.w1s, bf16[144,432]{1,0:T(8,128)(2,1)S(1)} %get-tuple-element.28.w2s, f32[5,48,1024]{2,1,0:T(8,128)S(1)} %get-tuple-element.29.acc1, ...), custom_call_target="tpu_custom_call" | custom-call | flops 300000000 | bytes 2000000 | tf_op jit(solution)/shard_map/low/pallas_call | solution.py:320
  17.4 7.1 %collective-permute-done.1.hi_ref = bf16[4,48,1024]{2,1,0:T(8,128)(2,1)S(1)} collective-permute-done((bf16[4,48,1024]{2,1,0:T(8,128)(2,1)S(1)}, bf16[4,48,1024]{2,1,0:T(8,128)(2,1)S(1)}, u32[]{:S(2)}, u32[]{:S(2)}) %collective-permute-start.1) | collective-permute-done | bytes 393248 | tf_op jit(solution)/shard_map/ppermute | solution.py:357
  24.5 0.0 copy-start.5
  24.5 4.3 %grads.1 = (bf16[5,48,1024]{2,1,0:T(8,128)(2,1)S(1)}, bf16[2,48,1024]{2,1,0:T(8,128)(2,1)S(1)}, bf16[2,48,1024]{2,1,0:T(8,128)(2,1)S(1)}, bf16[64,16,128]{2,1,0:T(8,128)(2,1)S(1)}) custom-call(s32[1,1]{1,0:T(1,128)S(6)} %copy.14.count_ref, bf16[5,144,1280]{2,1,0:T(8,128)(2,1)S(1)} %get-tuple-element.25.px, bf16[5,144,1280]{2,1,0:T(8,128)(2,1)S(1)} %get-tuple-element.26.pu, ...), custom_call_target="tpu_custom_call" | custom-call | flops 2000000000 | bytes 2000000 | tf_op jit(solution)/shard_map/grads/pallas_call | solution.py:320
  28.7 20.4 %all_to_all.10 = bf16[256,4,128]{2,1,0:T(4,128)(2,1)S(1)} all-to-all(bf16[256,4,128]{2,1,0:T(4,128)(2,1)S(1)} %bitcast.24), channel_id=1, replica_groups=mesh['box'=64,'snap'=4] {'box','snap'}, dimensions={0} | all-to-all | bytes 524288 | tf_op jit(solution)/shard_map/all_to_all | solution.py:338
  49.2 0.8 total.1
  49.9 10.8 %all-to-all-start.1 = ((bf16[256,4,128]{2,1,0:T(4,128)(2,1)}), bf16[256,4,128]{2,1,0:T(4,128)(2,1)S(1)}, u32[]{:S(2)}, u32[]{:S(2)}) async-start(bf16[256,4,128]{2,1,0:T(4,128)(2,1)} %bitcast.12), calls=%async_computation.1 | async-start | bytes 524288 | tf_op jit(solution)/shard_map/all_to_all | solution.py:344
  60.8 4.9 %collective-permute-start.2 = (bf16[2,48,1024]{2,1,0:T(8,128)(2,1)S(1)}, bf16[2,48,1024]{2,1,0:T(8,128)(2,1)S(1)}, u32[]{:S(2)}, u32[]{:S(2)}) collective-permute-start(bf16[2,48,1024]{2,1,0:T(8,128)(2,1)S(1)} %get-tuple-element.38), channel_id=1, source_target_pairs={{0,4},{4,8},{8,12},{12,16},{16,20},{20,24},{24,28},{28,32},{32,36}... | collective-permute-start | bytes 589832 | tf_op jit(solution)/shard_map/ppermute | solution.py:381
  65.7 1.9 %collective-permute-start.3 = (bf16[2,48,1024]{2,1,0:T(8,128)(2,1)S(1)}, bf16[2,48,1024]{2,1,0:T(8,128)(2,1)S(1)}, u32[]{:S(2)}, u32[]{:S(2)}) collective-permute-start(bf16[2,48,1024]{2,1,0:T(8,128)(2,1)S(1)} %get-tuple-element.39), channel_id=1, source_target_pairs={{4,0},{8,4},{12,8},{16,12},{20,16},{24,20},{28,24},{32,28},{36,32}... | collective-permute-start | bytes 589832 | tf_op jit(solution)/shard_map/ppermute | solution.py:382
  67.7 0.0 copy-done.5
  67.7 0.1 copy.13.b2_ref
  67.8 1.1 %inner.1 = (bf16[144,432]{1,0:T(8,128)(2,1)S(1)}, f32[5,48,1024]{2,1,0:T(8,128)S(1)}) custom-call(bf16[5,48,1024]{2,1,0:T(8,128)(2,1)S(1)} %get-tuple-element.35.hid, bf16[48,1296]{1,0:T(8,128)(2,1)S(1)} %copy-done.3), custom_call_target="tpu_custom_call" | custom-call | flops 1000000000 | bytes 2000000 | tf_op jit(solution)/shard_map/inner/pallas_call | solution.py:320
  68.9 1.9 %collective-permute-done.2.lo_ref = bf16[2,48,1024]{2,1,0:T(8,128)(2,1)S(1)} collective-permute-done((bf16[2,48,1024]{2,1,0:T(8,128)(2,1)S(1)}, bf16[2,48,1024]{2,1,0:T(8,128)(2,1)S(1)}, u32[]{:S(2)}, u32[]{:S(2)}) %collective-permute-start.2) | collective-permute-done | bytes 196640 | tf_op jit(solution)/shard_map/ppermute | solution.py:381
  70.8 7.8 %collective-permute-done.3.hi_ref = bf16[2,48,1024]{2,1,0:T(8,128)(2,1)S(1)} collective-permute-done((bf16[2,48,1024]{2,1,0:T(8,128)(2,1)S(1)}, bf16[2,48,1024]{2,1,0:T(8,128)(2,1)S(1)}, u32[]{:S(2)}, u32[]{:S(2)}) %collective-permute-start.3) | collective-permute-done | bytes 196640 | tf_op jit(solution)/shard_map/ppermute | solution.py:382
  78.5 2.0 %decode.1 = bf16[1,5,48,1024]{3,2,1,0:T(8,128)(2,1)} custom-call(s32[1,1]{1,0:T(1,128)S(6)} %copy.14.count_ref, bf16[144,432]{1,0:T(8,128)(2,1)S(1)} %get-tuple-element.36.w2s, f32[5,48,1024]{2,1,0:T(8,128)S(1)} %get-tuple-element.37.inner, bf16[2,48,1024]{2,1,0:T(8,128)(2,1)S(1)} %collective-permute-done.2.lo_ref, ...), custom_call_target="tpu_custom_call" | custom-call | flops 300000000 | bytes 2000000 | tf_op jit(solution)/shard_map/decode/pallas_call | solution.py:320
  80.5 0.0 all-to-all-done.1
  80.5 1.0 %spread.1 = (f32[48,1296]{1,0:T(8,128)}, f32[48,1296]{1,0:T(8,128)}, f32[1,48]{1,0:T(1,128)}, f32[1,48]{1,0:T(1,128)}) custom-call(bf16[64,16,128]{2,1,0:T(8,128)(2,1)S(1)} %bitcast.23), custom_call_target="tpu_custom_call" | custom-call | flops 100000000 | bytes 2000000 | tf_op jit(solution)/shard_map/spread/pallas_call | solution.py:320
  (2 shorter events, 0.1 us)
Async XLA Ops:
  0.6 9.2 %copy-start = (bf16[1,5,48,1024]{3,2,1,0:T(8,128)(2,1)S(1)}, bf16[1,5,48,1024]{3,2,1,0:T(8,128)(2,1)}, u32[]{:S(2)}) copy-start(bf16[1,5,48,1024]{3,2,1,0:T(8,128)(2,1)} %param.7) | copy-start | bytes 1474564
  0.6 9.2 %copy-start.1 = (bf16[1,5,48,1024]{3,2,1,0:T(8,128)(2,1)S(1)}, bf16[1,5,48,1024]{3,2,1,0:T(8,128)(2,1)}, u32[]{:S(2)}) copy-start(bf16[1,5,48,1024]{3,2,1,0:T(8,128)(2,1)} %param.8) | copy-start | bytes 1474564
  0.7 9.0 %copy-start.4 = (f32[48]{0:T(128)S(1)}, f32[48]{0:T(128)}, u32[]{:S(2)}) copy-start(f32[48]{0:T(128)} %param.11) | copy-start | bytes 580
  0.7 9.1 %copy-start.2 = (bf16[48,1296]{1,0:T(8,128)(2,1)S(1)}, bf16[48,1296]{1,0:T(8,128)(2,1)}, u32[]{:S(2)}) copy-start(bf16[48,1296]{1,0:T(8,128)(2,1)} %w1_ref.1) | copy-start | bytes 373252
  0.7 9.1 %copy-start.3 = (bf16[48,1296]{1,0:T(8,128)(2,1)S(1)}, bf16[48,1296]{1,0:T(8,128)(2,1)}, u32[]{:S(2)}) copy-start(bf16[48,1296]{1,0:T(8,128)(2,1)} %w2_ref.3) | copy-start | bytes 373252
  2.8 13.3 %collective-permute-start = (bf16[4,48,1024]{2,1,0:T(8,128)(2,1)S(1)}, bf16[4,48,1024]{2,1,0:T(8,128)(2,1)S(1)}, u32[]{:S(2)}, u32[]{:S(2)}) collective-permute-start(bf16[4,48,1024]{2,1,0:T(8,128)(2,1)S(1)} %pad_maximum_fusion), channel_id=1, source_target_pairs={{0,4},{4,8},{8,12},{12,16},{16,20},{20,24},{24,28},{28,32},{32,36}... | collective-permute-start | bytes 1179656 | tf_op jit(solution)/shard_map/ppermute | solution.py:356
  7.8 16.7 %collective-permute-start.1 = (bf16[4,48,1024]{2,1,0:T(8,128)(2,1)S(1)}, bf16[4,48,1024]{2,1,0:T(8,128)(2,1)S(1)}, u32[]{:S(2)}, u32[]{:S(2)}) collective-permute-start(bf16[4,48,1024]{2,1,0:T(8,128)(2,1)S(1)} %pad_maximum_fusion.1), channel_id=1, source_target_pairs={{4,0},{8,4},{12,8},{16,12},{20,16},{24,20},{28,24},{32,28},{36,32}... | collective-permute-start | bytes 1179656 | tf_op jit(solution)/shard_map/ppermute | solution.py:357
  24.5 43.2 %copy-start.5 = (f32[48]{0:T(128)S(1)}, f32[48]{0:T(128)}, u32[]{:S(2)}) copy-start(f32[48]{0:T(128)} %param.13) | copy-start | bytes 580
  49.9 30.5 %all-to-all-start.1 = ((bf16[256,4,128]{2,1,0:T(4,128)(2,1)}), bf16[256,4,128]{2,1,0:T(4,128)(2,1)S(1)}, u32[]{:S(2)}, u32[]{:S(2)}) async-start(bf16[256,4,128]{2,1,0:T(4,128)(2,1)} %bitcast.12), calls=%async_computation.1 | async-start | bytes 524288 | tf_op jit(solution)/shard_map/all_to_all | solution.py:344
  60.8 10.0 %collective-permute-start.2 = (bf16[2,48,1024]{2,1,0:T(8,128)(2,1)S(1)}, bf16[2,48,1024]{2,1,0:T(8,128)(2,1)S(1)}, u32[]{:S(2)}, u32[]{:S(2)}) collective-permute-start(bf16[2,48,1024]{2,1,0:T(8,128)(2,1)S(1)} %get-tuple-element.38), channel_id=1, source_target_pairs={{0,4},{4,8},{8,12},{12,16},{16,20},{20,24},{24,28},{28,32},{32,36}... | collective-permute-start | bytes 589832 | tf_op jit(solution)/shard_map/ppermute | solution.py:381
  65.7 12.8 %collective-permute-start.3 = (bf16[2,48,1024]{2,1,0:T(8,128)(2,1)S(1)}, bf16[2,48,1024]{2,1,0:T(8,128)(2,1)S(1)}, u32[]{:S(2)}, u32[]{:S(2)}) collective-permute-start(bf16[2,48,1024]{2,1,0:T(8,128)(2,1)S(1)} %get-tuple-element.39), channel_id=1, source_target_pairs={{4,0},{8,4},{12,8},{16,12},{20,16},{24,20},{28,24},{32,28},{36,32}... | collective-permute-start | bytes 589832 | tf_op jit(solution)/shard_map/ppermute | solution.py:382

commit v7 on v6

--- a/solution.py
+++ b/solution.py
@@ -289,15 +289,21 @@
     conv_local(acc, w2s, ph)
 
 
-def out_kernel(count_ref, w2s, inner, lo_ref, hi_ref, b2_ref, out_ref, lh, hh, acc):
+def edge_kernel(w2s, inner, lo_ref, two, lh):
+    masks = lane_masks()
+    for i in range(2):
+        put_shifts(split(lo_ref[i]), lh, i, masks)
+        two[i] = inner[i]
+    conv_halo(two, w2s[0:C, :], lh, 0)
+
+
+def out_kernel(count_ref, w2s, inner, two, hi_ref, b2_ref, out_ref, hh, acc):
     count = count_ref[0, 0]
     masks = lane_masks()
     for p in range(SLOTS):
-        acc[p] = inner[p]
-    for i in range(2):
-        put_shifts(split(lo_ref[i]), lh, i, masks)
+        acc[p] = two[p] if p < 2 else inner[p]
+    for i in range(2):
         put_shifts(split(hi_ref[i]), hh, i, masks)
-    conv_halo(acc, w2s[0:C, :], lh, 0)
     conv_halo(acc, w2s[2 * C : 3 * C, :], hh, count - 2)
     for p in range(SLOTS):
         keep = jnp.where(p < count, 1.0, 0.0).astype(F32)
@@ -385,10 +391,13 @@
         inner_kernel, "inner", (hid, w_second), (stacked, SUMS),
         [((SLOTS, ROWS, WIDE), BF16)], 16, 1_000_000_000, interpret,
     )
+    (edge,) = call(
+        edge_kernel, "edge", (second, inner, hid_lo), (two,), [halo], 8, 200_000_000, interpret
+    )
     (decoded,) = call(
-        out_kernel, "decode", (plane_counts, second, inner, hid_lo, hid_hi, b_second[:, None]),
+        out_kernel, "decode", (plane_counts, second, inner, edge, hid_hi, b_second[:, None]),
         (jax.ShapeDtypeStruct((1, SLOTS, C, CELLS), BF16),),
-        [halo, halo, ((SLOTS, C, CELLS), F32)], 16, 300_000_000, interpret,
+        [halo, ((SLOTS, C, CELLS), F32)], 16, 300_000_000, interpret,
     )
     grad = jax.ShapeDtypeStruct((C, 27 * C), F32)
     line = jax.ShapeDtypeStruct((1, C), F32)

time: 81.7 us -> 81.4 us (level)
    pallas_call x7 -> x8, Pallas kernels: 13.7 us -> 14 us  [call(): pl.pallas_call(kernel, out_shape=outs, in_specs=[SM if a.dtype == jnp.int...]
  transfers between devices with their start and end apart: 5 -> 5, of which waited for: 4 -> 4; matrix products, arithmetic and copies ran while one was open for 0% -> 0% of each run, Pallas kernels for 9% -> 10%
where the time goes in v7:
time: 81.4 us; the launch traced here: 81.1 us
  starting transfers between devices  24.6 us (30%)
  blocking collectives  20.4 us (25%)
  waiting for transfers between devices  19 us (23%)
  Pallas kernels  14 us (17%)
  between operations  1.54 us (2%)
  local copies, waits for them, and re-layouts  1.48 us (2%)
    all_to_all x1, blocking collectives, gradient_sum(): lax.all_to_all(tiles.reshape(parts, rows, 128), axes, 0, 0, tiled=True)  20.4 us
    pallas_call x8, Pallas kernels, call(): pl.pallas_call(kernel, out_shape=outs, in_specs=[SM if a.dtype == jnp.int...  14 us
    all_to_all x1, starting transfers between devices, gradient_sum(): lax.all_to_all(spread, axes, 0, 0, tiled=True).reshape(TILES, 16, 128)  10.8 us
    ppermute x1, waiting for transfers between devices, local(): hid_hi = lax.ppermute(head, 'box', backward)  7.13 us
    ppermute x1, waiting for transfers between devices, local(): lax.ppermute(jnp.concatenate([x[0:2], u[0:2]], axis=0), 'box', backward)  7.06 us
    ppermute x1, starting transfers between devices, local(): lax.ppermute(jnp.concatenate([last(x), last(u)], axis=0), 'box', forward)  4.96 us
    ppermute x1, starting transfers between devices, local(): hid_lo = lax.ppermute(tail, 'box', forward)  4.93 us
    ppermute x1, waiting for transfers between devices, local(): lax.ppermute(jnp.concatenate([last(x), last(u)], axis=0), 'box', forward)  2.94 us
  transfers between devices with their start and end apart: 5, of which 4 were waited for; matrix products, arithmetic and copies ran while one was open for 0% of the time, Pallas kernels for 10%

profile of v7, /device:TPU:126, one launch (start us, length us, event | category | flops | bytes accessed | tf_op | source)
XLA Modules:
  0.0 81.1 jit_solution(12335261497580406566)
XLA Ops:
  0.6 0.0 copy-start
  0.6 0.0 copy-start.1
  0.7 0.0 copy-start.4
  0.7 0.0 copy-start.2
  0.7 0.0 copy-start.3
  1.4 1.3 %slice_bitcast_fusion = (bf16[2,48,1024]{2,1,0:T(8,128)(2,1)S(1)}, bf16[2,48,1024]{2,1,0:T(8,128)(2,1)S(1)}, bf16[2,48,1024]{2,1,0:T(8,128)(2,1)S(1)}, bf16[2,48,1024]{2,1,0:T(8,128)(2,1)S(1)}) fusion(bf16[1,5,48,1024]{3,2,1,0:T(8,128)(2,1)} %param.8, s32[]{:T(128)S(6)} %select_n.4, bf16[1,5,48,1024]{3,2,1,0:T(8,128)(2,1)} %param.7), kind=kLoop, calls=%fused_computation.2 | loop fusion | bytes 1572868 | tf_op jit(solution)/shard_map/slice | solution.py:363
  2.8 5.0 %collective-permute-start = (bf16[4,48,1024]{2,1,0:T(8,128)(2,1)S(1)}, bf16[4,48,1024]{2,1,0:T(8,128)(2,1)S(1)}, u32[]{:S(2)}, u32[]{:S(2)}) collective-permute-start(bf16[4,48,1024]{2,1,0:T(8,128)(2,1)S(1)} %pad_maximum_fusion), channel_id=1, source_target_pairs={{0,4},{4,8},{8,12},{12,16},{16,20},{20,24},{24,28},{28,32},{32,36}... | collective-permute-start | bytes 1179656 | tf_op jit(solution)/shard_map/ppermute | solution.py:362
  7.8 1.9 %collective-permute-start.1 = (bf16[4,48,1024]{2,1,0:T(8,128)(2,1)S(1)}, bf16[4,48,1024]{2,1,0:T(8,128)(2,1)S(1)}, u32[]{:S(2)}, u32[]{:S(2)}) collective-permute-start(bf16[4,48,1024]{2,1,0:T(8,128)(2,1)S(1)} %pad_maximum_fusion.1), channel_id=1, source_target_pairs={{4,0},{8,4},{12,8},{16,12},{20,16},{24,20},{28,24},{32,28},{36,32}... | collective-permute-start | bytes 1179656 | tf_op jit(solution)/shard_map/ppermute | solution.py:363
  9.7 0.0 copy-done.4
  9.7 0.1 copy.12.b1_ref
  9.8 0.0 copy-done
  9.8 0.0 copy-done.1
  9.8 0.0 copy-done.2
  9.8 0.0 copy-done.3
  9.8 3.3 %front.1 = (bf16[5,144,1280]{2,1,0:T(8,128)(2,1)S(1)}, bf16[5,144,1280]{2,1,0:T(8,128)(2,1)S(1)}, bf16[144,432]{1,0:T(8,128)(2,1)S(1)}, bf16[144,432]{1,0:T(8,12...) custom-call(s32[1,1]{1,0:T(1,128)S(6)} %copy.14.count_ref, bf16[5,48,1024]{2,1,0:T(8,128)(2,1)S(1)} %bitcast.21, ...), custom_call_target="tpu_custom_call" | custom-call | flops 1200000000 | bytes 2000000 | tf_op jit(solution)/shard_map/front/pallas_call | solution.py:326
  13.1 2.9 %collective-permute-done.lo_ref = bf16[4,48,1024]{2,1,0:T(8,128)(2,1)S(1)} collective-permute-done((bf16[4,48,1024]{2,1,0:T(8,128)(2,1)S(1)}, bf16[4,48,1024]{2,1,0:T(8,128)(2,1)S(1)}, u32[]{:S(2)}, u32[]{:S(2)}) %collective-permute-start) | collective-permute-done | bytes 393248 | tf_op jit(solution)/shard_map/ppermute | solution.py:362
  16.1 1.3 %low.1 = (bf16[2,144,1280]{2,1,0:T(8,128)(2,1)S(1)}, bf16[2,144,1280]{2,1,0:T(8,128)(2,1)S(1)}, f32[2,48,1024]{2,1,0:T(8,128)S(1)}, f32[2,48,1024]{2,1,0:T(8,128)S(1)}) custom-call(bf16[144,432]{1,0:T(8,128)(2,1)S(1)} %get-tuple-element.27.w1s, bf16[144,432]{1,0:T(8,128)(2,1)S(1)} %get-tuple-element.28.w2s, f32[5,48,1024]{2,1,0:T(8,128)S(1)} %get-tuple-element.29.acc1, ...), custom_call_target="tpu_custom_call" | custom-call | flops 300000000 | bytes 2000000 | tf_op jit(solution)/shard_map/low/pallas_call | solution.py:326
  17.4 7.1 %collective-permute-done.1.hi_ref = bf16[4,48,1024]{2,1,0:T(8,128)(2,1)S(1)} collective-permute-done((bf16[4,48,1024]{2,1,0:T(8,128)(2,1)S(1)}, bf16[4,48,1024]{2,1,0:T(8,128)(2,1)S(1)}, u32[]{:S(2)}, u32[]{:S(2)}) %collective-permute-start.1) | collective-permute-done | bytes 393248 | tf_op jit(solution)/shard_map/ppermute | solution.py:363
  24.5 0.0 copy-start.5
  24.5 4.3 %grads.1 = (bf16[5,48,1024]{2,1,0:T(8,128)(2,1)S(1)}, bf16[2,48,1024]{2,1,0:T(8,128)(2,1)S(1)}, bf16[2,48,1024]{2,1,0:T(8,128)(2,1)S(1)}, bf16[64,16,128]{2,1,0:T(8,128)(2,1)S(1)}) custom-call(s32[1,1]{1,0:T(1,128)S(6)} %copy.14.count_ref, bf16[5,144,1280]{2,1,0:T(8,128)(2,1)S(1)} %get-tuple-element.25.px, bf16[5,144,1280]{2,1,0:T(8,128)(2,1)S(1)} %get-tuple-element.26.pu, ...), custom_call_target="tpu_custom_call" | custom-call | flops 2000000000 | bytes 2000000 | tf_op jit(solution)/shard_map/grads/pallas_call | solution.py:326
  28.7 20.4 %all_to_all.10 = bf16[256,4,128]{2,1,0:T(4,128)(2,1)S(1)} all-to-all(bf16[256,4,128]{2,1,0:T(4,128)(2,1)S(1)} %bitcast.24), channel_id=1, replica_groups=mesh['box'=64,'snap'=4] {'box','snap'}, dimensions={0} | all-to-all | bytes 524288 | tf_op jit(solution)/shard_map/all_to_all | solution.py:344
  49.2 0.8 total.1
  49.9 10.8 %all-to-all-start.1 = ((bf16[256,4,128]{2,1,0:T(4,128)(2,1)}), bf16[256,4,128]{2,1,0:T(4,128)(2,1)S(1)}, u32[]{:S(2)}, u32[]{:S(2)}) async-start(bf16[256,4,128]{2,1,0:T(4,128)(2,1)} %bitcast.12), calls=%async_computation.1 | async-start | bytes 524288 | tf_op jit(solution)/shard_map/all_to_all | solution.py:350
  60.8 4.9 %collective-permute-start.2 = (bf16[2,48,1024]{2,1,0:T(8,128)(2,1)S(1)}, bf16[2,48,1024]{2,1,0:T(8,128)(2,1)S(1)}, u32[]{:S(2)}, u32[]{:S(2)}) collective-permute-start(bf16[2,48,1024]{2,1,0:T(8,128)(2,1)S(1)} %get-tuple-element.38), channel_id=1, source_target_pairs={{0,4},{4,8},{8,12},{12,16},{16,20},{20,24},{24,28},{28,32},{32,36}... | collective-permute-start | bytes 589832 | tf_op jit(solution)/shard_map/ppermute | solution.py:387
  65.7 1.9 %collective-permute-start.3 = (bf16[2,48,1024]{2,1,0:T(8,128)(2,1)S(1)}, bf16[2,48,1024]{2,1,0:T(8,128)(2,1)S(1)}, u32[]{:S(2)}, u32[]{:S(2)}) collective-permute-start(bf16[2,48,1024]{2,1,0:T(8,128)(2,1)S(1)} %get-tuple-element.39), channel_id=1, source_target_pairs={{4,0},{8,4},{12,8},{16,12},{20,16},{24,20},{28,24},{32,28},{36,32}... | collective-permute-start | bytes 589832 | tf_op jit(solution)/shard_map/ppermute | solution.py:388
  67.7 0.0 copy-done.5
  67.7 0.1 copy.13.b2_ref
  67.8 1.1 %inner.1 = (bf16[144,432]{1,0:T(8,128)(2,1)S(1)}, f32[5,48,1024]{2,1,0:T(8,128)S(1)}) custom-call(bf16[5,48,1024]{2,1,0:T(8,128)(2,1)S(1)} %get-tuple-element.35.hid, bf16[48,1296]{1,0:T(8,128)(2,1)S(1)} %copy-done.3), custom_call_target="tpu_custom_call" | custom-call | flops 1000000000 | bytes 2000000 | tf_op jit(solution)/shard_map/inner/pallas_call | solution.py:326
  68.9 1.9 %collective-permute-done.2.lo_ref = bf16[2,48,1024]{2,1,0:T(8,128)(2,1)S(1)} collective-permute-done((bf16[2,48,1024]{2,1,0:T(8,128)(2,1)S(1)}, bf16[2,48,1024]{2,1,0:T(8,128)(2,1)S(1)}, u32[]{:S(2)}, u32[]{:S(2)}) %collective-permute-start.2) | collective-permute-done | bytes 196640 | tf_op jit(solution)/shard_map/ppermute | solution.py:387
  70.8 0.6 edge.1.two
  71.4 7.1 %collective-permute-done.3.hi_ref = bf16[2,48,1024]{2,1,0:T(8,128)(2,1)S(1)} collective-permute-done((bf16[2,48,1024]{2,1,0:T(8,128)(2,1)S(1)}, bf16[2,48,1024]{2,1,0:T(8,128)(2,1)S(1)}, u32[]{:S(2)}, u32[]{:S(2)}) %collective-permute-start.3) | collective-permute-done | bytes 196640 | tf_op jit(solution)/shard_map/ppermute | solution.py:388
  78.5 1.6 %decode.1 = bf16[1,5,48,1024]{3,2,1,0:T(8,128)(2,1)} custom-call(s32[1,1]{1,0:T(1,128)S(6)} %copy.14.count_ref, bf16[144,432]{1,0:T(8,128)(2,1)S(1)} %get-tuple-element.36.w2s, f32[5,48,1024]{2,1,0:T(8,128)S(1)} %get-tuple-element.37.inner, f32[2,48,1024]{2,1,0:T(8,128)S(1)} %edge.1.two, bf16[2,48,1024]{2,1,0:T(8,128)(2,1)S(1)} %collective-permute-done.3.hi_ref, ...), custom_call_target="tpu_custom_call" | custom-call | flops 300000000 | bytes 2000000 | tf_op jit(solution)/shard_map/decode/pallas_call | solution.py:326
  80.2 0.0 all-to-all-done.1
  80.2 1.0 %spread.1 = (f32[48,1296]{1,0:T(8,128)}, f32[48,1296]{1,0:T(8,128)}, f32[1,48]{1,0:T(1,128)}, f32[1,48]{1,0:T(1,128)}) custom-call(bf16[64,16,128]{2,1,0:T(8,128)(2,1)S(1)} %bitcast.23), custom_call_target="tpu_custom_call" | custom-call | flops 100000000 | bytes 2000000 | tf_op jit(solution)/shard_map/spread/pallas_call | solution.py:326
  (2 shorter events, 0.1 us)
Async XLA Ops:
  0.6 9.2 %copy-start = (bf16[1,5,48,1024]{3,2,1,0:T(8,128)(2,1)S(1)}, bf16[1,5,48,1024]{3,2,1,0:T(8,128)(2,1)}, u32[]{:S(2)}) copy-start(bf16[1,5,48,1024]{3,2,1,0:T(8,128)(2,1)} %param.7) | copy-start | bytes 1474564
  0.6 9.2 %copy-start.1 = (bf16[1,5,48,1024]{3,2,1,0:T(8,128)(2,1)S(1)}, bf16[1,5,48,1024]{3,2,1,0:T(8,128)(2,1)}, u32[]{:S(2)}) copy-start(bf16[1,5,48,1024]{3,2,1,0:T(8,128)(2,1)} %param.8) | copy-start | bytes 1474564
  0.7 9.0 %copy-start.4 = (f32[48]{0:T(128)S(1)}, f32[48]{0:T(128)}, u32[]{:S(2)}) copy-start(f32[48]{0:T(128)} %param.11) | copy-start | bytes 580
  0.7 9.1 %copy-start.2 = (bf16[48,1296]{1,0:T(8,128)(2,1)S(1)}, bf16[48,1296]{1,0:T(8,128)(2,1)}, u32[]{:S(2)}) copy-start(bf16[48,1296]{1,0:T(8,128)(2,1)} %w1_ref.1) | copy-start | bytes 373252
  0.7 9.1 %copy-start.3 = (bf16[48,1296]{1,0:T(8,128)(2,1)S(1)}, bf16[48,1296]{1,0:T(8,128)(2,1)}, u32[]{:S(2)}) copy-start(bf16[48,1296]{1,0:T(8,128)(2,1)} %w2_ref.3) | copy-start | bytes 373252
  2.8 13.3 %collective-permute-start = (bf16[4,48,1024]{2,1,0:T(8,128)(2,1)S(1)}, bf16[4,48,1024]{2,1,0:T(8,128)(2,1)S(1)}, u32[]{:S(2)}, u32[]{:S(2)}) collective-permute-start(bf16[4,48,1024]{2,1,0:T(8,128)(2,1)S(1)} %pad_maximum_fusion), channel_id=1, source_target_pairs={{0,4},{4,8},{8,12},{12,16},{16,20},{20,24},{24,28},{28,32},{32,36}... | collective-permute-start | bytes 1179656 | tf_op jit(solution)/shard_map/ppermute | solution.py:362
  7.8 16.7 %collective-permute-start.1 = (bf16[4,48,1024]{2,1,0:T(8,128)(2,1)S(1)}, bf16[4,48,1024]{2,1,0:T(8,128)(2,1)S(1)}, u32[]{:S(2)}, u32[]{:S(2)}) collective-permute-start(bf16[4,48,1024]{2,1,0:T(8,128)(2,1)S(1)} %pad_maximum_fusion.1), channel_id=1, source_target_pairs={{4,0},{8,4},{12,8},{16,12},{20,16},{24,20},{28,24},{32,28},{36,32}... | collective-permute-start | bytes 1179656 | tf_op jit(solution)/shard_map/ppermute | solution.py:363
  24.5 43.2 %copy-start.5 = (f32[48]{0:T(128)S(1)}, f32[48]{0:T(128)}, u32[]{:S(2)}) copy-start(f32[48]{0:T(128)} %param.13) | copy-start | bytes 580
  49.9 30.2 %all-to-all-start.1 = ((bf16[256,4,128]{2,1,0:T(4,128)(2,1)}), bf16[256,4,128]{2,1,0:T(4,128)(2,1)S(1)}, u32[]{:S(2)}, u32[]{:S(2)}) async-start(bf16[256,4,128]{2,1,0:T(4,128)(2,1)} %bitcast.12), calls=%async_computation.1 | async-start | bytes 524288 | tf_op jit(solution)/shard_map/all_to_all | solution.py:350
  60.8 10.0 %collective-permute-start.2 = (bf16[2,48,1024]{2,1,0:T(8,128)(2,1)S(1)}, bf16[2,48,1024]{2,1,0:T(8,128)(2,1)S(1)}, u32[]{:S(2)}, u32[]{:S(2)}) collective-permute-start(bf16[2,48,1024]{2,1,0:T(8,128)(2,1)S(1)} %get-tuple-element.38), channel_id=1, source_target_pairs={{0,4},{4,8},{8,12},{12,16},{16,20},{20,24},{24,28},{28,32},{32,36}... | collective-permute-start | bytes 589832 | tf_op jit(solution)/shard_map/ppermute | solution.py:387
  65.7 12.8 %collective-permute-start.3 = (bf16[2,48,1024]{2,1,0:T(8,128)(2,1)S(1)}, bf16[2,48,1024]{2,1,0:T(8,128)(2,1)S(1)}, u32[]{:S(2)}, u32[]{:S(2)}) collective-permute-start(bf16[2,48,1024]{2,1,0:T(8,128)(2,1)S(1)} %get-tuple-element.39), channel_id=1, source_target_pairs={{4,0},{8,4},{12,8},{16,12},{20,16},{24,20},{28,24},{32,28},{36,32}... | collective-permute-start | bytes 589832 | tf_op jit(solution)/shard_map/ppermute | solution.py:388
